TPU v7x, 32 devices: a whole 2x2x4 slice. The times are simulated.
32 devices in a mesh: groups: 2 (over y), trades: 8 (over z, x), dates: 2 (over core).
Axes of the slice: x: 2, y: 2, z: 4, core: 2. Of those that a mesh axis runs over, the one named last changes fastest.
Arguments:
- basis_values: bfloat16 [8, 256, 256], P('dates', 'groups'), parts along dimension 1, may hold values from -6 to 6
- coefficients: bfloat16 [8192, 256], P('trades'), may hold values from -0.0625 to 0.0625
- set_map: int32 [8192], P('trades'), may hold values from 0 to 255, as said below
- trade_type: int32 [8192], P('trades'), may hold values from 0 to 15
- type_gain: float32 [8, 16], P('dates'), may hold values from 0.25 to 4
- set_lags: int32 [256], replicated, may hold values from 1 to 2
- thresholds: float32 [256], replicated, may hold values from -1 to 1
Outputs:
- coef_grad: float32 [16384, 256], P(('groups', 'trades'), 'dates'), parts along dimension 0
There are 2 independent parts, one for each index of `groups`. A program takes and returns all parts, laid end to end along the dimension named above; an argument that names none is the same for every part. Nothing has to cross between parts.
Inputs may be any that keep to these rules, and one draw needn't show every extreme that they name: `set_map`: in every aligned block of 1024 trades, exactly 128 trades fall in each group of 32 consecutive netting sets (sets g * 32 to (g + 1) * 32 - 1).
All inputs are finite; a program needn't handle non-finite values.
Results may differ from a plain program's by a relative error of at most 0.0018.
Values may be sent and summed in bfloat16 or wider, within the bound.
No kernel may reach another device: no remote copies, remote signals or barrier semaphores. Data moves between devices by JAX's collectives and lax.ppermute only.
A program may use at most 64 MiB of HBM per device.

v0:
```python
import math

import jax
import jax.numpy as jnp
from jax import lax
from jax.sharding import PartitionSpec as P

LAG_MAX = 2


def shifted(array, axis, by):
    peers = lax.axis_size(axis)
    pairs = [(i, i + by) for i in range(peers) if 0 <= i + by < peers]
    return lax.ppermute(array, axis, pairs)


def on_device(basis_values, coefficients, set_map, trade_type, type_gain, set_lags, thresholds):
    set_count = thresholds.shape[0]
    type_count = type_gain.shape[1]
    local_dates = basis_values.shape[0]
    path_count = basis_values.shape[1]
    trade_local = coefficients.shape[0]
    loss_scale = 2.0 / math.sqrt(local_dates * lax.axis_size("dates") * path_count)
    empty_grad = jnp.zeros((trade_local, coefficients.shape[1]), jnp.float32)
    owner_count = lax.axis_size("trades")
    own_sets = set_count // owner_count
    set_owner = set_map // own_sets
    route_order = jnp.argsort(set_owner, stable=True)
    coef_sorted = jnp.take(coefficients, route_order, axis=0)
    labels = jnp.take(set_map * type_count + trade_type, route_order, axis=0)
    recv_coef = lax.all_to_all(coef_sorted, "trades", split_axis=0, concat_axis=0, tiled=True)
    recv_label = lax.all_to_all(labels, "trades", split_axis=0, concat_axis=0, tiled=True)
    first_set = lax.axis_index("trades") * own_sets
    local_set = recv_label // type_count - first_set
    own_member = (local_set[:, None] == jnp.arange(own_sets, dtype=jnp.int32)[None, :]).astype(
        jnp.bfloat16
    )
    type_onehot = (
        (recv_label % type_count)[:, None] == jnp.arange(type_count, dtype=jnp.int32)[None, :]
    ).astype(jnp.float32)
    own_gain = jnp.einsum(
        "dy,ty->dt",
        type_gain,
        type_onehot,
        precision=lax.Precision.HIGHEST,
        preferred_element_type=jnp.float32,
    )
    lag_rows = lax.dynamic_slice_in_dim(set_lags, first_set, own_sets, 0)
    limit_rows = lax.dynamic_slice_in_dim(thresholds, first_set, own_sets, 0)
    netted_dates = []
    for which_date in range(local_dates):
        raw_value = jnp.einsum(
            "pk,tk->pt", basis_values[which_date], recv_coef, preferred_element_type=jnp.float32
        )
        prices = (raw_value * own_gain[which_date][None, :]).astype(jnp.bfloat16)
        netted_dates.append(jnp.dot(prices, own_member, preferred_element_type=jnp.float32))
    netted = jnp.stack(netted_dates, axis=1)
    previous = shifted(netted[:, local_dates - LAG_MAX :, :], "dates", 1)
    padded = jnp.concatenate([previous, netted], axis=1)
    collateral = jnp.zeros_like(netted)
    for lag_value in range(1, LAG_MAX + 1):
        lag_mask = (lag_rows == lag_value).astype(jnp.float32)
        collateral = (
            collateral
            + lag_mask * padded[:, LAG_MAX - lag_value : LAG_MAX - lag_value + local_dates, :]
        )
    exposure = jnp.maximum(netted - collateral - limit_rows, 0.0)
    direct_term = exposure * loss_scale
    following = shifted(direct_term[:, :LAG_MAX, :].astype(jnp.bfloat16), "dates", -1).astype(
        jnp.float32
    )
    padded_back = jnp.concatenate([direct_term, following], axis=1)
    adjoint = direct_term
    for lag_value in range(1, LAG_MAX + 1):
        lag_mask = (lag_rows == lag_value).astype(jnp.float32)
        adjoint = adjoint - lag_mask * padded_back[:, lag_value : lag_value + local_dates, :]
    adjoint = adjoint.astype(jnp.bfloat16)
    total_grad = empty_grad
    for which_date in range(local_dates):
        spread = jnp.einsum(
            "ps,ts->pt", adjoint[:, which_date, :], own_member, preferred_element_type=jnp.float32
        )
        scaled = (spread * own_gain[which_date][None, :]).astype(jnp.bfloat16)
        total_grad = total_grad + jnp.einsum(
            "pt,pk->tk", scaled, basis_values[which_date], preferred_element_type=jnp.float32
        )
    own_grad = total_grad
    returned = lax.all_to_all(own_grad, "trades", split_axis=0, concat_axis=0, tiled=True)
    inverse = jnp.argsort(route_order, stable=True)
    total_grad = jnp.take(returned, inverse, axis=0)
    return lax.psum_scatter(total_grad, "dates", scatter_dimension=1, tiled=True)


def solution(mesh):
    return jax.shard_map(
        on_device,
        mesh=mesh,
        in_specs=(
            P("dates", "groups", None),
            P("trades", None),
            P("trades"),
            P("trades"),
            P("dates", None),
            P(),
            P(),
        ),
        out_specs=P(("groups", "trades"), "dates"),
        check_vma=False,
    )
```

profile of v0, /device:TPU:0, one launch (start us, length us, event | category | flops | bytes accessed | tf_op | source)
XLA Modules:
  0.0 108.9 jit_solution(13513787980426994334)
XLA Ops:
  6.5 0.0 copy-start
  6.5 0.8 add_select_fusion.2
  7.3 4.4 %sort.31 = (s32[1024]{0:T(1024)}, s32[1024]{0:T(1024)S(1)}) sort(s32[1024]{0:T(1024)S(1)} %get-tuple-element.17, s32[1024]{0:T(1024)S(1)} %iota.15), dimensions={0}, to_apply=%region_0.1 | sort | flops 10240 | bytes 16384 | tf_op jit(solution)/shard_map/jit(argsort)/sort | solution.py:28
  11.7 4.5 %gather_fusion.1 = s32[1024]{0:T(1024)S(1)} fusion(s32[1024]{0:T(1024)S(1)} %get-tuple-element.18, s32[1024]{0:T(1024)S(1)} %fusion.79), kind=kCustom, calls=%fused_computation.1 | custom fusion | bytes 12288 | tf_op jit(solution)/shard_map/jit(_take)/gather | solution.py:30
  16.2 0.6 broadcast_select_fusion.2
  16.8 7.3 %all-to-all-start.1 = ((s32[8,128,1]{1,2,0:T(1,128)}), s32[8,128,1]{1,2,0:T(1,128)S(1)}, u32[]{:S(2)}, u32[]{:S(2)}) async-start(s32[8,128,1]{1,2,0:T(1,128)} %bitcast.5), calls=%async_computation.1 | async-start | bytes 8192 | tf_op jit(solution)/shard_map/all_to_all | solution.py:32
  24.1 0.0 copy-done
  24.1 3.9 %gather_fusion = bf16[1024,256]{1,0:T(8,128)(2,1)S(1)} fusion(bf16[1024,256]{1,0:T(8,128)(2,1)S(1)} %copy-done, s32[1024]{0:T(1024)S(1)} %fusion.79), kind=kCustom, calls=%fused_computation | custom fusion | bytes 1052672 | tf_op jit(solution)/shard_map/jit(_take)/gather | solution.py:29
  28.0 1.0 broadcast_select_fusion.1
  29.0 0.0 copy-start.1
  29.0 1.5 %all-to-all-done.1 = s32[8,128,1]{1,2,0:T(1,128)S(1)} async-done(((s32[8,128,1]{1,2,0:T(1,128)}), s32[8,128,1]{1,2,0:T(1,128)S(1)}, u32[]{:S(2)}, u32[]{:S(2)}) %all-to-all-start.1) | async-done | bytes 4128 | tf_op jit(solution)/shard_map/all_to_all | solution.py:32
  30.5 4.6 %all-to-all-start = ((bf16[8,128,256]{2,1,0:T(8,128)(2,1)}), bf16[8,128,256]{2,1,0:T(8,128)(2,1)S(1)}, u32[]{:S(2)}, u32[]{:S(2)}) async-start(bf16[8,128,256]{2,1,0:T(8,128)(2,1)} %broadcast_select_fusion.1), calls=%async_computation | async-start | bytes 1048576 | tf_op jit(solution)/shard_map/all_to_all | solution.py:31
  35.1 0.0 copy-start.4
  35.1 0.7 copy-done.4
  35.8 0.0 copy-start.2
  35.8 0.1 dynamic_slice.7
  35.9 0.6 copy-done.2
  36.5 0.1 compare_convert_fusion.1
  36.6 0.0 copy-start.3
  36.6 0.7 copy-done.3
  37.3 0.4 convolution_bitcast_fusion
  37.7 11.4 %all-to-all-done = bf16[8,128,256]{2,1,0:T(8,128)(2,1)S(1)} async-done(((bf16[8,128,256]{2,1,0:T(8,128)(2,1)}), bf16[8,128,256]{2,1,0:T(8,128)(2,1)S(1)}, u32[]{:S(2)}, u32[]{:S(2)}) %all-to-all-start) | async-done | bytes 524320 | tf_op jit(solution)/shard_map/all_to_all | solution.py:31
  49.1 0.0 copy-done.1
  49.1 0.6 fusion.16
  49.7 0.6 fusion.15
  50.3 1.3 %collective-permute-start = (f32[128,2,32]{0,2,1:T(8,128)S(1)}, f32[128,2,32]{0,2,1:T(8,128)S(1)}, u32[]{:S(2)}, u32[]{:S(2)}) collective-permute-start(f32[128,2,32]{0,2,1:T(8,128)S(1)} %pad_maximum_fusion.4), channel_id=1, source_target_pairs={{0,1},{2,3},{4,5},{6,7},{8,9},{10,11},{12,13},{14,15},{16,17},{18,... | collective-permute-start | bytes 98312 | tf_op jit(solution)/shard_map/ppermute | solution.py:14
  51.6 0.6 fusion.13
  52.2 0.6 fusion.14
  52.9 0.0 collective-permute-done
  52.9 0.1 fusion.49
  53.0 1.3 %collective-permute-start.1 = (bf16[128,2,32]{0,2,1:T(8,128)(2,1)S(1)}, bf16[128,2,32]{0,2,1:T(8,128)(2,1)S(1)}, u32[]{:S(2)}, u32[]{:S(2)}) collective-permute-start(bf16[128,2,32]{0,2,1:T(8,128)(2,1)S(1)} %slice.158), channel_id=1, source_target_pairs={{1,0},{3,2},{5,4},{7,6},{9,8},{11,10},{13,12},{15,14},{17,16},{19,... | collective-permute-start | bytes 49160 | tf_op jit(solution)/shard_map/ppermute | solution.py:14
  54.3 1.8 %collective-permute-done.1 = bf16[128,2,32]{0,2,1:T(8,128)(2,1)S(1)} collective-permute-done((bf16[128,2,32]{0,2,1:T(8,128)(2,1)S(1)}, bf16[128,2,32]{0,2,1:T(8,128)(2,1)S(1)}, u32[]{:S(2)}, u32[]{:S(2)}) %collective-permute-start.1) | collective-permute-done | bytes 16416 | tf_op jit(solution)/shard_map/ppermute | solution.py:14
  56.1 0.1 fusion.42
  56.1 0.6 fusion.12
  56.8 0.6 convolution_add_fusion.2
  57.4 0.6 convolution_add_fusion.1
  58.1 1.6 %convolution_add_fusion = f32[1024,256]{1,0:T(8,128)} fusion(f32[1024,256]{1,0:T(8,128)S(1)} %convolution_add_fusion.1, f32[1024]{0:T(1024)S(1)} %bitcast.75, s32[1024]{0:T(1024)S(1)} %get-tuple-element.15, bf16[4,128,256]{2,1,0:T(8,128)(2,1)S(1)} %copy-done.1, bf16[128,4,32]{0,2,1:T(8,128)(2,1)S(1)} %fusion.42), kind=kOutput, calls=%fused_computation.3 | convolution fusion | flops 76054528 | bytes 2179072 | tf_op jit(solution)/shard_map/pt,pk->tk/dot_general | solution.py:84
  59.7 3.8 %all-to-all-start.2 = ((f32[8,128,256]{2,1,0:T(8,128)}), f32[8,128,256]{2,1,0:T(8,128)S(1)}, u32[]{:S(2)}, u32[]{:S(2)}) async-start(f32[8,128,256]{2,1,0:T(8,128)} %bitcast.23), calls=%async_computation.2 | async-start | bytes 2097152 | tf_op jit(solution)/shard_map/all_to_all | solution.py:88
  63.5 0.0 reduce-scatter.2.cloned.1.call-start
  63.5 4.4 %sort.32 = (s32[1024]{0:T(1024)}, s32[1024]{0:T(1024)S(1)}) sort(s32[1024]{0:T(1024)S(1)} %get-tuple-element.7, s32[1024]{0:T(1024)S(1)} %iota.16), dimensions={0}, to_apply=%region_1.2 | sort | flops 10240 | bytes 16384 | tf_op jit(solution)/shard_map/jit(argsort)/sort | solution.py:89
  67.9 21.7 %all-to-all-done.2 = f32[8,128,256]{2,1,0:T(8,128)S(1)} async-done(((f32[8,128,256]{2,1,0:T(8,128)}), f32[8,128,256]{2,1,0:T(8,128)S(1)}, u32[]{:S(2)}, u32[]{:S(2)}) %all-to-all-start.2) | async-done | bytes 1048608 | tf_op jit(solution)/shard_map/all_to_all | solution.py:88
  89.6 3.5 %gather_fusion.2 = f32[1024,256]{1,0:T(8,128)S(1)} fusion(f32[1024,256]{1,0:T(8,128)S(1)} %bitcast.68, s32[1024]{0:T(1024)S(1)} %fusion.78), kind=kCustom, calls=%fused_computation.2 | custom fusion | bytes 2101248 | tf_op jit(solution)/shard_map/jit(_take)/gather | solution.py:90
  93.0 1.2 %broadcast_select_fusion = f32[1024,256]{1,0:T(8,128)} fusion(f32[1024,256]{1,0:T(8,128)S(1)} %gather_fusion.2, pred[1024]{0:T(1024)(128)(4,1)S(1)} %compare_and_fusion.1), kind=kLoop, calls=%fused_computation.32 | loop fusion | flops 262144 | bytes 2098176 | tf_op jit(solution)/shard_map/jit(_take)/select_n | solution.py:90
  94.2 0.0 reduce-scatter.2.cloned.1.call-update
  94.2 7.8 %reduce-scatter.2.cloned.1.call-done = f32[1024,128]{1,0:T(8,128)} async-done(((f32[1024,256]{1,0:T(8,128)}), f32[1024,128]{1,0:T(8,128)}) %reduce-scatter.2.cloned.1.call-update) | async-done | bytes 524304 | tf_op jit(solution)/shard_map/reduce_scatter | solution.py:91
  (10 shorter events, 0.1 us)
Async XLA Ops:
  6.5 17.5 %copy-start = (bf16[1024,256]{1,0:T(8,128)(2,1)S(1)}, bf16[1024,256]{1,0:T(8,128)(2,1)}, u32[]{:S(2)}) copy-start(bf16[1024,256]{1,0:T(8,128)(2,1)} %param.8) | copy-start | bytes 1572868
  16.8 13.7 %all-to-all-start.1 = ((s32[8,128,1]{1,2,0:T(1,128)}), s32[8,128,1]{1,2,0:T(1,128)S(1)}, u32[]{:S(2)}, u32[]{:S(2)}) async-start(s32[8,128,1]{1,2,0:T(1,128)} %bitcast.5), calls=%async_computation.1 | async-start | bytes 8192 | tf_op jit(solution)/shard_map/all_to_all | solution.py:32
  29.0 20.1 %copy-start.1 = (bf16[4,128,256]{2,1,0:T(8,128)(2,1)S(1)}, bf16[4,128,256]{2,1,0:T(8,128)(2,1)}, u32[]{:S(2)}) copy-start(bf16[4,128,256]{2,1,0:T(8,128)(2,1)} %param.7) | copy-start | bytes 786436
  30.5 18.6 %all-to-all-start = ((bf16[8,128,256]{2,1,0:T(8,128)(2,1)}), bf16[8,128,256]{2,1,0:T(8,128)(2,1)S(1)}, u32[]{:S(2)}, u32[]{:S(2)}) async-start(bf16[8,128,256]{2,1,0:T(8,128)(2,1)} %broadcast_select_fusion.1), calls=%async_computation | async-start | bytes 1048576 | tf_op jit(solution)/shard_map/all_to_all | solution.py:31
  35.1 0.7 copy-start.4
  35.8 0.7 copy-start.2
  36.6 0.7 copy-start.3
  50.3 2.5 %collective-permute-start = (f32[128,2,32]{0,2,1:T(8,128)S(1)}, f32[128,2,32]{0,2,1:T(8,128)S(1)}, u32[]{:S(2)}, u32[]{:S(2)}) collective-permute-start(f32[128,2,32]{0,2,1:T(8,128)S(1)} %pad_maximum_fusion.4), channel_id=1, source_target_pairs={{0,1},{2,3},{4,5},{6,7},{8,9},{10,11},{12,13},{14,15},{16,17},{18,... | collective-permute-start | bytes 98312 | tf_op jit(solution)/shard_map/ppermute | solution.py:14
  53.0 3.1 %collective-permute-start.1 = (bf16[128,2,32]{0,2,1:T(8,128)(2,1)S(1)}, bf16[128,2,32]{0,2,1:T(8,128)(2,1)S(1)}, u32[]{:S(2)}, u32[]{:S(2)}) collective-permute-start(bf16[128,2,32]{0,2,1:T(8,128)(2,1)S(1)} %slice.158), channel_id=1, source_target_pairs={{1,0},{3,2},{5,4},{7,6},{9,8},{11,10},{13,12},{15,14},{17,16},{19,... | collective-permute-start | bytes 49160 | tf_op jit(solution)/shard_map/ppermute | solution.py:14
  59.7 29.9 %all-to-all-start.2 = ((f32[8,128,256]{2,1,0:T(8,128)}), f32[8,128,256]{2,1,0:T(8,128)S(1)}, u32[]{:S(2)}, u32[]{:S(2)}) async-start(f32[8,128,256]{2,1,0:T(8,128)} %bitcast.23), calls=%async_computation.2 | async-start | bytes 2097152 | tf_op jit(solution)/shard_map/all_to_all | solution.py:88
  63.5 38.5 %reduce-scatter.2.cloned.1.call-start = ((), (), s32[]{:S(2)}) async-start(), calls=%async_computation.4 | async-start | bytes 1572864 | tf_op jit(solution)/shard_map/reduce_scatter | solution.py:91
Sparse Core Ops, SparseCore 0:
  94.4 7.5 reduce-scatter.1
where the time goes:
time: 109 us
  waiting for transfers between devices  44.1 us (40%)
  starting transfers between devices  18.3 us (17%)
  local copies, waits for them, and re-layouts  14 us (13%)
  between operations  13.5 us (12%)
  other arithmetic  12.6 us (12%)
  matrix products  6.4 us (6%)
    all_to_all x1, waiting for transfers between devices, on_device(): lax.all_to_all(own_grad, 'trades', split_axis=0, concat_axis=0, tiled=True)  21.7 us
    all_to_all x1, waiting for transfers between devices, on_device(): lax.all_to_all(coef_sorted, 'trades', split_axis=0, concat_axis=0, tiled=...  11.4 us
    reduce_scatter x1, waiting for transfers between devices, on_device(): lax.psum_scatter(total_grad, 'dates', scatter_dimension=1, tiled=True)  7.76 us
    all_to_all x1, starting transfers between devices, on_device(): lax.all_to_all(labels, 'trades', split_axis=0, concat_axis=0, tiled=True)  7.25 us
    all_to_all x1, starting transfers between devices, on_device(): lax.all_to_all(coef_sorted, 'trades', split_axis=0, concat_axis=0, tiled=...  4.61 us
    gather x1, local copies, waits for them, and re-layouts, on_device(): labels = jnp.take(set_map * type_count + trade_type, route_order, axis=0)  4.52 us
    sort x1, other arithmetic, on_device(): route_order = jnp.argsort(set_owner, stable=True)  4.37 us
    sort x1, other arithmetic, on_device(): inverse = jnp.argsort(route_order, stable=True)  4.37 us
  transfers between devices with their start and end apart: 6, of which 5 were waited for; matrix products, arithmetic and copies ran while one was open for 10% of the time, Pallas kernels for 0%

commit v1 on v0

v1 whole, which is shorter than its diff:
```python
import math

import jax
import jax.numpy as jnp
from jax import lax
from jax.sharding import PartitionSpec as P

LAG_MAX = 2


def swap_sum(blocks_of, axis):
    peers = lax.axis_size(axis)
    me = lax.axis_index(axis)
    arrived = []
    for step in range(1, peers):
        pairs = [(i, (i + step) % peers) for i in range(peers)]
        arrived.append(lax.ppermute(blocks_of((me + step) % peers), axis, pairs))
    total = blocks_of(me)
    for part in arrived:
        total = total + part
    return total


def on_device(basis_values, coefficients, set_map, trade_type, type_gain, set_lags, thresholds):
    local_dates, path_count, depth = basis_values.shape
    trade_local = coefficients.shape[0]
    set_count = thresholds.shape[0]
    type_count = type_gain.shape[1]
    trade_peers = lax.axis_size("trades")
    date_peers = lax.axis_size("dates")
    blocks = trade_peers * date_peers
    block_paths = path_count // blocks
    dates = local_dates * date_peers
    rows = local_dates * path_count
    loss_scale = 2.0 / math.sqrt(dates * path_count)
    member = (set_map[:, None] == jnp.arange(set_count, dtype=jnp.int32)[None, :]).astype(jnp.bfloat16)
    type_onehot = (trade_type[:, None] == jnp.arange(type_count, dtype=jnp.int32)[None, :]).astype(
        jnp.float32
    )
    own_gain = jnp.einsum(
        "dy,ty->dt",
        type_gain,
        type_onehot,
        precision=lax.Precision.HIGHEST,
        preferred_element_type=jnp.float32,
    )
    basis_rows = basis_values.reshape(rows, depth)
    raw_value = jnp.einsum("rk,tk->rt", basis_rows, coefficients, preferred_element_type=jnp.float32)
    prices = raw_value.reshape(local_dates, path_count, trade_local) * own_gain[:, None, :]
    prices = prices.astype(jnp.bfloat16).reshape(rows, trade_local)
    partial = jnp.dot(prices, member, preferred_element_type=jnp.float32)
    partial = partial.reshape(local_dates, blocks, block_paths, set_count).transpose(1, 0, 2, 3)
    partial = partial.astype(jnp.float16)
    arrived = lax.all_to_all(partial, ("trades", "dates"), split_axis=0, concat_axis=0, tiled=True)
    arrived = arrived.reshape(trade_peers, dates, block_paths, set_count)
    netted = jnp.sum(arrived.astype(jnp.float32), axis=0)
    collateral = jnp.zeros_like(netted)
    padded = jnp.pad(netted, ((LAG_MAX, 0), (0, 0), (0, 0)))
    for lag_value in range(1, LAG_MAX + 1):
        lag_mask = (set_lags == lag_value).astype(jnp.float32)
        collateral = collateral + lag_mask * padded[LAG_MAX - lag_value : LAG_MAX - lag_value + dates]
    direct_term = jnp.maximum(netted - collateral - thresholds, 0.0) * loss_scale
    padded_back = jnp.pad(direct_term, ((0, LAG_MAX), (0, 0), (0, 0)))
    adjoint = direct_term
    for lag_value in range(1, LAG_MAX + 1):
        lag_mask = (set_lags == lag_value).astype(jnp.float32)
        adjoint = adjoint - lag_mask * padded_back[lag_value : lag_value + dates]
    adjoint = adjoint.astype(jnp.bfloat16).reshape(1, date_peers, local_dates, block_paths, set_count)
    adjoint = jnp.broadcast_to(adjoint, (trade_peers,) + adjoint.shape[1:])
    adjoint = adjoint.reshape(blocks, local_dates, block_paths, set_count)
    adjoint = lax.all_to_all(adjoint, ("trades", "dates"), split_axis=0, concat_axis=0, tiled=True)
    adjoint = adjoint.transpose(1, 0, 2, 3).reshape(rows, set_count)
    spread = jnp.einsum("ts,rs->tr", member, adjoint, preferred_element_type=jnp.float32)
    scaled = spread.reshape(trade_local, local_dates, path_count) * own_gain.T[:, :, None]
    scaled = scaled.astype(jnp.bfloat16).reshape(trade_local, rows)
    own_depth = depth // date_peers

    def part_of(which):
        columns = lax.dynamic_slice_in_dim(basis_rows, which * own_depth, own_depth, 1)
        return jnp.dot(scaled, columns, preferred_element_type=jnp.float32)

    return swap_sum(part_of, "dates")


def solution(mesh):
    return jax.shard_map(
        on_device,
        mesh=mesh,
        in_specs=(
            P("dates", "groups", None),
            P("trades", None),
            P("trades"),
            P("trades"),
            P("dates", None),
            P(),
            P(),
        ),
        out_specs=P(("groups", "trades"), "dates"),
        check_vma=False,
    )
```

time: 109 us -> 40.4 us (0.37)
  waiting for transfers between devices: 44.1 us -> 21.9 us
  between operations: 13.5 us -> 0.14 us
  other arithmetic: 12.6 us -> 0.08 us
  local copies, waits for them, and re-layouts: 14 us -> 1.51 us
  starting transfers between devices: 18.3 us -> 11.1 us
  matrix products: 6.4 us -> 5.31 us
    all_to_all x3 -> x2, waiting for transfers between devices: 34.5 us -> 20 us  [the longest x1 10 us: on_device(): lax.all_to_all(partial, ('trades', 'dates'), split_axis=0, concat_axis=0,...]
    gather x3 -> x0, local copies, waits for them, and re-layouts: 11.9 us -> none  [the longest x1 4.52 us: on_device(): labels = jnp.take(set_map * type_count + trade_type, route_order, axis=0)]
    sort x2 -> x0, other arithmetic: 8.73 us -> none  [the longest x1 4.37 us: on_device(): route_order = jnp.argsort(set_owner, stable=True)]
    reduce_scatter x1 -> x0, waiting for transfers between devices: 7.76 us -> none  [on_device(): lax.psum_scatter(total_grad, 'dates', scatter_dimension=1, tiled=True)]
    all_to_all x3 -> x2, starting transfers between devices: 15.7 us -> 11 us  [the longest x1 7.49 us: on_device(): lax.all_to_all(partial, ('trades', 'dates'), split_axis=0, concat_axis=0,...]
    select_n x4 -> x0, other arithmetic: 3.54 us -> none  [the longest x1 1.18 us: on_device(): total_grad = jnp.take(returned, inverse, axis=0)]
    ppermute x2 -> x1, starting transfers between devices: 2.58 us -> 0.07 us  [swap_sum(): arrived.append(lax.ppermute(blocks_of((me + step) % peers), axis, pairs))]
    unnamed x10, local copies, waits for them, and re-layouts: 1.96 us -> 0.03 us
  transfers between devices with their start and end apart: 6 -> 3, of which waited for: 5 -> 3; matrix products, arithmetic and copies ran while one was open for 10% -> 0% of each run, Pallas kernels for 0% -> 0%
where the time goes in v1:
time: 40.4 us; the launch traced here: 40 us
  waiting for transfers between devices  21.9 us (54%)
  starting transfers between devices  11.1 us (27%)
  matrix products  5.31 us (13%)
  local copies, waits for them, and re-layouts  1.51 us (4%)
    all_to_all x1, waiting for transfers between devices, on_device(): lax.all_to_all(partial, ('trades', 'dates'), split_axis=0, concat_axis=0,...  10 us
    all_to_all x1, waiting for transfers between devices, on_device(): lax.all_to_all(adjoint, ('trades', 'dates'), split_axis=0, concat_axis=0,...  9.98 us
    all_to_all x1, starting transfers between devices, on_device(): lax.all_to_all(partial, ('trades', 'dates'), split_axis=0, concat_axis=0,...  7.49 us
    all_to_all x1, starting transfers between devices, on_device(): lax.all_to_all(adjoint, ('trades', 'dates'), split_axis=0, concat_axis=0,...  3.53 us
    ppermute x1, waiting for transfers between devices, swap_sum(): arrived.append(lax.ppermute(blocks_of((me + step) % peers), axis, pairs))  1.89 us
    dot_general x1, matrix products, on_device(): partial = jnp.dot(prices, member, preferred_element_type=jnp.float32)  1.81 us
    dot_general x2, matrix products, part_of(): return jnp.dot(scaled, columns, preferred_element_type=jnp.float32)  1.74 us
    dot_general x1, matrix products, on_device(): jnp.einsum('dy,ty->dt', type_gain, type_onehot, precision=lax.Precision.H...  1.2 us
  transfers between devices with their start and end apart: 3, of which 3 were waited for; matrix products, arithmetic and copies ran while one was open for 0% of the time, Pallas kernels for 0%

profile of v1, /device:TPU:0, one launch (start us, length us, event | category | flops | bytes accessed | tf_op | source)
XLA Modules:
  0.0 40.0 jit_solution(12827794903694908821)
XLA Ops:
  0.0 0.0 copy-start
  0.0 1.2 %fusion.10 = f32[1024,4]{0,1:T(4,128)S(1)} fusion(f32[4,16]{1,0:T(4,128)} %param.11, s32[1024]{0:T(1024)} %param.10), kind=kOutput, calls=%fused_computation.14 | convolution fusion | flops 802816 | bytes 20736 | tf_op jit(solution)/shard_map/dy,ty->dt/dot_general | solution.py:40
  1.2 0.0 copy-done
  1.2 1.8 %fusion.1 = f16[16,4,8,256]{3,2,0,1:T(8,128)(2,1)S(1)} fusion(bf16[4,128,256]{2,1,0:T(8,128)(2,1)} %param.7, f32[4,1024]{1,0:T(4,128)S(1)} %bitcast.44, bf16[1024,256]{1,0:T(8,128)(2,1)S(1)} %copy-done, s32[1024]{0:T(1024)} %param.9), kind=kOutput, calls=%fused_computation.5 | convolution fusion | flops 538312704 | bytes 1069056 | tf_op jit(solution)/shard_map/dot_general | solution.py:51
  3.0 0.0 copy-start.3
  3.0 0.0 copy-start.2
  3.0 0.8 %copy.10 = f16[16,4,8,256]{3,2,1,0:T(8,128)(2,1)} copy(f16[16,4,8,256]{3,2,0,1:T(8,128)(2,1)S(1)} %fusion.1) | data formatting | bytes 524288 | tf_op jit(solution)/shard_map/convert_element_type | solution.py:53
  3.8 0.0 copy-start.4
  3.8 7.5 %all-to-all-start = ((f16[16,4,8,256]{3,2,1,0:T(8,128)(2,1)}), f16[16,4,8,256]{3,2,1,0:T(8,128)(2,1)S(1)}, u32[]{:S(2)}, u32[]{:S(2)}) async-start(f16[16,4,8,256]{3,2,1,0:T(8,128)(2,1)} %copy.10), calls=%async_computation | async-start | bytes 524288 | tf_op jit(solution)/shard_map/all_to_all | solution.py:54
  11.3 0.0 copy-done.3
  11.3 10.0 %all-to-all-done = f16[16,4,8,256]{3,2,1,0:T(8,128)(2,1)S(1)} async-done(((f16[16,4,8,256]{3,2,1,0:T(8,128)(2,1)}), f16[16,4,8,256]{3,2,1,0:T(8,128)(2,1)S(1)}, u32[]{:S(2)}, u32[]{:S(2)}) %all-to-all-start) | async-done | bytes 262176 | tf_op jit(solution)/shard_map/all_to_all | solution.py:54
  21.4 0.0 copy-done.2
  21.4 0.7 %broadcast_in_dim.5 = bf16[8,2,4,8,256]{4,3,2,1,0:T(8,128)(2,1)} broadcast(bf16[2,4,8,256]{3,2,1,0:T(8,128)(2,1)S(1)} %bitcast.43), dimensions={1,2,3,4} | broadcast | bytes 294912 | tf_op jit(solution)/shard_map/broadcast_in_dim | solution.py:69
  22.2 3.5 %all-to-all-start.1 = ((bf16[16,4,8,256]{3,2,1,0:T(8,128)(2,1)}), bf16[16,4,8,256]{3,2,1,0:T(8,128)(2,1)S(1)}, u32[]{:S(2)}, u32[]{:S(2)}) async-start(bf16[16,4,8,256]{3,2,1,0:T(8,128)(2,1)} %bitcast.9), calls=%async_computation.1 | async-start | bytes 524288 | tf_op jit(solution)/shard_map/all_to_all | solution.py:71
  25.7 0.0 copy-start.1
  25.7 10.0 %all-to-all-done.1 = bf16[16,4,8,256]{3,2,1,0:T(8,128)(2,1)S(1)} async-done(((bf16[16,4,8,256]{3,2,1,0:T(8,128)(2,1)}), bf16[16,4,8,256]{3,2,1,0:T(8,128)(2,1)S(1)}, u32[]{:S(2)}, u32[]{:S(2)}) %all-to-all-start.1) | async-done | bytes 262176 | tf_op jit(solution)/shard_map/all_to_all | solution.py:71
  35.7 0.0 copy-done.4
  35.7 0.6 %multiply_convert_fusion = bf16[1024,4,128]{0,2,1:T(8,128)(2,1)S(1)} fusion(f32[1024,4]{0,1:T(4,128)S(1)} %fusion.10, s32[1024]{0:T(1024)S(1)} %copy-done.4, bf16[16,4,8,256]{3,2,1,0:T(8,128)(2,1)S(1)} %all-to-all-done.1), kind=kOutput, calls=%fused_computation | convolution fusion | flops 269746176 | bytes 1331200 | tf_op jit(solution)/shard_map/ts,rs->tr/dot_general | solution.py:73
  36.3 0.0 copy-done.1
  36.3 0.5 %fusion.14 = f32[1024,128]{1,0:T(8,128)S(1)} fusion(bf16[1024,512]{0,1:T(8,128)(2,1)S(1)} %bitcast.38, bf16[512,256]{1,0:T(8,128)(2,1)S(1)} %bitcast.41, s32[]{:T(128)S(6)} %select_n.15), kind=kOutput, calls=%fused_computation.18 | convolution fusion | flops 134217728 | bytes 1703940 | tf_op jit(solution)/shard_map/dot_general | solution.py:80
  36.8 0.1 collective-permute-start
  36.9 1.9 %collective-permute-done = f32[1024,128]{1,0:T(8,128)S(1)} collective-permute-done((f32[1024,128]{1,0:T(8,128)S(1)}, f32[1024,128]{1,0:T(8,128)S(1)}, u32[]{:S(2)}, u32[]{:S(2)}) %collective-permute-start) | collective-permute-done | bytes 524320 | tf_op jit(solution)/shard_map/ppermute | solution.py:17
  38.8 1.3 %convolution_add_fusion = f32[1024,128]{1,0:T(8,128)} fusion(f32[1024,128]{1,0:T(8,128)S(1)} %collective-permute-done, bf16[1024,512]{0,1:T(8,128)(2,1)S(1)} %bitcast.39, bf16[512,256]{1,0:T(8,128)(2,1)S(1)} %bitcast.42, s32[]{:T(128)S(6)} %select_n.13), kind=kOutput, calls=%fused_computation.3 | convolution fusion | flops 134348800 | bytes 2228228 | tf_op jit(solution)/shard_map/dot_general | solution.py:80
  (4 shorter events, 0.1 us)
Async XLA Ops:
  0.0 1.2 %copy-start = (bf16[1024,256]{1,0:T(8,128)(2,1)S(1)}, bf16[1024,256]{1,0:T(8,128)(2,1)}, u32[]{:S(2)}) copy-start(bf16[1024,256]{1,0:T(8,128)(2,1)} %param.8) | copy-start | bytes 1572868
  3.0 8.3 %copy-start.3 = (s32[256]{0:T(256)S(1)}, s32[256]{0:T(256)}, u32[]{:S(2)}) copy-start(s32[256]{0:T(256)} %param.12) | copy-start | bytes 3076
  3.0 18.4 %copy-start.2 = (f32[256]{0:T(256)S(1)}, f32[256]{0:T(256)}, u32[]{:S(2)}) copy-start(f32[256]{0:T(256)} %param.13) | copy-start | bytes 3076
  3.8 31.9 %copy-start.4 = (s32[1024]{0:T(1024)S(1)}, s32[1024]{0:T(1024)}, u32[]{:S(2)}) copy-start(s32[1024]{0:T(1024)} %param.9) | copy-start | bytes 12292
  3.8 17.5 %all-to-all-start = ((f16[16,4,8,256]{3,2,1,0:T(8,128)(2,1)}), f16[16,4,8,256]{3,2,1,0:T(8,128)(2,1)S(1)}, u32[]{:S(2)}, u32[]{:S(2)}) async-start(f16[16,4,8,256]{3,2,1,0:T(8,128)(2,1)} %copy.10), calls=%async_computation | async-start | bytes 524288 | tf_op jit(solution)/shard_map/all_to_all | solution.py:54
  22.2 13.5 %all-to-all-start.1 = ((bf16[16,4,8,256]{3,2,1,0:T(8,128)(2,1)}), bf16[16,4,8,256]{3,2,1,0:T(8,128)(2,1)S(1)}, u32[]{:S(2)}, u32[]{:S(2)}) async-start(bf16[16,4,8,256]{3,2,1,0:T(8,128)(2,1)} %bitcast.9), calls=%async_computation.1 | async-start | bytes 524288 | tf_op jit(solution)/shard_map/all_to_all | solution.py:71
  25.7 10.6 %copy-start.1 = (bf16[4,128,256]{2,1,0:T(8,128)(2,1)S(1)}, bf16[4,128,256]{2,1,0:T(8,128)(2,1)}, u32[]{:S(2)}) copy-start(bf16[4,128,256]{2,1,0:T(8,128)(2,1)} %param.7) | copy-start | bytes 786436
  36.8 2.0 %collective-permute-start = (f32[1024,128]{1,0:T(8,128)S(1)}, f32[1024,128]{1,0:T(8,128)S(1)}, u32[]{:S(2)}, u32[]{:S(2)}) collective-permute-start(f32[1024,128]{1,0:T(8,128)S(1)} %fusion.14), channel_id=1, source_target_pairs={{0,1},{1,0},{2,3},{3,2},{4,5},{5,4},{6,7},{7,6},{8,9},{9,8},{10,11... | collective-permute-start | bytes 1572872 | tf_op jit(solution)/shard_map/ppermute | solution.py:17

commit v2 on v1

v2 whole, which is shorter than its diff:
```python
import functools
import math

import jax
import jax.numpy as jnp
from jax import lax
from jax.experimental import pallas as pl
from jax.experimental.pallas import tpu as pltpu
from jax.sharding import PartitionSpec as P

LAG_MAX = 2
NT = (((1,), (1,)), ((), ()))
VMEM_BYTES = 40 * 1024 * 1024


def in_hbm(*arrays):
    return [pltpu.with_memory_space_constraint(array, pltpu.HBM) for array in arrays]


def whole(*shape):
    return pl.BlockSpec(shape, lambda *_: (0,) * len(shape))


def netting_kernel(
    basis_ref, coef_ref, set_ref, type_ref, gain_ref, lags_ref, limits_ref, out_ref, lags_out_ref, limits_out_ref
):
    lags_out_ref[...] = lags_ref[...]
    limits_out_ref[...] = limits_ref[...]
    dates, paths, depth = basis_ref.shape
    blocks, _, block_paths, set_count = out_ref.shape
    trades = coef_ref.shape[0]
    gain = jnp.zeros((dates, trades), jnp.float32)
    for which in range(gain_ref.shape[1]):
        gain = jnp.where(type_ref[...] == which, gain_ref[:, which : which + 1], gain)
    member = lax.broadcasted_iota(jnp.int32, (set_count, trades), 0) == set_ref[...]
    member = member.astype(jnp.float32).astype(jnp.bfloat16)
    rows = basis_ref[...].reshape(dates * paths, depth)
    raw = lax.dot_general(rows, coef_ref[...], NT, preferred_element_type=jnp.float32)
    prices = raw.reshape(dates, paths, trades) * gain[:, None, :]
    prices = prices.astype(jnp.bfloat16).reshape(dates * paths, trades)
    netted = lax.dot_general(prices, member, NT, preferred_element_type=jnp.float32)
    netted = netted.reshape(dates, blocks, block_paths, set_count)
    for date in range(dates):
        out_ref[:, date] = netted[date]


def net_own(basis_values, coefficients, set_map, trade_type, type_gain, set_lags, thresholds, blocks):
    set_count = thresholds.shape[0]
    dates, paths, depth = basis_values.shape
    trades = coefficients.shape[0]
    block_paths = paths // blocks
    span = math.gcd(paths, max(block_paths, 128))
    shape = (blocks, dates, block_paths, set_count)
    return pl.pallas_call(
        netting_kernel,
        grid=(paths // span,),
        in_specs=[
            pl.BlockSpec((dates, span, depth), lambda i: (0, i, 0)),
            whole(trades, depth),
            whole(1, trades),
            whole(1, trades),
            whole(dates, type_gain.shape[1]),
            whole(1, set_count),
            whole(1, set_count),
        ],
        out_specs=[
            pl.BlockSpec((span // block_paths,) + shape[1:], lambda i: (i, 0, 0, 0)),
            whole(1, set_count),
            whole(1, set_count),
        ],
        out_shape=[
            pltpu.VMEM(shape, jnp.float32),
            pltpu.VMEM((1, set_count), jnp.int32),
            pltpu.VMEM((1, set_count), jnp.float32),
        ],
        compiler_params=pltpu.CompilerParams(vmem_limit_bytes=VMEM_BYTES),
    )(
        *in_hbm(
            basis_values,
            coefficients,
            set_map.reshape(1, trades),
            trade_type.reshape(1, trades),
            type_gain,
            set_lags.reshape(1, set_count),
            thresholds.reshape(1, set_count),
        )
    )


def adjoint_kernel(scale, netted_ref, lags_ref, limits_ref, out_ref):
    dates, block_paths, set_count = netted_ref.shape
    lag = lags_ref[...].reshape(1, set_count)
    limit = limits_ref[...].reshape(1, set_count)
    masks = [(lag == value).astype(jnp.float32) for value in range(1, LAG_MAX + 1)]
    netted = [netted_ref[date] for date in range(dates)]
    direct = []
    for date in range(dates):
        collateral = jnp.zeros_like(netted[date])
        for value, mask in enumerate(masks, 1):
            if date >= value:
                collateral = collateral + mask * netted[date - value]
        direct.append(jnp.maximum(netted[date] - collateral - limit, 0.0) * scale)
    adjoints = []
    for date in range(dates):
        adjoint = direct[date]
        for value, mask in enumerate(masks, 1):
            if date + value < dates:
                adjoint = adjoint - mask * direct[date + value]
        adjoints.append(adjoint)
    block = jnp.concatenate(adjoints, axis=0).astype(jnp.bfloat16)
    for peer in range(out_ref.shape[0]):
        out_ref[peer] = block


def adjoint_of(netted, set_lags, thresholds, scale, peers):
    dates, block_paths, set_count = netted.shape
    return pl.pallas_call(
        functools.partial(adjoint_kernel, scale),
        out_shape=pltpu.VMEM((peers, dates * block_paths, set_count), jnp.bfloat16),
        compiler_params=pltpu.CompilerParams(vmem_limit_bytes=VMEM_BYTES),
    )(netted, set_lags, thresholds)


def grad_kernel(carry, *refs):
    if carry:
        total_ref, member_ref, gain_ref, adjoint_ref, basis_ref, out_ref = refs
    else:
        member_ref, gain_ref, adjoint_ref, basis_ref, out_ref = refs
    rows = adjoint_ref.shape[0]
    period = gain_ref.shape[1]
    spread = lax.dot_general(member_ref[...], adjoint_ref[...], NT, preferred_element_type=jnp.float32)
    gain = gain_ref[...]
    scaled = [
        (spread[:, first : first + period] * gain).astype(jnp.bfloat16) for first in range(0, rows, period)
    ]
    scaled = jnp.concatenate(scaled, axis=1)
    part = jnp.dot(scaled, basis_ref[...], preferred_element_type=jnp.float32)
    last = pl.program_id(1)

    if carry:
        part = jnp.where(last == 0, total_ref[...], 0.0) + part

    @pl.when(last == 0)
    def _():
        out_ref[...] = part

    @pl.when(last > 0)
    def _():
        out_ref[...] += part


def add_grad(total, member, gain, adjoint, basis, final):
    trades, set_count = member.shape
    rows, depth = basis.shape
    period = gain.shape[1]
    span = math.gcd(rows, max(period, 512))
    tile = math.gcd(trades, 1024)
    shape = (trades, depth)
    carry = total is not None
    row = lambda i, j: (i, 0)
    return pl.pallas_call(
        functools.partial(grad_kernel, carry),
        grid=(trades // tile, rows // span),
        in_specs=([pl.BlockSpec((tile, depth), row)] if carry else [])
        + [
            pl.BlockSpec((tile, set_count), row),
            pl.BlockSpec((tile, period), row),
            pl.BlockSpec((span, set_count), lambda i, j: (j, 0)),
            pl.BlockSpec((span, depth), lambda i, j: (j, 0)),
        ],
        out_specs=pl.BlockSpec((tile, depth), row),
        out_shape=jax.ShapeDtypeStruct(shape, jnp.float32) if final else pltpu.VMEM(shape, jnp.float32),
        compiler_params=pltpu.CompilerParams(vmem_limit_bytes=VMEM_BYTES),
        cost_estimate=pl.CostEstimate(
            flops=2 * trades * rows * (set_count + depth), bytes_accessed=4 * trades * depth, transcendentals=0
        ),
    )(*([total] if carry else []), member, gain, adjoint, basis)


def from_dates(pieces_of, like):
    peers = lax.axis_size("dates")
    me = lax.axis_index("dates")
    size = like.shape[0]
    full = jnp.zeros((size * peers,) + like.shape[1:], like.dtype)
    for step in range(peers):
        piece = pieces_of((me + step) % peers)
        if step:
            piece = lax.ppermute(piece, "dates", [(i, (i + step) % peers) for i in range(peers)])
        owner = (me - step) % peers
        full = lax.dynamic_update_slice_in_dim(full, piece, owner * size, 0)
    return full


def on_device(basis_values, coefficients, set_map, trade_type, type_gain, set_lags, thresholds):
    local_dates, path_count, depth = basis_values.shape
    trade_local = coefficients.shape[0]
    set_count = thresholds.shape[0]
    type_count = type_gain.shape[1]
    trade_peers = lax.axis_size("trades")
    date_peers = lax.axis_size("dates")
    me = lax.axis_index("dates")
    blocks = trade_peers * date_peers
    block_paths = path_count // blocks
    dates = local_dates * date_peers
    own_depth = depth // date_peers
    loss_scale = 2.0 / math.sqrt(dates * path_count)
    partial, lags, limits = net_own(
        basis_values, coefficients, set_map, trade_type, type_gain, set_lags, thresholds, blocks
    )
    partial = partial.astype(jnp.float16)
    arrived = lax.all_to_all(partial, ("trades", "dates"), split_axis=0, concat_axis=0, tiled=True)
    netted = jnp.sum(
        arrived.reshape(trade_peers, dates, block_paths, set_count).astype(jnp.float32), axis=0
    )
    adjoint = adjoint_of(netted, lags, limits, loss_scale, trade_peers)
    basis_late, gain_late, set_late, type_late, adjoint = lax.optimization_barrier(
        (basis_values, type_gain, set_map, trade_type, adjoint)
    )
    adjoint = lax.all_to_all(adjoint, "trades", split_axis=0, concat_axis=0, tiled=True)
    adjoint = adjoint.reshape(trade_peers * dates * block_paths, set_count)

    def own_columns(which):
        return lax.dynamic_slice_in_dim(basis_late, which * own_depth, own_depth, 2)

    basis = from_dates(own_columns, basis_late[:, :, :own_depth])
    basis = basis.reshape(dates, trade_peers, date_peers, block_paths, own_depth).transpose(2, 1, 0, 3, 4)
    basis = basis.reshape(date_peers, trade_peers * dates * block_paths, own_depth)
    gain = from_dates(lambda which: gain_late, gain_late)
    period = dates * block_paths
    while period % 128:
        period *= 2
    gain_rows = jnp.tile(jnp.repeat(gain, block_paths, axis=0), (period // (dates * block_paths), 1))
    member = (set_late[:, None] == jnp.arange(set_count, dtype=jnp.int32)[None, :]).astype(jnp.bfloat16)
    trade_gain = jnp.zeros((trade_local, period), jnp.float32)
    for which in range(type_count):
        trade_gain = jnp.where(type_late[:, None] == which, gain_rows[:, which][None, :], trade_gain)
    total = None
    for step in range(date_peers):
        there = adjoint
        if step:
            there = lax.ppermute(adjoint, "dates", [(i, (i + step) % date_peers) for i in range(date_peers)])
        rows = lax.dynamic_index_in_dim(basis, (me - step) % date_peers, 0, keepdims=False)
        total = add_grad(total, member, trade_gain, there, rows, step == date_peers - 1)
    return total


def solution(mesh):
    return jax.shard_map(
        on_device,
        mesh=mesh,
        in_specs=(
            P("dates", "groups", None),
            P("trades", None),
            P("trades"),
            P("trades"),
            P("dates", None),
            P(),
            P(),
        ),
        out_specs=P(("groups", "trades"), "dates"),
        check_vma=False,
    )
```

time: 40.4 us -> 37.1 us (0.918)
  waiting for transfers between devices: 21.9 us -> 15.4 us
  matrix products: 5.31 us -> 0 us
  Pallas kernels: 0 us -> 5.1 us
  other arithmetic: 0.08 us -> 3.25 us
    dot_general x5 -> x0, matrix products: 5.31 us -> none  [the longest x1 1.81 us: on_device(): partial = jnp.dot(prices, member, preferred_element_type=jnp.float32)]
    all_to_all x1, waiting for transfers between devices: 9.98 us -> 4.81 us  [on_device(): lax.all_to_all(adjoint, 'trades', split_axis=0, concat_axis=0, tiled=True)]
    pallas_call x0 -> x4, Pallas kernels: none -> 5.1 us  [the longest x2 2.37 us: add_grad(): pl.pallas_call(functools.partial(grad_kernel, carry), grid=(trades // til...]
    select_n x0 -> x1, other arithmetic: none -> 2.24 us  [on_device(): jnp.where(type_late[:, None] == which, gain_rows[:, which][None, :], trad...]
    ppermute x1 -> x3, waiting for transfers between devices: 1.89 us -> 0.57 us  [the longest x1 0.56 us: on_device(): lax.ppermute(adjoint, 'dates', [(i, (i + step) % date_peers) for i in ran...]
    unnamed x10 -> x8, local copies, waits for them, and re-layouts: 0.03 us -> 1.34 us
    convert_element_type x2, other arithmetic: 0.02 us -> 0.95 us  [the longest x1 0.75 us: on_device(): partial = partial.astype(jnp.float16)]
    convert_element_type x1 -> x0, local copies, waits for them, and re-layouts: 0.75 us -> none  [on_device(): partial = partial.astype(jnp.float16)]
  transfers between devices with their start and end apart: 3 -> 5, of which waited for: 3 -> 3; matrix products, arithmetic and copies ran while one was open for 0% -> 8% of each run, Pallas kernels for 0% -> 2%
where the time goes in v2:
time: 37.1 us; the launch traced here: 36.7 us
  waiting for transfers between devices  15.4 us (42%)
  starting transfers between devices  11 us (30%)
  Pallas kernels  5.1 us (14%)
  other arithmetic  3.25 us (9%)
  local copies, waits for them, and re-layouts  1.74 us (5%)
    all_to_all x1, waiting for transfers between devices, on_device(): lax.all_to_all(partial, ('trades', 'dates'), split_axis=0, concat_axis=0,...  9.98 us
    all_to_all x1, starting transfers between devices, on_device(): lax.all_to_all(partial, ('trades', 'dates'), split_axis=0, concat_axis=0,...  7.36 us
    all_to_all x1, waiting for transfers between devices, on_device(): lax.all_to_all(adjoint, 'trades', split_axis=0, concat_axis=0, tiled=True)  4.81 us
    all_to_all x1, starting transfers between devices, on_device(): lax.all_to_all(adjoint, 'trades', split_axis=0, concat_axis=0, tiled=True)  3.54 us
    pallas_call x2, Pallas kernels, add_grad(): pl.pallas_call(functools.partial(grad_kernel, carry), grid=(trades // til...  2.37 us
    select_n x1, other arithmetic, on_device(): jnp.where(type_late[:, None] == which, gain_rows[:, which][None, :], trad...  2.24 us
    pallas_call x1, Pallas kernels, net_own(): pl.pallas_call(netting_kernel, grid=(paths // span,), in_specs=[pl.BlockS...  1.99 us
    unnamed x8, local copies, waits for them, and re-layouts  1.34 us
  transfers between devices with their start and end apart: 5, of which 3 were waited for; matrix products, arithmetic and copies ran while one was open for 8% of the time, Pallas kernels for 2%

profile of v2, /device:TPU:0, one launch (start us, length us, event | category | flops | bytes accessed | tf_op | source)
XLA Modules:
  0.0 36.7 jit_solution(10073016422739337676)
XLA Ops:
  0.0 2.0 %shard_map.73 = (f32[16,4,8,256]{3,2,1,0:T(8,128)S(1)}, s32[1,256]{1,0:T(1,128)S(1)}, f32[1,256]{1,0:T(1,128)S(1)}) custom-call(bf16[4,128,256]{2,1,0:T(8,128)(2,1)} %basis_ref.1, bf16[1024,256]{1,0:T(8,128)(2,1)} %coef_ref.1, s32[1,1024]{1,0:T(1,128)} %bitcast.58, s32[1,1024]{1,0:T(1,128)} %bitcast.59, f32[4,16]{1,0:T(4,128)} %gain_ref.1, ...), custom_call_target="tpu_custom_call" | custom-call | tf_op jit(solution)/shard_map/pallas_call | solution.py:54
  2.0 0.8 %convert_element_type.12 = f16[16,4,8,256]{3,2,1,0:T(8,128)(2,1)} convert(f32[16,4,8,256]{3,2,1,0:T(8,128)S(1)} %get-tuple-element.13) | non-fusion elementwise | flops 131072 | bytes 786432 | tf_op jit(solution)/shard_map/convert_element_type | solution.py:210
  2.7 7.4 %all-to-all-start = ((f16[16,4,8,256]{3,2,1,0:T(8,128)(2,1)}), f16[16,4,8,256]{3,2,1,0:T(8,128)(2,1)S(1)}, u32[]{:S(2)}, u32[]{:S(2)}) async-start(f16[16,4,8,256]{3,2,1,0:T(8,128)(2,1)} %convert_element_type.12), calls=%async_computation | async-start | bytes 524288 | tf_op jit(solution)/shard_map/all_to_all | solution.py:211
  10.2 10.0 %all-to-all-done = f16[16,4,8,256]{3,2,1,0:T(8,128)(2,1)S(1)} async-done(((f16[16,4,8,256]{3,2,1,0:T(8,128)(2,1)}), f16[16,4,8,256]{3,2,1,0:T(8,128)(2,1)S(1)}, u32[]{:S(2)}, u32[]{:S(2)}) %all-to-all-start) | async-done | bytes 262176 | tf_op jit(solution)/shard_map/all_to_all | solution.py:211
  20.2 0.7 %shard_map.74 = bf16[8,64,256]{2,1,0:T(8,128)(2,1)} custom-call(f32[8,8,256]{2,1,0:T(8,128)S(1)} %convert_reduce_fusion.netted_ref, s32[1,256]{1,0:T(1,128)S(1)} %get-tuple-element.14.lags_ref, f32[1,256]{1,0:T(1,128)S(1)} %get-tuple-element.15.limits_ref), custom_call_target="tpu_custom_call" | custom-call | tf_op jit(solution)/shard_map/pallas_call | solution.py:117
  20.9 0.0 copy-start.3
  20.9 0.0 copy-start.2
  20.9 3.5 %all-to-all-start.1 = ((bf16[8,64,256]{2,1,0:T(8,128)(2,1)}), bf16[8,64,256]{2,1,0:T(8,128)(2,1)S(1)}, u32[]{:S(2)}, u32[]{:S(2)}) async-start(bf16[8,64,256]{2,1,0:T(8,128)(2,1)} %shard_map.74), calls=%async_computation.1 | async-start | bytes 524288 | tf_op jit(solution)/shard_map/all_to_all | solution.py:219
  24.5 0.0 copy-done.3
  24.5 0.0 copy-start
  24.5 0.1 collective-permute-start
  24.6 0.0 copy-done.2
  24.7 0.8 %copy-done = bf16[4,128,256]{2,1,0:T(8,128)(2,1)S(1)} copy-done((bf16[4,128,256]{2,1,0:T(8,128)(2,1)S(1)}, bf16[4,128,256]{2,1,0:T(8,128)(2,1)}, u32[]{:S(2)}) %copy-start) | copy-done | bytes 262168
  25.5 0.0 copy-start.1
  25.5 0.1 constant_dynamic-slice_fusion
  25.5 0.1 collective-permute-start.1
  25.6 0.5 %copy-done.1 = s32[1024]{0:T(1024)S(1)} copy-done((s32[1024]{0:T(1024)S(1)}, s32[1024]{0:T(1024)}, u32[]{:S(2)}) %copy-start.1) | copy-done | bytes 4120
  26.1 0.2 fusion.refs_0_.refs_1_
  26.4 0.0 collective-permute-done
  26.4 0.1 copy.11
  26.5 0.1 tile.12
  26.6 2.2 %select_select_fusion.refs_1_.refs_2_ = f32[1024,128]{1,0:T(8,128)S(1)} fusion(f32[128]{0:T(128)S(1)} %get-tuple-element.26, f32[128]{0:T(128)S(1)} %get-tuple-element.27, f32[128]{0:T(128)S(1)} %get-tuple-element.28, f32[128]{0:T(128)S(1)} %get-tuple-element.29, f32[128]{0:T(128)S(1)} %get-tuple-element.30, f32[128]{0:T(128)S(1)} %get-tuple-element.31, ...), kind=kLoop, calls=%fused_computation.3 | loop fusion | flops 2097152 | bytes 548864 | tf_op jit(solution)/shard_map/jit(_where)/select_n | solution.py:236
  28.8 4.8 %all-to-all-done.1 = bf16[8,64,256]{2,1,0:T(8,128)(2,1)S(1)} async-done(((bf16[8,64,256]{2,1,0:T(8,128)(2,1)}), bf16[8,64,256]{2,1,0:T(8,128)(2,1)S(1)}, u32[]{:S(2)}, u32[]{:S(2)}) %all-to-all-start.1) | async-done | bytes 262176 | tf_op jit(solution)/shard_map/all_to_all | solution.py:219
  33.6 0.0 collective-permute-start.2
  33.7 0.0 collective-permute-done.1
  33.7 0.1 copy.12
  33.8 0.8 %shard_map.75.refs_0_ = f32[1024,128]{1,0:T(8,128)S(1)} custom-call(bf16[1024,256]{1,0:T(8,128)(2,1)S(1)} %fusion.refs_0_.refs_1_, f32[1024,128]{1,0:T(8,128)S(1)} %select_select_fusion.refs_1_.refs_2_, bf16[512,256]{1,0:T(8,128)(2,1)S(1)} %bitcast.54, bf16[512,128]{1,0:T(8,128)(2,1)S(1)} %get-tuple-element.22.refs_3_), custom_call_target="tpu_custom_call" | custom-call | flops 402653184 | bytes 524288 | tf_op jit(solution)/shard_map/pallas_call | solution.py:161
  34.6 0.6 %collective-permute-done.2.refs_3_ = bf16[512,256]{1,0:T(8,128)(2,1)S(1)} collective-permute-done((bf16[512,256]{1,0:T(8,128)(2,1)S(1)}, bf16[512,256]{1,0:T(8,128)(2,1)S(1)}, u32[]{:S(2)}, u32[]{:S(2)}) %collective-permute-start.2) | collective-permute-done | bytes 262176 | tf_op jit(solution)/shard_map/ppermute | solution.py:241
  35.2 1.5 %shard_map.76 = f32[1024,128]{1,0:T(8,128)} custom-call(f32[1024,128]{1,0:T(8,128)S(1)} %shard_map.75.refs_0_, bf16[1024,256]{1,0:T(8,128)(2,1)S(1)} %fusion.refs_0_.refs_1_, f32[1024,128]{1,0:T(8,128)S(1)} %select_select_fusion.refs_1_.refs_2_, bf16[512,256]{1,0:T(8,128)(2,1)S(1)} %collective-permute-done.2.refs_3_, ...), custom_call_target="tpu_custom_call" | custom-call | flops 402653184 | bytes 524288 | tf_op jit(solution)/shard_map/pallas_call | solution.py:161
  (11 shorter events, 0.2 us)
Async XLA Ops:
  2.7 17.4 %all-to-all-start = ((f16[16,4,8,256]{3,2,1,0:T(8,128)(2,1)}), f16[16,4,8,256]{3,2,1,0:T(8,128)(2,1)S(1)}, u32[]{:S(2)}, u32[]{:S(2)}) async-start(f16[16,4,8,256]{3,2,1,0:T(8,128)(2,1)} %convert_element_type.12), calls=%async_computation | async-start | bytes 524288 | tf_op jit(solution)/shard_map/all_to_all | solution.py:211
  20.9 3.6 %copy-start.3 = (f32[4,16]{1,0:T(4,128)S(1)}, f32[4,16]{1,0:T(4,128)}, u32[]{:S(2)}) copy-start(f32[4,16]{1,0:T(4,128)} %gain_ref.1) | copy-start | bytes 772
  20.9 3.7 %copy-start.2 = (s32[1024]{0:T(1024)S(1)}, s32[1024]{0:T(1024)}, u32[]{:S(2)}) copy-start(s32[1024]{0:T(1024)} %param.10) | copy-start | bytes 12292
  20.9 12.7 %all-to-all-start.1 = ((bf16[8,64,256]{2,1,0:T(8,128)(2,1)}), bf16[8,64,256]{2,1,0:T(8,128)(2,1)S(1)}, u32[]{:S(2)}, u32[]{:S(2)}) async-start(bf16[8,64,256]{2,1,0:T(8,128)(2,1)} %shard_map.74), calls=%async_computation.1 | async-start | bytes 524288 | tf_op jit(solution)/shard_map/all_to_all | solution.py:219
  24.5 1.0 %copy-start = (bf16[4,128,256]{2,1,0:T(8,128)(2,1)S(1)}, bf16[4,128,256]{2,1,0:T(8,128)(2,1)}, u32[]{:S(2)}) copy-start(bf16[4,128,256]{2,1,0:T(8,128)(2,1)} %basis_ref.1) | copy-start | bytes 786436
  24.5 1.9 %collective-permute-start = (f32[4,16]{1,0:T(4,128)S(1)}, f32[4,16]{1,0:T(4,128)S(1)}, u32[]{:S(2)}, u32[]{:S(2)}) collective-permute-start(f32[4,16]{1,0:T(4,128)S(1)} %copy-done.3), channel_id=1, source_target_pairs={{0,1},{1,0},{2,3},{3,2},{4,5},{5,4},{6,7},{7,6},{8,9},{9,8},{10,11... | collective-permute-start | bytes 776 | tf_op jit(solution)/shard_map/ppermute | solution.py:188
  25.5 0.7 %copy-start.1 = (s32[1024]{0:T(1024)S(1)}, s32[1024]{0:T(1024)}, u32[]{:S(2)}) copy-start(s32[1024]{0:T(1024)} %param.9) | copy-start | bytes 12292
  25.5 8.1 %collective-permute-start.1 = (bf16[4,128,128]{2,1,0:T(8,128)(2,1)S(1)}, bf16[4,128,128]{2,1,0:T(8,128)(2,1)S(1)}, u32[]{:S(2)}, u32[]{:S(2)}) collective-permute-start(bf16[4,128,128]{2,1,0:T(8,128)(2,1)S(1)} %get-tuple-element.23), channel_id=1, source_target_pairs={{0,1},{1,0},{2,3},{3,2},{4,5},{5,4},{6,7},{7,6},{8,9},{9,8},{10,11... | collective-permute-start | bytes 393224 | tf_op jit(solution)/shard_map/ppermute | solution.py:188
  33.6 1.5 %collective-permute-start.2 = (bf16[512,256]{1,0:T(8,128)(2,1)S(1)}, bf16[512,256]{1,0:T(8,128)(2,1)S(1)}, u32[]{:S(2)}, u32[]{:S(2)}) collective-permute-start(bf16[512,256]{1,0:T(8,128)(2,1)S(1)} %bitcast.53), channel_id=1, source_target_pairs={{0,1},{1,0},{2,3},{3,2},{4,5},{5,4},{6,7},{7,6},{8,9},{9,8},{10,11... | collective-permute-start | bytes 786440 | tf_op jit(solution)/shard_map/ppermute | solution.py:241

commit v3 on v1

v3 whole, which is shorter than its diff:
```python
import functools
import math

import jax
import jax.numpy as jnp
from jax import lax
from jax.experimental import pallas as pl
from jax.experimental.pallas import tpu as pltpu
from jax.sharding import PartitionSpec as P

LAG_MAX = 2
SPAN = 64
NT = (((1,), (1,)), ((), ()))
TN = (((0,), (0,)), ((), ()))
TT = (((0,), (1,)), ((), ()))
PARAMS = pltpu.CompilerParams(vmem_limit_bytes=40 * 1024 * 1024)
SCALAR = pl.BlockSpec(memory_space=pltpu.SMEM)
LOCAL = pl.BlockSpec(memory_space=pltpu.VMEM)


def in_hbm(*arrays):
    return [pltpu.with_memory_space_constraint(array, pltpu.HBM) for array in arrays]


def kept(array):
    return pltpu.VMEM(array.shape, array.dtype)


def shifted(array, axis, step):
    peers = lax.axis_size(axis)
    return lax.ppermute(array, axis, [(i, (i + step) % peers) for i in range(peers)])


def gain_of_trades(gain, types):
    rows = jnp.zeros((gain.shape[0], types.shape[1]), jnp.float32)
    for which in range(gain.shape[1]):
        rows = jnp.where(types == which, gain[:, which : which + 1], rows)
    return rows


def net_paths(me, basis_ref, coef, gain, member, out_ref):
    dates, _, depth = basis_ref.shape
    peers, rows, set_count = out_ref.shape
    block_paths = rows // dates
    paths = peers * block_paths
    trades = coef.shape[0]
    span = math.gcd(paths, max(SPAN, block_paths))
    for first in range(0, paths, span):
        at = pl.multiple_of(me * paths + first, span)
        basis = basis_ref[:, pl.ds(at, span), :].reshape(dates * span, depth)
        raw = lax.dot_general(basis, coef, NT, preferred_element_type=jnp.float32)
        prices = raw.reshape(dates, span, trades) * gain[:, None, :]
        prices = prices.astype(jnp.bfloat16).reshape(dates * span, trades)
        netted = lax.dot_general(prices, member, NT, preferred_element_type=jnp.float32)
        netted = netted.reshape(dates, span // block_paths, block_paths, set_count)
        for date in range(dates):
            out_ref[
                pl.ds(first // block_paths, span // block_paths), pl.ds(date * block_paths, block_paths)
            ] = netted[date]


def first_net_kernel(
    me_ref, basis_ref, coef_ref, set_ref, type_ref, gain_ref, lags_ref, limits_ref, out_ref, member_ref, *copies
):
    set_count, trades = member_ref.shape
    member = lax.broadcasted_iota(jnp.int32, (set_count, trades), 0) == set_ref[...]
    member = member.astype(jnp.float32).astype(jnp.bfloat16)
    gain = gain_of_trades(gain_ref[...], type_ref[...])
    net_paths(me_ref[0], basis_ref, coef_ref[...], gain, member, out_ref)
    member_ref[...] = member
    for given, copy in zip((basis_ref, coef_ref, type_ref, gain_ref, lags_ref, limits_ref), copies, strict=True):
        copy[...] = given[...]


def next_net_kernel(me_ref, basis_ref, coef_ref, type_ref, gain_ref, member_ref, out_ref):
    gain = gain_of_trades(gain_ref[...], type_ref[...])
    net_paths(me_ref[0], basis_ref, coef_ref[...], gain, member_ref[...], out_ref)


def pricing_cost(basis, coef, set_count, owners):
    dates, paths, depth = basis.shape
    return pl.CostEstimate(
        flops=2 * dates * paths // owners * coef.shape[0] * (depth + set_count),
        bytes_accessed=coef.size * 2,
        transcendentals=0,
    )


def net_first(me, basis, coef, sets, types, gain, lags, limits, peers, owners):
    dates, paths, _ = basis.shape
    set_count = limits.shape[1]
    block_paths = paths // (peers * owners)
    return pl.pallas_call(
        first_net_kernel,
        in_specs=[SCALAR] + [LOCAL] * 7,
        out_specs=[LOCAL] * 8,
        out_shape=[
            pltpu.VMEM((peers, dates * block_paths, set_count), jnp.float32),
            pltpu.VMEM((set_count, coef.shape[0]), jnp.bfloat16),
        ]
        + [kept(array) for array in (basis, coef, types, gain, lags, limits)],
        compiler_params=PARAMS,
        cost_estimate=pricing_cost(basis, coef, set_count, owners),
    )(me, *in_hbm(basis, coef, sets, types, gain, lags, limits))


def net_next(me, basis, coef, types, gain, member, like, owners):
    return pl.pallas_call(
        next_net_kernel,
        in_specs=[SCALAR] + [LOCAL] * 5,
        out_specs=LOCAL,
        out_shape=kept(like),
        compiler_params=PARAMS,
        cost_estimate=pricing_cost(basis, coef, member.shape[0], owners),
    )(me, basis, coef, types, gain, member)


def adjoint_kernel(scale, owners, block_paths, me_ref, netted_ref, lags_ref, limits_ref, out_ref):
    rows, set_count = netted_ref.shape
    local_rows = rows // owners
    local_dates = local_rows // block_paths
    dates = owners * local_dates
    lag = lags_ref[...]
    masks = [(lag == value).astype(jnp.float32) for value in range(1, LAG_MAX + 1)]
    places = [
        pl.multiple_of(lax.rem(me_ref[0] + owners - owner, owners) * local_rows, local_rows)
        for owner in range(owners)
    ]
    netted = []
    for place in places:
        block = netted_ref[pl.ds(place, local_rows)]
        netted += [block[i : i + block_paths] for i in range(0, local_rows, block_paths)]
    direct = []
    for date in range(dates):
        collateral = jnp.zeros_like(netted[date])
        for value, mask in enumerate(masks, 1):
            if date >= value:
                collateral = collateral + mask * netted[date - value]
        direct.append(jnp.maximum(netted[date] - collateral - limits_ref[...], 0.0) * scale)
    adjoints = []
    for date in range(dates):
        adjoint = direct[date]
        for value, mask in enumerate(masks, 1):
            if date + value < dates:
                adjoint = adjoint - mask * direct[date + value]
        adjoints.append(adjoint)
    for owner, place in enumerate(places):
        block = jnp.concatenate(adjoints[owner * local_dates : (owner + 1) * local_dates], axis=0)
        block = block.astype(jnp.bfloat16)
        for peer in range(out_ref.shape[0]):
            out_ref[peer, pl.ds(place, local_rows)] = block


def adjoint_of(me, netted, lags, limits, scale, owners, block_paths, peers):
    return pl.pallas_call(
        functools.partial(adjoint_kernel, scale, owners, block_paths),
        in_specs=[SCALAR] + [LOCAL] * 3,
        out_specs=LOCAL,
        out_shape=pltpu.VMEM((peers,) + netted.shape, jnp.bfloat16),
        compiler_params=PARAMS,
    )(me, netted, lags, limits)


def grad_of(member, adjoint_ref, gain, basis):
    peers, rows, set_count = adjoint_ref.shape
    period = gain.shape[1]
    total = None
    together = min(peers, max(1, 512 // rows))
    for first in range(0, peers, together):
        adjoint = adjoint_ref[pl.ds(first, together)].reshape(together * rows, set_count)
        spread = lax.dot_general(member, adjoint, TT, preferred_element_type=jnp.float32)
        scaled = [
            (spread[:, at : at + period] * gain).astype(jnp.bfloat16) for at in range(0, together * rows, period)
        ]
        part = jnp.dot(
            jnp.concatenate(scaled, axis=1),
            basis[first * rows : (first + together) * rows],
            preferred_element_type=jnp.float32,
        )
        total = part if total is None else total + part
    return total


def first_grad_kernel(owners, *refs):
    me_ref, member_ref, adjoint_ref, type_ref = refs[:4]
    gain_refs, basis_refs = refs[4 : 4 + owners], refs[4 + owners : 4 + 2 * owners]
    out_ref, *later_refs = refs[4 + 2 * owners :]
    local_dates, paths, _ = basis_refs[0].shape
    peers, rows, _ = adjoint_ref.shape
    trades, own_depth = out_ref.shape
    local_rows = rows // owners
    block_paths = local_rows // local_dates
    core_paths = peers * block_paths
    me = me_ref[0]
    columns = pl.ds(pl.multiple_of(me * own_depth, own_depth), own_depth)
    orders = [[(step + place) % owners for place in range(owners)] for step in range(owners)]
    basis = []
    for step, order in enumerate(orders):
        sender = lax.rem(me + owners - step, owners)
        at = pl.ds(pl.multiple_of(sender * core_paths, core_paths), core_paths)
        parts = []
        for which in order:
            part = basis_refs[which][:, at, columns].astype(jnp.float32)
            part = part.reshape(local_dates, peers, block_paths, own_depth)
            parts.append(jnp.concatenate([part[date] for date in range(local_dates)], axis=1))
        block = jnp.concatenate(parts, axis=1).reshape(peers * rows, own_depth)
        basis.append(block.astype(jnp.bfloat16))
    period = rows
    while period % 128:
        period *= 2
    dates = owners * local_dates
    rest = jnp.concatenate([gain_of_trades(ref[...], type_ref[...]) for ref in gain_refs], axis=0)
    pieces = []
    for _ in range(3):
        piece = rest.astype(jnp.bfloat16).astype(jnp.float32)
        pieces.append(piece)
        rest = rest - piece
    pieces = jnp.concatenate(pieces, axis=0).astype(jnp.bfloat16)
    lane = lax.broadcasted_iota(jnp.int32, (3 * dates, period), 1)
    have = lax.rem(lax.broadcasted_iota(jnp.int32, (3 * dates, period), 0), dates)
    gain = []
    for step in range(owners):
        want = lax.rem(lax.div(lane, block_paths) + step * local_dates, dates)
        expand = (want == have).astype(jnp.float32).astype(jnp.bfloat16)
        gain.append(lax.dot_general(pieces, expand, TN, preferred_element_type=jnp.float32))
    out_ref[...] = grad_of(member_ref[...], adjoint_ref, gain[0], basis[0])
    for ref, value in zip(later_refs, gain[1:] + basis[1:], strict=True):
        ref[...] = value


def next_grad_kernel(member_ref, adjoint_ref, gain_ref, basis_ref, total_ref, out_ref):
    out_ref[...] = total_ref[...] + grad_of(member_ref[...], adjoint_ref, gain_ref[...], basis_ref[...])


def grad_cost(member, adjoint, own_depth):
    set_count, trades = member.shape
    peers, rows, _ = adjoint.shape
    return pl.CostEstimate(
        flops=2 * trades * peers * rows * (set_count + own_depth),
        bytes_accessed=4 * trades * own_depth,
        transcendentals=0,
    )


def on_device(basis_values, coefficients, set_map, trade_type, type_gain, set_lags, thresholds):
    local_dates, path_count, depth = basis_values.shape
    trades = coefficients.shape[0]
    set_count = thresholds.shape[0]
    peers = lax.axis_size("trades")
    owners = lax.axis_size("dates")
    block_paths = path_count // (peers * owners)
    rows = owners * local_dates * block_paths
    own_depth = depth // owners
    scale = 2.0 / math.sqrt(local_dates * owners * path_count)
    me = lax.axis_index("dates").astype(jnp.int32).reshape(1)

    bases = [shifted(basis_values, "dates", step) for step in range(1, owners)]
    gains = [shifted(type_gain, "dates", step) for step in range(1, owners)]
    partial, member, basis, coef, types, gain, lags, limits = net_first(
        me,
        basis_values,
        coefficients,
        set_map.reshape(1, trades),
        trade_type.reshape(1, trades),
        type_gain,
        set_lags.reshape(1, set_count),
        thresholds.reshape(1, set_count),
        peers,
        owners,
    )
    partials = [partial]
    for other_basis, other_gain in zip(bases, gains, strict=True):
        partials.append(net_next(me, other_basis, coef, types, other_gain, member, partial, owners))
    bases, gains = [basis] + bases, [gain] + gains

    partials = jnp.concatenate(partials, axis=1).astype(jnp.float16)
    arrived = lax.all_to_all(partials, "trades", split_axis=0, concat_axis=0, tiled=True)
    netted = jnp.sum(arrived.astype(jnp.float32), axis=0)
    adjoint = adjoint_of(me, netted, lags, limits, scale, owners, block_paths, peers)
    adjoint = lax.all_to_all(adjoint, "trades", split_axis=0, concat_axis=0, tiled=True)

    adjoints = [adjoint] + [shifted(adjoint, "dates", step) for step in range(1, owners)]
    period = math.lcm(rows, 128)
    later = owners - 1
    total, *ready = pl.pallas_call(
        functools.partial(first_grad_kernel, owners),
        in_specs=[SCALAR] + [LOCAL] * (3 + 2 * owners),
        out_specs=[LOCAL] * (1 + 2 * later),
        out_shape=[pltpu.VMEM((trades, own_depth), jnp.float32)]
        + [pltpu.VMEM((trades, period), jnp.float32)] * later
        + [pltpu.VMEM((peers * rows, own_depth), jnp.bfloat16)] * later,
        compiler_params=PARAMS,
        cost_estimate=grad_cost(member, adjoint, own_depth),
    )(me, member, adjoint, types, *gains, *bases)
    for step in range(later):
        last = step == later - 1
        total = pl.pallas_call(
            next_grad_kernel,
            in_specs=[LOCAL] * 5,
            out_specs=LOCAL,
            out_shape=jax.ShapeDtypeStruct(total.shape, total.dtype) if last else kept(total),
            compiler_params=PARAMS,
            cost_estimate=grad_cost(member, adjoint, own_depth),
        )(member, adjoints[step + 1], ready[step], ready[later + step], total)
    return total


def solution(mesh):
    return jax.shard_map(
        on_device,
        mesh=mesh,
        in_specs=(
            P("dates", "groups", None),
            P("trades", None),
            P("trades"),
            P("trades"),
            P("dates", None),
            P(),
            P(),
        ),
        out_specs=P(("groups", "trades"), "dates"),
        check_vma=False,
    )
```

time: 40.4 us -> 34.5 us (0.85)
  blocking collectives: 0 us -> 28.1 us
  waiting for transfers between devices: 21.9 us -> 0.36 us
  starting transfers between devices: 11.1 us -> 0.51 us
  matrix products: 5.31 us -> 0 us
  Pallas kernels: 0 us -> 5.11 us
  local copies, waits for them, and re-layouts: 1.51 us -> 0 us
    all_to_all x0 -> x2, blocking collectives: none -> 28.1 us  [the longest x1 16.1 us: on_device(): lax.all_to_all(partials, 'trades', split_axis=0, concat_axis=0, tiled=True)]
    all_to_all x2 -> x0, waiting for transfers between devices: 20 us -> none  [the longest x1 10 us: on_device(): lax.all_to_all(partial, ('trades', 'dates'), split_axis=0, concat_axis=0,...]
    all_to_all x2 -> x0, starting transfers between devices: 11 us -> none  [the longest x1 7.49 us: on_device(): lax.all_to_all(partial, ('trades', 'dates'), split_axis=0, concat_axis=0,...]
    dot_general x5 -> x0, matrix products: 5.31 us -> none  [the longest x1 1.81 us: on_device(): partial = jnp.dot(prices, member, preferred_element_type=jnp.float32)]
    pallas_call x0 -> x5, Pallas kernels: none -> 5.11 us  [the longest x1 1.77 us: net_first(): pl.pallas_call(first_net_kernel, in_specs=[SCALAR] + [LOCAL] * 7, out_spe...]
    ppermute x1 -> x3, waiting for transfers between devices: 1.89 us -> 0.36 us  [shifted(): lax.ppermute(array, axis, [(i, (i + step) % peers) for i in range(peers)])]
    convert_element_type x1 -> x0, local copies, waits for them, and re-layouts: 0.75 us -> none  [on_device(): partial = partial.astype(jnp.float16)]
    broadcast_in_dim x1 -> x0, local copies, waits for them, and re-layouts: 0.73 us -> none  [on_device(): adjoint = jnp.broadcast_to(adjoint, (trade_peers,) + adjoint.shape[1:])]
  transfers between devices with their start and end apart: 3 -> 3, of which waited for: 3 -> 1; matrix products, arithmetic and copies ran while one was open for 0% -> 0% of each run, Pallas kernels for 0% -> 9%
where the time goes in v3:
time: 34.5 us; the launch traced here: 34.3 us
  blocking collectives  28.1 us (81%)
  Pallas kernels  5.11 us (15%)
  starting transfers between devices  0.51 us (1%)
  waiting for transfers between devices  0.36 us (1%)
    all_to_all x1, blocking collectives, on_device(): lax.all_to_all(partials, 'trades', split_axis=0, concat_axis=0, tiled=True)  16.1 us
    all_to_all x1, blocking collectives, on_device(): lax.all_to_all(adjoint, 'trades', split_axis=0, concat_axis=0, tiled=True)  12 us
    pallas_call x1, Pallas kernels, net_first(): pl.pallas_call(first_net_kernel, in_specs=[SCALAR] + [LOCAL] * 7, out_spe...  1.77 us
    pallas_call x1, Pallas kernels, on_device(): pl.pallas_call(next_grad_kernel, in_specs=[LOCAL] * 5, out_specs=LOCAL, o...  1.55 us
    pallas_call x1, Pallas kernels, on_device(): pl.pallas_call(functools.partial(first_grad_kernel, owners), in_specs=[SC...  1.17 us
  transfers between devices with their start and end apart: 3, of which 1 were waited for; matrix products, arithmetic and copies ran while one was open for 0% of the time, Pallas kernels for 9%

profile of v3, /device:TPU:0, one launch (start us, length us, event | category | flops | bytes accessed | tf_op | source)
XLA Modules:
  0.0 34.3 jit_solution(5410752451928524522)
XLA Ops:
  0.0 0.5 %collective-permute-start = (bf16[4,128,256]{2,1,0:T(8,128)(2,1)}, bf16[4,128,256]{2,1,0:T(8,128)(2,1)S(1)}, u32[]{:S(2)}, u32[]{:S(2)}) collective-permute-start(bf16[4,128,256]{2,1,0:T(8,128)(2,1)} %basis_ref.1), channel_id=1, source_target_pairs={{0,1},{1,0},{2,3},{3,2},{4,5},{5,4},{6,7},{7,6},{8,9},{9,8},{10,11... | collective-permute-start | bytes 786440 | tf_op jit(solution)/shard_map/ppermute | solution.py:31
  0.5 0.1 collective-permute-start.1
  0.5 1.8 %shard_map.73 = (f32[8,32,256]{2,1,0:T(8,128)S(1)}, bf16[256,1024]{1,0:T(8,128)(2,1)S(1)}, bf16[4,128,256]{2,1,0:T(8,128)(2,1)S(1)}, bf16[1024,256]{1,0:T(8,128)...) custom-call(s32[1]{0:T(128)} %bitcast.me_ref.refs_0_, ...), custom_call_target="tpu_custom_call" | custom-call | flops 268435456 | bytes 524288 | tf_op jit(solution)/shard_map/pallas_call | solution.py:93
  2.3 0.0 collective-permute-done.1.gain_ref.refs_5_
  2.3 0.0 collective-permute-done.basis_ref.refs_7_
  2.3 0.6 %shard_map.74 = f32[8,32,256]{2,1,0:T(8,128)S(1)} custom-call(s32[1]{0:T(128)} %bitcast.me_ref.refs_0_, bf16[4,128,256]{2,1,0:T(8,128)(2,1)S(1)} %collective-permute-done.basis_ref.refs_7_, bf16[1024,256]{1,0:T(8,128)(2,1)S(1)} %get-tuple-element.18.coef_ref, s32[1,1024]{1,0:T(1,128)S(1)} %get-tuple-element.19.type_ref.refs_3_, ...), custom_call_target="tpu_custom_call" | custom-call | flops 268435456 | bytes 524288 | tf_op jit(solution)/shard_map/pallas_call | solution.py:108
  2.9 0.1 pad_maximum_fusion
  3.0 16.1 %all_to_all.10 = f16[8,64,256]{2,1,0:T(8,128)(2,1)S(1)} all-to-all(f16[8,64,256]{2,1,0:T(8,128)(2,1)S(1)} %pad_maximum_fusion), channel_id=1, replica_groups=mesh['groups'=2,'trades'=8,'dates'=2] {'trades'}, dimensions={0} | all-to-all | bytes 524288 | tf_op jit(solution)/shard_map/all_to_all | solution.py:277
  19.2 12.0 %all_to_all.11.refs_2_ = bf16[8,64,256]{2,1,0:T(8,128)(2,1)S(1)} all-to-all(bf16[8,64,256]{2,1,0:T(8,128)(2,1)S(1)} %shard_map.75), channel_id=1, replica_groups=mesh['groups'=2,'trades'=8,'dates'=2] {'trades'}, dimensions={0} | all-to-all | bytes 524288 | tf_op jit(solution)/shard_map/all_to_all | solution.py:280
  31.2 0.0 collective-permute-start.2
  31.2 1.2 %shard_map.76 = (f32[1024,128]{1,0:T(8,128)S(1)}, f32[1024,128]{1,0:T(8,128)S(1)}, bf16[512,128]{1,0:T(8,128)(2,1)S(1)}) custom-call(s32[1]{0:T(128)} %bitcast.me_ref.refs_0_, bf16[256,1024]{1,0:T(8,128)(2,1)S(1)} %get-tuple-element.16.member_ref.refs_1_, bf16[8,64,256]{2,1,0:T(8,128)(2,1)S(1)} %all_to_all.11.refs_2_, ...), custom_call_target="tpu_custom_call" | custom-call | flops 402653184 | bytes 524288 | tf_op jit(solution)/shard_map/pallas_call | solution.py:285
  32.4 0.4 %collective-permute-done.2.adjoint_ref = bf16[8,64,256]{2,1,0:T(8,128)(2,1)S(1)} collective-permute-done((bf16[8,64,256]{2,1,0:T(8,128)(2,1)S(1)}, bf16[8,64,256]{2,1,0:T(8,128)(2,1)S(1)}, u32[]{:S(2)}, u32[]{:S(2)}) %collective-permute-start.2) | collective-permute-done | bytes 262176 | tf_op jit(solution)/shard_map/ppermute | solution.py:31
  32.7 1.5 %shard_map.77 = f32[1024,128]{1,0:T(8,128)} custom-call(bf16[256,1024]{1,0:T(8,128)(2,1)S(1)} %get-tuple-element.16.member_ref.refs_1_, bf16[8,64,256]{2,1,0:T(8,128)(2,1)S(1)} %collective-permute-done.2.adjoint_ref, f32[1024,128]{1,0:T(8,128)S(1)} %get-tuple-element.24.gain_ref, bf16[512,128]{1,0:T(8,128)(2,1)S(1)} %get-tuple-element.25.basis_ref, ...), custom_call_target="tpu_custom_call" | custom-call | flops 402653184 | bytes 524288 | tf_op jit(solution)/shard_map/pallas_call | solution.py:297
  (4 shorter events, 0.1 us)
Async XLA Ops:
  0.0 2.3 %collective-permute-start = (bf16[4,128,256]{2,1,0:T(8,128)(2,1)}, bf16[4,128,256]{2,1,0:T(8,128)(2,1)S(1)}, u32[]{:S(2)}, u32[]{:S(2)}) collective-permute-start(bf16[4,128,256]{2,1,0:T(8,128)(2,1)} %basis_ref.1), channel_id=1, source_target_pairs={{0,1},{1,0},{2,3},{3,2},{4,5},{5,4},{6,7},{7,6},{8,9},{9,8},{10,11... | collective-permute-start | bytes 786440 | tf_op jit(solution)/shard_map/ppermute | solution.py:31
  0.5 1.9 %collective-permute-start.1 = (f32[4,16]{1,0:T(4,128)}, f32[4,16]{1,0:T(4,128)S(1)}, u32[]{:S(2)}, u32[]{:S(2)}) collective-permute-start(f32[4,16]{1,0:T(4,128)} %gain_ref.1), channel_id=1, source_target_pairs={{0,1},{1,0},{2,3},{3,2},{4,5},{5,4},{6,7},{7,6},{8,9},{9,8},{10,11... | collective-permute-start | bytes 776 | tf_op jit(solution)/shard_map/ppermute | solution.py:31
  31.2 1.5 %collective-permute-start.2 = (bf16[8,64,256]{2,1,0:T(8,128)(2,1)S(1)}, bf16[8,64,256]{2,1,0:T(8,128)(2,1)S(1)}, u32[]{:S(2)}, u32[]{:S(2)}) collective-permute-start(bf16[8,64,256]{2,1,0:T(8,128)(2,1)S(1)} %all_to_all.11.refs_2_), channel_id=1, source_target_pairs={{0,1},{1,0},{2,3},{3,2},{4,5},{5,4},{6,7},{7,6},{8,9},{9,8},{10,11... | collective-permute-start | bytes 786440 | tf_op jit(solution)/shard_map/ppermute | solution.py:31

commit v4 on v3

--- a/solution.py
+++ b/solution.py
@@ -38,8 +38,9 @@
     return rows
 
 
-def net_paths(me, basis_ref, coef, gain, member, out_ref):
-    dates, _, depth = basis_ref.shape
+def net_paths(me, basis_refs, coef, gain, member, out_ref):
+    dates = gain.shape[0]
+    depth = coef.shape[1]
     peers, rows, set_count = out_ref.shape
     block_paths = rows // dates
     paths = peers * block_paths
@@ -47,7 +48,8 @@
     span = math.gcd(paths, max(SPAN, block_paths))
     for first in range(0, paths, span):
         at = pl.multiple_of(me * paths + first, span)
-        basis = basis_ref[:, pl.ds(at, span), :].reshape(dates * span, depth)
+        basis = jnp.concatenate([ref[:, pl.ds(at, span), :] for ref in basis_refs], axis=0)
+        basis = basis.reshape(dates * span, depth)
         raw = lax.dot_general(basis, coef, NT, preferred_element_type=jnp.float32)
         prices = raw.reshape(dates, span, trades) * gain[:, None, :]
         prices = prices.astype(jnp.bfloat16).reshape(dates * span, trades)
@@ -59,60 +61,63 @@
             ] = netted[date]
 
 
-def first_net_kernel(
-    me_ref, basis_ref, coef_ref, set_ref, type_ref, gain_ref, lags_ref, limits_ref, out_ref, member_ref, *copies
-):
+def load_kernel(*refs):
+    given, (member_ref, gain_rows_ref, *copies), (set_ref, arrived) = refs[:7], refs[7:-2], refs[-2:]
     set_count, trades = member_ref.shape
+    type_ref, gain_ref = copies[2:4]
+    moves = [
+        pltpu.make_async_copy(source, target, arrived.at[at])
+        for at, (source, target) in enumerate(zip(given, copies + [set_ref], strict=True))
+    ]
+    basis_move, coef_move, type_move, gain_move, lags_move, limits_move, set_move = moves
+    for move in (set_move, type_move, gain_move, basis_move, coef_move, lags_move, limits_move):
+        move.start()
+    set_move.wait()
     member = lax.broadcasted_iota(jnp.int32, (set_count, trades), 0) == set_ref[...]
-    member = member.astype(jnp.float32).astype(jnp.bfloat16)
-    gain = gain_of_trades(gain_ref[...], type_ref[...])
-    net_paths(me_ref[0], basis_ref, coef_ref[...], gain, member, out_ref)
-    member_ref[...] = member
-    for given, copy in zip((basis_ref, coef_ref, type_ref, gain_ref, lags_ref, limits_ref), copies, strict=True):
-        copy[...] = given[...]
-
-
-def next_net_kernel(me_ref, basis_ref, coef_ref, type_ref, gain_ref, member_ref, out_ref):
-    gain = gain_of_trades(gain_ref[...], type_ref[...])
-    net_paths(me_ref[0], basis_ref, coef_ref[...], gain, member_ref[...], out_ref)
-
-
-def pricing_cost(basis, coef, set_count, owners):
-    dates, paths, depth = basis.shape
-    return pl.CostEstimate(
-        flops=2 * dates * paths // owners * coef.shape[0] * (depth + set_count),
-        bytes_accessed=coef.size * 2,
-        transcendentals=0,
-    )
-
-
-def net_first(me, basis, coef, sets, types, gain, lags, limits, peers, owners):
-    dates, paths, _ = basis.shape
-    set_count = limits.shape[1]
-    block_paths = paths // (peers * owners)
+    member_ref[...] = member.astype(jnp.float32).astype(jnp.bfloat16)
+    type_move.wait()
+    gain_move.wait()
+    gain_rows_ref[...] = gain_of_trades(gain_ref[...], type_ref[...])
+    basis_move.wait()
+    coef_move.wait()
+    lags_move.wait()
+    limits_move.wait()
+
+
+def net_kernel(owners, me_ref, coef_ref, type_ref, member_ref, gain_rows_ref, *refs):
+    bases, gains, out_ref = refs[:owners], refs[owners:-1], refs[-1]
+    rows = [gain_rows_ref[...]] + [gain_of_trades(ref[...], type_ref[...]) for ref in gains]
+    net_paths(me_ref[0], bases, coef_ref[...], jnp.concatenate(rows, axis=0), member_ref[...], out_ref)
+
+
+def load(basis, coef, sets, types, gain, lags, limits):
+    trades = coef.shape[0]
     return pl.pallas_call(
-        first_net_kernel,
-        in_specs=[SCALAR] + [LOCAL] * 7,
+        load_kernel,
+        in_specs=[pl.BlockSpec(memory_space=pl.ANY)] * 7,
         out_specs=[LOCAL] * 8,
         out_shape=[
-            pltpu.VMEM((peers, dates * block_paths, set_count), jnp.float32),
-            pltpu.VMEM((set_count, coef.shape[0]), jnp.bfloat16),
+            pltpu.VMEM((limits.shape[1], trades), jnp.bfloat16),
+            pltpu.VMEM((gain.shape[0], trades), jnp.float32),
         ]
         + [kept(array) for array in (basis, coef, types, gain, lags, limits)],
+        scratch_shapes=[pltpu.VMEM(sets.shape, sets.dtype), pltpu.SemaphoreType.DMA((7,))],
         compiler_params=PARAMS,
-        cost_estimate=pricing_cost(basis, coef, set_count, owners),
-    )(me, *in_hbm(basis, coef, sets, types, gain, lags, limits))
-
-
-def net_next(me, basis, coef, types, gain, member, like, owners):
+        cost_estimate=pl.CostEstimate(flops=coef.size * 512, bytes_accessed=coef.size * 2, transcendentals=0),
+    )(*in_hbm(basis, coef, types, gain, lags, limits, sets))
+
+
+def net(me, coef, types, member, gain_rows, bases, later_gains, peers):
+    owners = len(bases)
+    dates, paths, _ = bases[0].shape
+    rows = dates * paths // peers
     return pl.pallas_call(
-        next_net_kernel,
-        in_specs=[SCALAR] + [LOCAL] * 5,
+        functools.partial(net_kernel, owners),
+        in_specs=[SCALAR] + [LOCAL] * (3 + 2 * owners),
         out_specs=LOCAL,
-        out_shape=kept(like),
+        out_shape=pltpu.VMEM((peers, rows, member.shape[0]), jnp.float32),
         compiler_params=PARAMS,
-        cost_estimate=pricing_cost(basis, coef, member.shape[0], owners),
-    )(me, basis, coef, types, gain, member)
+    )(me, coef, types, member, gain_rows, *bases, *later_gains)
 
 
 def adjoint_kernel(scale, owners, block_paths, me_ref, netted_ref, lags_ref, limits_ref, out_ref):
@@ -256,8 +261,7 @@
 
     bases = [shifted(basis_values, "dates", step) for step in range(1, owners)]
     gains = [shifted(type_gain, "dates", step) for step in range(1, owners)]
-    partial, member, basis, coef, types, gain, lags, limits = net_first(
-        me,
+    member, gain_rows, basis, coef, types, gain, lags, limits = load(
         basis_values,
         coefficients,
         set_map.reshape(1, trades),
@@ -265,15 +269,9 @@
         type_gain,
         set_lags.reshape(1, set_count),
         thresholds.reshape(1, set_count),
-        peers,
-        owners,
     )
-    partials = [partial]
-    for other_basis, other_gain in zip(bases, gains, strict=True):
-        partials.append(net_next(me, other_basis, coef, types, other_gain, member, partial, owners))
     bases, gains = [basis] + bases, [gain] + gains
-
-    partials = jnp.concatenate(partials, axis=1).astype(jnp.float16)
+    partials = net(me, coef, types, member, gain_rows, bases, gains[1:], peers).astype(jnp.float16)
     arrived = lax.all_to_all(partials, "trades", split_axis=0, concat_axis=0, tiled=True)
     netted = jnp.sum(arrived.astype(jnp.float32), axis=0)
     adjoint = adjoint_of(me, netted, lags, limits, scale, owners, block_paths, peers)

time: 34.5 us -> 34.3 us (level)
  transfers between devices with their start and end apart: 3 -> 3, of which waited for: 1 -> 2; matrix products, arithmetic and copies ran while one was open for 0% -> 0% of each run, Pallas kernels for 9% -> 7%
where the time goes in v4:
time: 34.3 us; the launch traced here: 34 us
  blocking collectives  28.1 us (82%)
  Pallas kernels  4.84 us (14%)
  starting transfers between devices  0.51 us (1%)
  waiting for transfers between devices  0.43 us (1%)
    all_to_all x1, blocking collectives, on_device(): lax.all_to_all(partials, 'trades', split_axis=0, concat_axis=0, tiled=True)  16.2 us
    all_to_all x1, blocking collectives, on_device(): lax.all_to_all(adjoint, 'trades', split_axis=0, concat_axis=0, tiled=True)  12 us
    pallas_call x1, Pallas kernels, on_device(): pl.pallas_call(next_grad_kernel, in_specs=[LOCAL] * 5, out_specs=LOCAL, o...  1.54 us
    pallas_call x1, Pallas kernels, load(): pl.pallas_call(load_kernel, in_specs=[pl.BlockSpec(memory_space=pl.ANY)]...  1.23 us
    pallas_call x1, Pallas kernels, on_device(): pl.pallas_call(functools.partial(first_grad_kernel, owners), in_specs=[SC...  1.17 us
    pallas_call x1, Pallas kernels, net(): pl.pallas_call(functools.partial(net_kernel, owners), in_specs=[SCALAR] +...  0.85 us
  transfers between devices with their start and end apart: 3, of which 2 were waited for; matrix products, arithmetic and copies ran while one was open for 0% of the time, Pallas kernels for 7%

profile of v4, /device:TPU:0, one launch (start us, length us, event | category | flops | bytes accessed | tf_op | source)
XLA Modules:
  0.0 34.0 jit_solution(15382060186177002843)
XLA Ops:
  0.0 0.5 %collective-permute-start = (bf16[4,128,256]{2,1,0:T(8,128)(2,1)}, bf16[4,128,256]{2,1,0:T(8,128)(2,1)S(1)}, u32[]{:S(2)}, u32[]{:S(2)}) collective-permute-start(bf16[4,128,256]{2,1,0:T(8,128)(2,1)} %refs_0_.1), channel_id=1, source_target_pairs={{0,1},{1,0},{2,3},{3,2},{4,5},{5,4},{6,7},{7,6},{8,9},{9,8},{10,11... | collective-permute-start | bytes 786440 | tf_op jit(solution)/shard_map/ppermute | solution.py:31
  0.5 0.1 collective-permute-start.1
  0.5 1.2 %shard_map.73 = (bf16[256,1024]{1,0:T(8,128)(2,1)S(1)}, f32[4,1024]{1,0:T(4,128)S(1)}, bf16[4,128,256]{2,1,0:T(8,128)(2,1)S(1)}, bf16[1024,256]{1,0:T(8,128)(2,1...) custom-call(bf16[4,128,256]{2,1,0:T(8,128)(2,1)} %refs_0_.1, ...), custom_call_target="tpu_custom_call" | custom-call | flops 134217728 | bytes 524288 | tf_op jit(solution)/shard_map/pallas_call | solution.py:95
  1.8 0.1 collective-permute-done.1.refs_2_.refs_5_
  1.8 0.0 collective-permute-done.refs_1_.refs_7_
  1.8 0.8 %shard_map.74 = f32[8,64,256]{2,1,0:T(8,128)S(1)} custom-call(s32[1]{0:T(128)} %bitcast.4.me_ref.refs_0_, bf16[1024,256]{1,0:T(8,128)(2,1)S(1)} %get-tuple-element.17.coef_ref, s32[1,1024]{1,0:T(1,128)S(1)} %get-tuple-element.18.type_ref.refs_3_, bf16[256,1024]{1,0:T(8,128)(2,1)S(1)} %get-tuple-element.16.member_ref.refs_1_, ...), custom_call_target="tpu_custom_call" | custom-call | tf_op jit(solution)/shard_map/pallas_call | solution.py:114
  2.7 16.2 %all_to_all.10 = f16[8,64,256]{2,1,0:T(8,128)(2,1)S(1)} all-to-all(f16[8,64,256]{2,1,0:T(8,128)(2,1)S(1)} %convert_element_type.6), channel_id=1, replica_groups=mesh['groups'=2,'trades'=8,'dates'=2] {'trades'}, dimensions={0} | all-to-all | bytes 524288 | tf_op jit(solution)/shard_map/all_to_all | solution.py:275
  19.0 12.0 %all_to_all.11.refs_2_ = bf16[8,64,256]{2,1,0:T(8,128)(2,1)S(1)} all-to-all(bf16[8,64,256]{2,1,0:T(8,128)(2,1)S(1)} %shard_map.75), channel_id=1, replica_groups=mesh['groups'=2,'trades'=8,'dates'=2] {'trades'}, dimensions={0} | all-to-all | bytes 524288 | tf_op jit(solution)/shard_map/all_to_all | solution.py:278
  31.0 0.0 collective-permute-start.2
  31.0 1.2 %shard_map.76 = (f32[1024,128]{1,0:T(8,128)S(1)}, f32[1024,128]{1,0:T(8,128)S(1)}, bf16[512,128]{1,0:T(8,128)(2,1)S(1)}) custom-call(s32[1]{0:T(128)} %bitcast.4.me_ref.refs_0_, bf16[256,1024]{1,0:T(8,128)(2,1)S(1)} %get-tuple-element.16.member_ref.refs_1_, bf16[8,64,256]{2,1,0:T(8,128)(2,1)S(1)} %all_to_all.11.refs_2_, ...), custom_call_target="tpu_custom_call" | custom-call | flops 402653184 | bytes 524288 | tf_op jit(solution)/shard_map/pallas_call | solution.py:283
  32.1 0.4 %collective-permute-done.2.adjoint_ref = bf16[8,64,256]{2,1,0:T(8,128)(2,1)S(1)} collective-permute-done((bf16[8,64,256]{2,1,0:T(8,128)(2,1)S(1)}, bf16[8,64,256]{2,1,0:T(8,128)(2,1)S(1)}, u32[]{:S(2)}, u32[]{:S(2)}) %collective-permute-start.2) | collective-permute-done | bytes 262176 | tf_op jit(solution)/shard_map/ppermute | solution.py:31
  32.5 1.5 %shard_map.77 = f32[1024,128]{1,0:T(8,128)} custom-call(bf16[256,1024]{1,0:T(8,128)(2,1)S(1)} %get-tuple-element.16.member_ref.refs_1_, bf16[8,64,256]{2,1,0:T(8,128)(2,1)S(1)} %collective-permute-done.2.adjoint_ref, f32[1024,128]{1,0:T(8,128)S(1)} %get-tuple-element.24.gain_ref, bf16[512,128]{1,0:T(8,128)(2,1)S(1)} %get-tuple-element.25.basis_ref, ...), custom_call_target="tpu_custom_call" | custom-call | flops 402653184 | bytes 524288 | tf_op jit(solution)/shard_map/pallas_call | solution.py:295
  (3 shorter events, 0.1 us)
Async XLA Ops:
  0.0 1.8 %collective-permute-start = (bf16[4,128,256]{2,1,0:T(8,128)(2,1)}, bf16[4,128,256]{2,1,0:T(8,128)(2,1)S(1)}, u32[]{:S(2)}, u32[]{:S(2)}) collective-permute-start(bf16[4,128,256]{2,1,0:T(8,128)(2,1)} %refs_0_.1), channel_id=1, source_target_pairs={{0,1},{1,0},{2,3},{3,2},{4,5},{5,4},{6,7},{7,6},{8,9},{9,8},{10,11... | collective-permute-start | bytes 786440 | tf_op jit(solution)/shard_map/ppermute | solution.py:31
  0.5 1.4 %collective-permute-start.1 = (f32[4,16]{1,0:T(4,128)}, f32[4,16]{1,0:T(4,128)S(1)}, u32[]{:S(2)}, u32[]{:S(2)}) collective-permute-start(f32[4,16]{1,0:T(4,128)} %refs_3_.1), channel_id=1, source_target_pairs={{0,1},{1,0},{2,3},{3,2},{4,5},{5,4},{6,7},{7,6},{8,9},{9,8},{10,11... | collective-permute-start | bytes 776 | tf_op jit(solution)/shard_map/ppermute | solution.py:31
  31.0 1.5 %collective-permute-start.2 = (bf16[8,64,256]{2,1,0:T(8,128)(2,1)S(1)}, bf16[8,64,256]{2,1,0:T(8,128)(2,1)S(1)}, u32[]{:S(2)}, u32[]{:S(2)}) collective-permute-start(bf16[8,64,256]{2,1,0:T(8,128)(2,1)S(1)} %all_to_all.11.refs_2_), channel_id=1, source_target_pairs={{0,1},{1,0},{2,3},{3,2},{4,5},{5,4},{6,7},{7,6},{8,9},{9,8},{10,11... | collective-permute-start | bytes 786440 | tf_op jit(solution)/shard_map/ppermute | solution.py:31

commit v5 on v1

v5 whole, which is shorter than its diff:
```python
import functools
import math

import jax
import jax.numpy as jnp
from jax import lax
from jax.experimental import pallas as pl
from jax.experimental.pallas import tpu as pltpu
from jax.sharding import PartitionSpec as P

LAG_MAX = 2
ROWS = 512
CUTS = (4,)
ORDER = (0, 2, 1, 3, 7, 5, 4, 6)
NT = (((1,), (1,)), ((), ()))
TN = (((0,), (0,)), ((), ()))
TT = (((0,), (1,)), ((), ()))
PARAMS = pltpu.CompilerParams(vmem_limit_bytes=40 * 1024 * 1024)
SCALAR = pl.BlockSpec(memory_space=pltpu.SMEM)
LOCAL = pl.BlockSpec(memory_space=pltpu.VMEM)


def in_hbm(*arrays):
    return [pltpu.with_memory_space_constraint(array, pltpu.HBM) for array in arrays]


def kept(array):
    return pltpu.VMEM(array.shape, array.dtype)


def rounds_of(peers, owners):
    base = ORDER if peers % len(ORDER) == 0 else range(peers)
    offsets = [first + offset for first in range(0, peers, len(base)) for offset in base]
    assert peers % owners == 0
    return [tuple(offsets[at : at + owners]) for at in range(0, peers, owners)]


def target_of(index, offset, peers):
    return index ^ offset if peers & (peers - 1) == 0 else lax.rem(index + offset, peers)


def source_of(index, offset, peers):
    return index ^ offset if peers & (peers - 1) == 0 else lax.rem(index + (peers - offset), peers)


def offset_at(core, offsets):
    found = jnp.int32(offsets[0])
    for other, offset in enumerate(offsets):
        found = jnp.where(core == other, jnp.int32(offset), found)
    return found


def exchanged(array, offsets, peers):
    owners = len(offsets)
    pairs = [
        (trade * owners + core, int(target_of(trade, offsets[core], peers)) * owners + core)
        for trade in range(peers)
        for core in range(owners)
    ]
    return lax.ppermute(array, ("trades", "dates"), pairs)


def shifted(array, axis, step):
    peers = lax.axis_size(axis)
    return lax.ppermute(array, axis, [(i, (i + step) % peers) for i in range(peers)])


def gain_of_trades(gain, types):
    rows = jnp.zeros((gain.shape[0], types.shape[1]), jnp.float32)
    for which in range(gain.shape[1]):
        rows = jnp.where(types == which, gain[:, which : which + 1], rows)
    return rows


def load_kernel(*refs):
    given, (member_ref, gain_rows_ref, *copies), (set_ref, arrived) = refs[:7], refs[7:-2], refs[-2:]
    set_count, trades = member_ref.shape
    type_ref, gain_ref = copies[2:4]
    moves = [
        pltpu.make_async_copy(source, target, arrived.at[at])
        for at, (source, target) in enumerate(zip(given, copies + [set_ref], strict=True))
    ]
    basis_move, coef_move, type_move, gain_move, lags_move, limits_move, set_move = moves
    for move in (set_move, type_move, gain_move, basis_move, coef_move, lags_move, limits_move):
        move.start()
    set_move.wait()
    member = lax.broadcasted_iota(jnp.int32, (set_count, trades), 0) == set_ref[...]
    member_ref[...] = member.astype(jnp.float32).astype(jnp.bfloat16)
    type_move.wait()
    gain_move.wait()
    gain_rows_ref[...] = gain_of_trades(gain_ref[...], type_ref[...])
    basis_move.wait()
    coef_move.wait()
    lags_move.wait()
    limits_move.wait()


def load(basis, coef, sets, types, gain, lags, limits):
    trades = coef.shape[0]
    return pl.pallas_call(
        load_kernel,
        in_specs=[pl.BlockSpec(memory_space=pl.ANY)] * 7,
        out_specs=[LOCAL] * 8,
        out_shape=[
            pltpu.VMEM((limits.shape[1], trades), jnp.bfloat16),
            pltpu.VMEM((gain.shape[0], trades), jnp.float32),
        ]
        + [kept(array) for array in (basis, coef, types, gain, lags, limits)],
        scratch_shapes=[pltpu.VMEM(sets.shape, sets.dtype), pltpu.SemaphoreType.DMA((7,))],
        compiler_params=PARAMS,
        cost_estimate=pl.CostEstimate(flops=coef.size * 512, bytes_accessed=coef.size * 2, transcendentals=0),
    )(*in_hbm(basis, coef, types, gain, lags, limits, sets))


def net_kernel(rounds, me_ref, trade_ref, coef_ref, type_ref, member_ref, lags_ref, gain_rows_ref, *refs):
    owners = len(rounds[0])
    peers = owners * len(rounds)
    bases, gains, outs = refs[:owners], refs[owners : 2 * owners - 1], refs[2 * owners - 1 :]
    me, trade = me_ref[0], trade_ref[0]
    coef, member, lags = coef_ref[...], member_ref[...], lags_ref[...]
    local_dates, paths, depth = bases[0].shape
    dates = owners * local_dates
    block_paths = paths // peers
    trades, set_count = coef.shape[0], member.shape[0]
    gain = [gain_rows_ref[...]] + [gain_of_trades(ref[...], type_ref[...]) for ref in gains]
    gain = jnp.concatenate(gain, axis=0)
    masks = [(lags == value).astype(jnp.float32) for value in range(1, LAG_MAX + 1)]
    holder = [lax.rem(me + (owners - place), owners) for place in range(owners)]
    earlier = [(owner > 0).astype(jnp.float32) for owner in holder]
    together = max(1, ROWS // (dates * block_paths))
    for first in range(0, len(rounds), together):
        chunk = rounds[first : first + together]
        rows = []
        for offsets in chunk:
            target = target_of(trade, offset_at(me, offsets), peers)
            at = pl.ds(pl.multiple_of(target * block_paths, block_paths), block_paths)
            rows += [ref[:, at, :].reshape(local_dates * block_paths, depth) for ref in bases]
        rows = jnp.concatenate(rows, axis=0)
        raw = lax.dot_general(rows, coef, NT, preferred_element_type=jnp.float32)
        prices = raw.reshape(len(chunk), dates, block_paths, trades) * gain[None, :, None, :]
        prices = prices.astype(jnp.bfloat16).reshape(rows.shape[0], trades)
        netted = lax.dot_general(prices, member, NT, preferred_element_type=jnp.float32)
        netted = netted.reshape(len(chunk), dates, block_paths, set_count)
        for at, out_ref in enumerate(outs[first : first + together]):
            for date in range(dates):
                place, local = divmod(date, local_dates)
                value = netted[at, date]
                for lag, mask in enumerate(masks, 1):
                    if local >= lag:
                        value = value - mask * netted[at, date - lag]
                    else:
                        before = ((place + 1) % owners + 1) * local_dates + local - lag
                        value = value - (mask * earlier[place]) * netted[at, before]
                row = (holder[place] * local_dates + local) * block_paths
                out_ref[pl.ds(pl.multiple_of(row, block_paths), block_paths)] = value


def net(rounds, me, trade, coef, types, member, lags, gain_rows, bases, later_gains):
    owners = len(bases)
    local_dates, paths, _ = bases[0].shape
    rows = local_dates * paths // len(rounds)
    return pl.pallas_call(
        functools.partial(net_kernel, rounds),
        in_specs=[SCALAR] * 2 + [LOCAL] * (4 + 2 * owners),
        out_specs=[LOCAL] * len(rounds),
        out_shape=[pltpu.VMEM((rows, member.shape[0]), jnp.float32)] * len(rounds),
        compiler_params=PARAMS,
    )(me, trade, coef, types, member, lags, gain_rows, *bases, *later_gains)


def adjoint_kernel(scale, block_paths, lags_ref, limits_ref, *refs):
    excess = refs[0][...]
    for ref in refs[1:-1]:
        excess = excess + ref[...]
    rows = excess.shape[0]
    masks = [(lags_ref[...] == value).astype(jnp.float32) for value in range(1, LAG_MAX + 1)]
    direct = jnp.maximum(2.0 * excess - limits_ref[...], 0.0) * scale
    direct = [direct[first : first + block_paths] for first in range(0, rows, block_paths)]
    adjoints = []
    for date, adjoint in enumerate(direct):
        for value, mask in enumerate(masks, 1):
            if date + value < len(direct):
                adjoint = adjoint - mask * direct[date + value]
        adjoints.append(adjoint)
    refs[-1][...] = jnp.concatenate(adjoints, axis=0).astype(jnp.bfloat16)


def adjoint_of(sums, lags, limits, scale, block_paths):
    return pl.pallas_call(
        functools.partial(adjoint_kernel, scale, block_paths),
        in_specs=[LOCAL] * (2 + len(sums)),
        out_specs=LOCAL,
        out_shape=pltpu.VMEM(sums[0].shape, jnp.bfloat16),
        compiler_params=PARAMS,
    )(lags, limits, *sums)


def ready_kernel(rounds, me_ref, trade_ref, type_ref, *refs):
    owners = len(rounds[0])
    peers = owners * len(rounds)
    gain_refs, basis_refs = refs[:owners], refs[owners : 2 * owners]
    gain_ref, *out_refs = refs[2 * owners :]
    local_dates, paths, _ = basis_refs[0].shape
    own_depth = out_refs[0].shape[1]
    block_paths = paths // peers
    local_rows = local_dates * block_paths
    dates = owners * local_dates
    me, trade = me_ref[0], trade_ref[0]
    columns = pl.ds(pl.multiple_of(me * own_depth, own_depth), own_depth)
    for step, out_ref in enumerate(out_refs):
        core = lax.rem(me + (owners - step), owners)
        for at, offsets in enumerate(rounds):
            source = source_of(trade, offset_at(core, offsets), peers)
            span = pl.ds(pl.multiple_of(source * block_paths, block_paths), block_paths)
            for place, ref in enumerate(basis_refs):
                row = at * owners * local_rows + lax.rem(me + (owners - place), owners) * local_rows
                block = ref[:, span, columns].reshape(local_rows, own_depth)
                out_ref[pl.ds(pl.multiple_of(row, local_rows), local_rows)] = block
    rest = jnp.concatenate([gain_of_trades(ref[...], type_ref[...]) for ref in gain_refs], axis=0)
    pieces = []
    for _ in range(3):
        piece = rest.astype(jnp.bfloat16).astype(jnp.float32)
        pieces.append(piece)
        rest = rest - piece
    pieces = jnp.concatenate(pieces, axis=0).astype(jnp.bfloat16)
    shape = (3 * dates, gain_ref.shape[1])
    want = lax.rem(lax.div(lax.broadcasted_iota(jnp.int32, shape, 1), block_paths), dates)
    have = lax.rem(lax.broadcasted_iota(jnp.int32, shape, 0), dates)
    place, local = lax.div(have, local_dates), lax.rem(have, local_dates)
    have = lax.rem(me + owners - place, owners) * local_dates + local
    expand = (want == have).astype(jnp.float32).astype(jnp.bfloat16)
    gain_ref[...] = lax.dot_general(pieces, expand, TN, preferred_element_type=jnp.float32)


def ready(rounds, me, trade, types, gains, bases):
    owners = len(bases)
    local_dates, paths, depth = bases[0].shape
    block_rows = owners * local_dates * paths // (owners * len(rounds))
    rows = block_rows * len(rounds)
    return pl.pallas_call(
        functools.partial(ready_kernel, rounds),
        in_specs=[SCALAR] * 2 + [LOCAL] * (1 + 2 * owners),
        out_specs=[LOCAL] * (1 + owners),
        out_shape=[pltpu.VMEM((types.shape[1], math.lcm(block_rows, 128)), jnp.float32)]
        + [pltpu.VMEM((rows, depth // owners), jnp.bfloat16)] * owners,
        compiler_params=PARAMS,
        cost_estimate=pl.CostEstimate(flops=types.shape[1] * 256 * 1024, bytes_accessed=0, transcendentals=0),
    )(me, trade, types, *gains, *bases)


def grad_kernel(first, carry, member_ref, gain_ref, basis_ref, *refs):
    adjoint_refs, out_ref = refs[carry:-1], refs[-1]
    rows, set_count = adjoint_refs[0].shape
    gain = gain_ref[...]
    period = gain.shape[1]
    member = member_ref[...]
    total = refs[0][...] if carry else None
    together = max(1, ROWS // rows)
    for at in range(0, len(adjoint_refs), together):
        adjoint = jnp.concatenate([ref[...] for ref in adjoint_refs[at : at + together]], axis=0)
        count = adjoint.shape[0]
        spread = lax.dot_general(member, adjoint, TT, preferred_element_type=jnp.float32)
        scaled = [
            (spread[:, left : left + period] * gain).astype(jnp.bfloat16) for left in range(0, count, period)
        ]
        basis = basis_ref[pl.ds((first + at) * rows, count)]
        part = jnp.dot(jnp.concatenate(scaled, axis=1), basis, preferred_element_type=jnp.float32)
        total = part if total is None else total + part
    out_ref[...] = total


def add_grad(total, member, gain, basis, adjoints, first, last):
    carry = int(total is not None)
    trades, own_depth = member.shape[1], basis.shape[1]
    shape = (trades, own_depth)
    count = len(adjoints) * adjoints[0].shape[0]
    return pl.pallas_call(
        functools.partial(grad_kernel, first, carry),
        in_specs=[LOCAL] * (3 + carry + len(adjoints)),
        out_specs=LOCAL,
        out_shape=jax.ShapeDtypeStruct(shape, jnp.float32) if last else pltpu.VMEM(shape, jnp.float32),
        compiler_params=PARAMS,
        cost_estimate=pl.CostEstimate(
            flops=2 * trades * count * (member.shape[0] + own_depth),
            bytes_accessed=4 * trades * own_depth,
            transcendentals=0,
        ),
    )(member, gain, basis, *([total] if carry else []), *adjoints)


def on_device(basis_values, coefficients, set_map, trade_type, type_gain, set_lags, thresholds):
    local_dates, path_count, _ = basis_values.shape
    trades = coefficients.shape[0]
    set_count = thresholds.shape[0]
    peers = lax.axis_size("trades")
    owners = lax.axis_size("dates")
    rounds = rounds_of(peers, owners)
    block_paths = path_count // peers
    scale = 2.0 / math.sqrt(local_dates * owners * path_count)
    me = lax.axis_index("dates").astype(jnp.int32).reshape(1)
    trade = lax.axis_index("trades").astype(jnp.int32).reshape(1)

    bases = [shifted(basis_values, "dates", step) for step in range(1, owners)]
    gains = [shifted(type_gain, "dates", step) for step in range(1, owners)]
    member, gain_rows, basis, coef, types, gain, lags, limits = load(
        basis_values,
        coefficients,
        set_map.reshape(1, trades),
        trade_type.reshape(1, trades),
        type_gain,
        set_lags.reshape(1, set_count),
        thresholds.reshape(1, set_count),
    )
    bases, gains = [basis] + bases, [gain] + gains
    partials = net(rounds, me, trade, coef, types, member, lags, gain_rows, bases, gains[1:])
    arrived = [
        exchanged((partial * 0.5).astype(jnp.float16), offsets, peers)
        for partial, offsets in zip(partials, rounds, strict=True)
    ]
    trade_gain, *basis_rows = ready(rounds, me, trade, types, gains, bases)
    excess = functools.reduce(jnp.add, [part.astype(jnp.float32) for part in arrived])
    excess, trade_gain, *basis_rows = lax.optimization_barrier((excess, trade_gain, *basis_rows))
    sums = [excess] + [shifted(excess, "dates", step) for step in range(1, owners)]
    adjoint = adjoint_of(sums, lags, limits, scale, block_paths)
    adjoints = lax.optimization_barrier([exchanged(adjoint, offsets, peers) for offsets in rounds])

    total = None
    firsts = [0, *(len(rounds) * cut // CUTS[-1] for cut in CUTS[:-1])]
    for first, end in zip(firsts, firsts[1:] + [len(rounds)], strict=True):
        parts = adjoints[first:end]
        if total is not None:
            total, *parts = lax.optimization_barrier((total, *parts))
        swaps = [jnp.stack(parts) if len(parts) > 1 else parts[0]]
        swaps = [shifted(swaps[0], "dates", step) for step in range(1, owners)]
        for step in range(owners):
            if step:
                parts = list(swaps[step - 1]) if len(parts) > 1 else [swaps[step - 1]]
            last = step == owners - 1 and end == len(rounds)
            total = add_grad(total, member, trade_gain, basis_rows[step], parts, first, last)
    return total


def solution(mesh):
    return jax.shard_map(
        on_device,
        mesh=mesh,
        in_specs=(
            P("dates", "groups", None),
            P("trades", None),
            P("trades"),
            P("trades"),
            P("dates", None),
            P(),
            P(),
        ),
        out_specs=P(("groups", "trades"), "dates"),
        check_vma=False,
    )
```

time: 40.4 us -> 29.1 us (0.72)
  waiting for transfers between devices: 21.9 us -> 9.9 us
  matrix products: 5.31 us -> 0 us
  Pallas kernels: 0 us -> 4.96 us
  starting transfers between devices: 11.1 us -> 13.8 us
  local copies, waits for them, and re-layouts: 1.51 us -> 0.02 us
    all_to_all x2 -> x0, waiting for transfers between devices: 20 us -> none  [the longest x1 10 us: on_device(): lax.all_to_all(partial, ('trades', 'dates'), split_axis=0, concat_axis=0,...]
    ppermute x1 -> x12, starting transfers between devices: 0.07 us -> 13.8 us  [the longest x8 13 us: exchanged(): return lax.ppermute(array, ('trades', 'dates'), pairs)]
    all_to_all x2 -> x0, starting transfers between devices: 11 us -> none  [the longest x1 7.49 us: on_device(): lax.all_to_all(partial, ('trades', 'dates'), split_axis=0, concat_axis=0,...]
    ppermute x1 -> x12, waiting for transfers between devices: 1.89 us -> 9.9 us  [the longest x8 8 us: exchanged(): return lax.ppermute(array, ('trades', 'dates'), pairs)]
    dot_general x5 -> x0, matrix products: 5.31 us -> none  [the longest x1 1.81 us: on_device(): partial = jnp.dot(prices, member, preferred_element_type=jnp.float32)]
    pallas_call x0 -> x6, Pallas kernels: none -> 4.96 us  [the longest x2 2.38 us: add_grad(): pl.pallas_call(functools.partial(grad_kernel, first, carry), in_specs=[LO...]
    convert_element_type x1 -> x0, local copies, waits for them, and re-layouts: 0.75 us -> none  [on_device(): partial = partial.astype(jnp.float16)]
    broadcast_in_dim x1 -> x0, local copies, waits for them, and re-layouts: 0.73 us -> none  [on_device(): adjoint = jnp.broadcast_to(adjoint, (trade_peers,) + adjoint.shape[1:])]
  transfers between devices with their start and end apart: 3 -> 12, of which waited for: 3 -> 7; matrix products, arithmetic and copies ran while one was open for 0% -> 0% of each run, Pallas kernels for 0% -> 9%
where the time goes in v5:
time: 29.1 us; the launch traced here: 29 us
  starting transfers between devices  13.8 us (47%)
  waiting for transfers between devices  9.9 us (34%)
  Pallas kernels  4.96 us (17%)
    ppermute x8, starting transfers between devices, exchanged(): return lax.ppermute(array, ('trades', 'dates'), pairs)  13 us
    ppermute x8, waiting for transfers between devices, exchanged(): return lax.ppermute(array, ('trades', 'dates'), pairs)  8 us
    pallas_call x2, Pallas kernels, add_grad(): pl.pallas_call(functools.partial(grad_kernel, first, carry), in_specs=[LO...  2.38 us
    ppermute x4, waiting for transfers between devices, shifted(): lax.ppermute(array, axis, [(i, (i + step) % peers) for i in range(peers)])  1.9 us
    pallas_call x1, Pallas kernels, load(): pl.pallas_call(load_kernel, in_specs=[pl.BlockSpec(memory_space=pl.ANY)]...  1.23 us
    pallas_call x1, Pallas kernels, net(): pl.pallas_call(functools.partial(net_kernel, rounds), in_specs=[SCALAR] *...  0.86 us
    ppermute x4, starting transfers between devices, shifted(): lax.ppermute(array, axis, [(i, (i + step) % peers) for i in range(peers)])  0.86 us
  transfers between devices with their start and end apart: 12, of which 7 were waited for; matrix products, arithmetic and copies ran while one was open for 0% of the time, Pallas kernels for 9%

profile of v5, /device:TPU:0, one launch (start us, length us, event | category | flops | bytes accessed | tf_op | source)
XLA Modules:
  0.0 29.0 jit_solution(5586267366931207411)
XLA Ops:
  0.0 0.5 %collective-permute-start = (bf16[4,128,256]{2,1,0:T(8,128)(2,1)}, bf16[4,128,256]{2,1,0:T(8,128)(2,1)S(1)}, u32[]{:S(2)}, u32[]{:S(2)}) collective-permute-start(bf16[4,128,256]{2,1,0:T(8,128)(2,1)} %refs_0_.1), channel_id=1, source_target_pairs={{0,1},{1,0},{2,3},{3,2},{4,5},{5,4},{6,7},{7,6},{8,9},{9,8},{10,11... | collective-permute-start | bytes 786440 | tf_op jit(solution)/shard_map/ppermute | solution.py:65
  0.5 0.1 collective-permute-start.1
  0.5 1.2 %shard_map.73 = (bf16[256,1024]{1,0:T(8,128)(2,1)S(1)}, f32[4,1024]{1,0:T(4,128)S(1)}, bf16[4,128,256]{2,1,0:T(8,128)(2,1)S(1)}, bf16[1024,256]{1,0:T(8,128)(2,1...) custom-call(bf16[4,128,256]{2,1,0:T(8,128)(2,1)} %refs_0_.1, ...), custom_call_target="tpu_custom_call" | custom-call | flops 134217728 | bytes 524288 | tf_op jit(solution)/shard_map/pallas_call | solution.py:100
  1.8 0.1 collective-permute-done.1.refs_2_.refs_1_
  1.8 0.0 collective-permute-done.refs_1_.refs_3_
  1.8 0.9 %shard_map.74 = (f32[128,256]{1,0:T(8,128)S(1)}, f32[128,256]{1,0:T(8,128)S(1)}, f32[128,256]{1,0:T(8,128)S(1)}, f32[128,256]{1,0:T(8,128)S(1)}) custom-call(s32[1]{0:T(128)} %bitcast.4.me_ref, s32[1]{0:T(128)} %bitcast.5.trade_ref, bf16[1024,256]{1,0:T(8,128)(2,1)S(1)} %get-tuple-element.29.coef_ref, s32[1,1024]{1,0:T(1,128)S(1)} %get-tuple-element.30.type_ref, ...), custom_call_target="tpu_custom_call" | custom-call | tf_op jit(solution)/shard_map/pallas_call | solution.py:162
  2.8 4.0 %collective-permute-start.5 = (f16[128,256]{1,0:T(8,128)(2,1)S(1)}, f16[128,256]{1,0:T(8,128)(2,1)S(1)}, u32[]{:S(2)}, u32[]{:S(2)}) collective-permute-start(f16[128,256]{1,0:T(8,128)(2,1)S(1)} %multiply_convert_fusion), channel_id=1, source_target_pairs={{0,8},{1,13},{2,10},{3,15},{4,12},{5,9},{6,14},{7,11},{8,0},{9,5},... | collective-permute-start | bytes 196616 | tf_op jit(solution)/shard_map/ppermute | solution.py:60
  6.8 2.3 %collective-permute-start.4 = (f16[128,256]{1,0:T(8,128)(2,1)S(1)}, f16[128,256]{1,0:T(8,128)(2,1)S(1)}, u32[]{:S(2)}, u32[]{:S(2)}) collective-permute-start(f16[128,256]{1,0:T(8,128)(2,1)S(1)} %multiply_convert_fusion.1), channel_id=1, source_target_pairs={{0,14},{1,11},{2,12},{3,9},{4,10},{5,15},{6,8},{7,13},{8,6},{9,3},... | collective-permute-start | bytes 196616 | tf_op jit(solution)/shard_map/ppermute | solution.py:60
  9.1 0.5 %collective-permute-start.3 = (f16[128,256]{1,0:T(8,128)(2,1)S(1)}, f16[128,256]{1,0:T(8,128)(2,1)S(1)}, u32[]{:S(2)}, u32[]{:S(2)}) collective-permute-start(f16[128,256]{1,0:T(8,128)(2,1)S(1)} %multiply_convert_fusion.2), channel_id=1, source_target_pairs={{0,2},{1,7},{2,0},{3,5},{4,6},{5,3},{6,4},{7,1},{8,10},{9,15},{10,... | collective-permute-start | bytes 196616 | tf_op jit(solution)/shard_map/ppermute | solution.py:60
  9.7 0.7 %collective-permute-start.2 = (f16[128,256]{1,0:T(8,128)(2,1)S(1)}, f16[128,256]{1,0:T(8,128)(2,1)S(1)}, u32[]{:S(2)}, u32[]{:S(2)}) collective-permute-start(f16[128,256]{1,0:T(8,128)(2,1)S(1)} %multiply_convert_fusion.3), channel_id=1, source_target_pairs={{0,0},{1,5},{2,2},{3,7},{4,4},{5,1},{6,6},{7,3},{8,8},{9,13},{10,1... | collective-permute-start | bytes 196616 | tf_op jit(solution)/shard_map/ppermute | solution.py:60
  10.3 0.4 %shard_map.75 = (f32[1024,128]{1,0:T(8,128)S(1)}, bf16[512,128]{1,0:T(8,128)(2,1)S(1)}, bf16[512,128]{1,0:T(8,128)(2,1)S(1)}) custom-call(s32[1]{0:T(128)} %bitcast.4.me_ref, s32[1]{0:T(128)} %bitcast.5.trade_ref, s32[1,1024]{1,0:T(1,128)S(1)} %get-tuple-element.30.type_ref, f32[4,16]{1,0:T(4,128)S(1)} %get-tuple-element.38.refs_0_, ...), custom_call_target="tpu_custom_call" | custom-call | flops 268435456 | tf_op jit(solution)/shard_map/pallas_call | solution.py:240
  10.8 0.0 collective-permute-done.5
  10.8 3.2 %collective-permute-done.4 = f16[128,256]{1,0:T(8,128)(2,1)S(1)} collective-permute-done((f16[128,256]{1,0:T(8,128)(2,1)S(1)}, f16[128,256]{1,0:T(8,128)(2,1)S(1)}, u32[]{:S(2)}, u32[]{:S(2)}) %collective-permute-start.4) | collective-permute-done | bytes 65568 | tf_op jit(solution)/shard_map/ppermute | solution.py:60
  14.0 0.5 %collective-permute-done.3 = f16[128,256]{1,0:T(8,128)(2,1)S(1)} collective-permute-done((f16[128,256]{1,0:T(8,128)(2,1)S(1)}, f16[128,256]{1,0:T(8,128)(2,1)S(1)}, u32[]{:S(2)}, u32[]{:S(2)}) %collective-permute-start.3) | collective-permute-done | bytes 65568 | tf_op jit(solution)/shard_map/ppermute | solution.py:60
  14.5 0.0 collective-permute-done.2
  14.5 0.2 collective-permute-start.6
  14.7 1.2 %collective-permute-done.6.refs_1_ = f32[128,256]{1,0:T(8,128)S(1)} collective-permute-done((f32[128,256]{1,0:T(8,128)S(1)}, f32[128,256]{1,0:T(8,128)S(1)}, u32[]{:S(2)}, u32[]{:S(2)}) %collective-permute-start.6) | collective-permute-done | bytes 131104 | tf_op jit(solution)/shard_map/ppermute | solution.py:65
  16.0 2.5 %collective-permute-start.10 = (bf16[128,256]{1,0:T(8,128)(2,1)S(1)}, bf16[128,256]{1,0:T(8,128)(2,1)S(1)}, u32[]{:S(2)}, u32[]{:S(2)}) collective-permute-start(bf16[128,256]{1,0:T(8,128)(2,1)S(1)} %shard_map.76), channel_id=1, source_target_pairs={{0,8},{1,13},{2,10},{3,15},{4,12},{5,9},{6,14},{7,11},{8,0},{9,5},... | collective-permute-start | bytes 196616 | tf_op jit(solution)/shard_map/ppermute | solution.py:60
  18.5 1.2 %collective-permute-start.9 = (bf16[128,256]{1,0:T(8,128)(2,1)S(1)}, bf16[128,256]{1,0:T(8,128)(2,1)S(1)}, u32[]{:S(2)}, u32[]{:S(2)}) collective-permute-start(bf16[128,256]{1,0:T(8,128)(2,1)S(1)} %shard_map.76), channel_id=1, source_target_pairs={{0,14},{1,11},{2,12},{3,9},{4,10},{5,15},{6,8},{7,13},{8,6},{9,3},... | collective-permute-start | bytes 196616 | tf_op jit(solution)/shard_map/ppermute | solution.py:60
  19.6 1.2 %collective-permute-start.8 = (bf16[128,256]{1,0:T(8,128)(2,1)S(1)}, bf16[128,256]{1,0:T(8,128)(2,1)S(1)}, u32[]{:S(2)}, u32[]{:S(2)}) collective-permute-start(bf16[128,256]{1,0:T(8,128)(2,1)S(1)} %shard_map.76), channel_id=1, source_target_pairs={{0,2},{1,7},{2,0},{3,5},{4,6},{5,3},{6,4},{7,1},{8,10},{9,15},{10,... | collective-permute-start | bytes 196616 | tf_op jit(solution)/shard_map/ppermute | solution.py:60
  20.8 0.7 %collective-permute-start.7 = (bf16[128,256]{1,0:T(8,128)(2,1)S(1)}, bf16[128,256]{1,0:T(8,128)(2,1)S(1)}, u32[]{:S(2)}, u32[]{:S(2)}) collective-permute-start(bf16[128,256]{1,0:T(8,128)(2,1)S(1)} %shard_map.76), channel_id=1, source_target_pairs={{0,0},{1,5},{2,2},{3,7},{4,4},{5,1},{6,6},{7,3},{8,8},{9,13},{10,1... | collective-permute-start | bytes 196616 | tf_op jit(solution)/shard_map/ppermute | solution.py:60
  21.5 2.1 %collective-permute-done.10.refs_3_ = bf16[128,256]{1,0:T(8,128)(2,1)S(1)} collective-permute-done((bf16[128,256]{1,0:T(8,128)(2,1)S(1)}, bf16[128,256]{1,0:T(8,128)(2,1)S(1)}, u32[]{:S(2)}, u32[]{:S(2)}) %collective-permute-start.10) | collective-permute-done | bytes 65568 | tf_op jit(solution)/shard_map/ppermute | solution.py:60
  23.6 2.2 %collective-permute-done.9.refs_2_ = bf16[128,256]{1,0:T(8,128)(2,1)S(1)} collective-permute-done((bf16[128,256]{1,0:T(8,128)(2,1)S(1)}, bf16[128,256]{1,0:T(8,128)(2,1)S(1)}, u32[]{:S(2)}, u32[]{:S(2)}) %collective-permute-start.9) | collective-permute-done | bytes 65568 | tf_op jit(solution)/shard_map/ppermute | solution.py:60
  25.7 0.0 collective-permute-done.8.refs_1_
  25.7 0.0 collective-permute-done.7.refs_0_
  25.8 0.2 collective-permute-start.11
  26.0 0.8 %shard_map.77.refs_0_ = f32[1024,128]{1,0:T(8,128)S(1)} custom-call(bf16[256,1024]{1,0:T(8,128)(2,1)S(1)} %get-tuple-element.28.member_ref, f32[1024,128]{1,0:T(8,128)S(1)} %get-tuple-element.42.gain_ref, bf16[512,128]{1,0:T(8,128)(2,1)S(1)} %get-tuple-element.44.basis_ref, bf16[128,256]{1,0:T(8,128)(2,1)S(1)} %collective-permute-done.7.refs_0_, ...), custom_call_target="tpu_custom_call" | custom-call | flops 402653184 | bytes 524288 | tf_op jit(solution)/shard_map/pallas_call | solution.py:277
  26.8 0.6 %collective-permute-done.11 = bf16[4,128,256]{2,1,0:T(8,128)(2,1)S(1)} collective-permute-done((bf16[4,128,256]{2,1,0:T(8,128)(2,1)S(1)}, bf16[4,128,256]{2,1,0:T(8,128)(2,1)S(1)}, u32[]{:S(2)}, u32[]{:S(2)}) %collective-permute-start.11) | collective-permute-done | bytes 262176 | tf_op jit(solution)/shard_map/ppermute | solution.py:65
  27.4 1.5 %shard_map.78 = f32[1024,128]{1,0:T(8,128)} custom-call(bf16[256,1024]{1,0:T(8,128)(2,1)S(1)} %get-tuple-element.28.member_ref, f32[1024,128]{1,0:T(8,128)S(1)} %get-tuple-element.42.gain_ref, bf16[512,128]{1,0:T(8,128)(2,1)S(1)} %get-tuple-element.43.basis_ref, f32[1024,128]{1,0:T(8,128)S(1)} %shard_map.77.refs_0_, ...), custom_call_target="tpu_custom_call" | custom-call | flops 402653184 | bytes 524288 | tf_op jit(solution)/shard_map/pallas_call | solution.py:277
  (8 shorter events, 0.2 us)
Async XLA Ops:
  0.0 1.8 %collective-permute-start = (bf16[4,128,256]{2,1,0:T(8,128)(2,1)}, bf16[4,128,256]{2,1,0:T(8,128)(2,1)S(1)}, u32[]{:S(2)}, u32[]{:S(2)}) collective-permute-start(bf16[4,128,256]{2,1,0:T(8,128)(2,1)} %refs_0_.1), channel_id=1, source_target_pairs={{0,1},{1,0},{2,3},{3,2},{4,5},{5,4},{6,7},{7,6},{8,9},{9,8},{10,11... | collective-permute-start | bytes 786440 | tf_op jit(solution)/shard_map/ppermute | solution.py:65
  0.5 1.4 %collective-permute-start.1 = (f32[4,16]{1,0:T(4,128)}, f32[4,16]{1,0:T(4,128)S(1)}, u32[]{:S(2)}, u32[]{:S(2)}) collective-permute-start(f32[4,16]{1,0:T(4,128)} %refs_3_.1), channel_id=1, source_target_pairs={{0,1},{1,0},{2,3},{3,2},{4,5},{5,4},{6,7},{7,6},{8,9},{9,8},{10,11... | collective-permute-start | bytes 776 | tf_op jit(solution)/shard_map/ppermute | solution.py:65
  2.8 8.0 %collective-permute-start.5 = (f16[128,256]{1,0:T(8,128)(2,1)S(1)}, f16[128,256]{1,0:T(8,128)(2,1)S(1)}, u32[]{:S(2)}, u32[]{:S(2)}) collective-permute-start(f16[128,256]{1,0:T(8,128)(2,1)S(1)} %multiply_convert_fusion), channel_id=1, source_target_pairs={{0,8},{1,13},{2,10},{3,15},{4,12},{5,9},{6,14},{7,11},{8,0},{9,5},... | collective-permute-start | bytes 196616 | tf_op jit(solution)/shard_map/ppermute | solution.py:60
  6.8 7.1 %collective-permute-start.4 = (f16[128,256]{1,0:T(8,128)(2,1)S(1)}, f16[128,256]{1,0:T(8,128)(2,1)S(1)}, u32[]{:S(2)}, u32[]{:S(2)}) collective-permute-start(f16[128,256]{1,0:T(8,128)(2,1)S(1)} %multiply_convert_fusion.1), channel_id=1, source_target_pairs={{0,14},{1,11},{2,12},{3,9},{4,10},{5,15},{6,8},{7,13},{8,6},{9,3},... | collective-permute-start | bytes 196616 | tf_op jit(solution)/shard_map/ppermute | solution.py:60
  9.1 5.4 %collective-permute-start.3 = (f16[128,256]{1,0:T(8,128)(2,1)S(1)}, f16[128,256]{1,0:T(8,128)(2,1)S(1)}, u32[]{:S(2)}, u32[]{:S(2)}) collective-permute-start(f16[128,256]{1,0:T(8,128)(2,1)S(1)} %multiply_convert_fusion.2), channel_id=1, source_target_pairs={{0,2},{1,7},{2,0},{3,5},{4,6},{5,3},{6,4},{7,1},{8,10},{9,15},{10,... | collective-permute-start | bytes 196616 | tf_op jit(solution)/shard_map/ppermute | solution.py:60
  9.7 4.8 %collective-permute-start.2 = (f16[128,256]{1,0:T(8,128)(2,1)S(1)}, f16[128,256]{1,0:T(8,128)(2,1)S(1)}, u32[]{:S(2)}, u32[]{:S(2)}) collective-permute-start(f16[128,256]{1,0:T(8,128)(2,1)S(1)} %multiply_convert_fusion.3), channel_id=1, source_target_pairs={{0,0},{1,5},{2,2},{3,7},{4,4},{5,1},{6,6},{7,3},{8,8},{9,13},{10,1... | collective-permute-start | bytes 196616 | tf_op jit(solution)/shard_map/ppermute | solution.py:60
  14.5 1.4 %collective-permute-start.6 = (f32[128,256]{1,0:T(8,128)S(1)}, f32[128,256]{1,0:T(8,128)S(1)}, u32[]{:S(2)}, u32[]{:S(2)}) collective-permute-start(f32[128,256]{1,0:T(8,128)S(1)} %convert_add_fusion.refs_0_), channel_id=1, source_target_pairs={{0,1},{1,0},{2,3},{3,2},{4,5},{5,4},{6,7},{7,6},{8,9},{9,8},{10,11... | collective-permute-start | bytes 393224 | tf_op jit(solution)/shard_map/ppermute | solution.py:65
  16.0 7.6 %collective-permute-start.10 = (bf16[128,256]{1,0:T(8,128)(2,1)S(1)}, bf16[128,256]{1,0:T(8,128)(2,1)S(1)}, u32[]{:S(2)}, u32[]{:S(2)}) collective-permute-start(bf16[128,256]{1,0:T(8,128)(2,1)S(1)} %shard_map.76), channel_id=1, source_target_pairs={{0,8},{1,13},{2,10},{3,15},{4,12},{5,9},{6,14},{7,11},{8,0},{9,5},... | collective-permute-start | bytes 196616 | tf_op jit(solution)/shard_map/ppermute | solution.py:60
  18.5 7.3 %collective-permute-start.9 = (bf16[128,256]{1,0:T(8,128)(2,1)S(1)}, bf16[128,256]{1,0:T(8,128)(2,1)S(1)}, u32[]{:S(2)}, u32[]{:S(2)}) collective-permute-start(bf16[128,256]{1,0:T(8,128)(2,1)S(1)} %shard_map.76), channel_id=1, source_target_pairs={{0,14},{1,11},{2,12},{3,9},{4,10},{5,15},{6,8},{7,13},{8,6},{9,3},... | collective-permute-start | bytes 196616 | tf_op jit(solution)/shard_map/ppermute | solution.py:60
  19.6 6.1 %collective-permute-start.8 = (bf16[128,256]{1,0:T(8,128)(2,1)S(1)}, bf16[128,256]{1,0:T(8,128)(2,1)S(1)}, u32[]{:S(2)}, u32[]{:S(2)}) collective-permute-start(bf16[128,256]{1,0:T(8,128)(2,1)S(1)} %shard_map.76), channel_id=1, source_target_pairs={{0,2},{1,7},{2,0},{3,5},{4,6},{5,3},{6,4},{7,1},{8,10},{9,15},{10,... | collective-permute-start | bytes 196616 | tf_op jit(solution)/shard_map/ppermute | solution.py:60
  20.8 4.9 %collective-permute-start.7 = (bf16[128,256]{1,0:T(8,128)(2,1)S(1)}, bf16[128,256]{1,0:T(8,128)(2,1)S(1)}, u32[]{:S(2)}, u32[]{:S(2)}) collective-permute-start(bf16[128,256]{1,0:T(8,128)(2,1)S(1)} %shard_map.76), channel_id=1, source_target_pairs={{0,0},{1,5},{2,2},{3,7},{4,4},{5,1},{6,6},{7,3},{8,8},{9,13},{10,1... | collective-permute-start | bytes 196616 | tf_op jit(solution)/shard_map/ppermute | solution.py:60
  25.8 1.6 %collective-permute-start.11 = (bf16[4,128,256]{2,1,0:T(8,128)(2,1)S(1)}, bf16[4,128,256]{2,1,0:T(8,128)(2,1)S(1)}, u32[]{:S(2)}, u32[]{:S(2)}) collective-permute-start(bf16[4,128,256]{2,1,0:T(8,128)(2,1)S(1)} %pad_maximum_fusion), channel_id=1, source_target_pairs={{0,1},{1,0},{2,3},{3,2},{4,5},{5,4},{6,7},{7,6},{8,9},{9,8},{10,11... | collective-permute-start | bytes 786440 | tf_op jit(solution)/shard_map/ppermute | solution.py:65

commit v6 on v5

--- a/solution.py
+++ b/solution.py
@@ -10,7 +10,7 @@
 
 LAG_MAX = 2
 ROWS = 512
-CUTS = (4,)
+PIECES = 4
 ORDER = (0, 2, 1, 3, 7, 5, 4, 6)
 NT = (((1,), (1,)), ((), ()))
 TN = (((0,), (0,)), ((), ()))
@@ -248,9 +248,11 @@
     )(me, trade, types, *gains, *bases)
 
 
-def grad_kernel(first, carry, member_ref, gain_ref, basis_ref, *refs):
-    adjoint_refs, out_ref = refs[carry:-1], refs[-1]
+def grad_kernel(carry, last, member_ref, gain_ref, basis_ref, *refs):
+    out_ref, *scratch = refs[-3:] if last else refs[-1:]
+    adjoint_refs = refs[carry : -3 if last else -1]
     rows, set_count = adjoint_refs[0].shape
+    trades = member_ref.shape[1]
     gain = gain_ref[...]
     period = gain.shape[1]
     member = member_ref[...]
@@ -263,22 +265,39 @@
         scaled = [
             (spread[:, left : left + period] * gain).astype(jnp.bfloat16) for left in range(0, count, period)
         ]
-        basis = basis_ref[pl.ds((first + at) * rows, count)]
-        part = jnp.dot(jnp.concatenate(scaled, axis=1), basis, preferred_element_type=jnp.float32)
+        scaled = jnp.concatenate(scaled, axis=1)
+        basis = basis_ref[pl.ds(at * rows, count)]
+        if last and at + together >= len(adjoint_refs):
+            sum_ref, written = scratch
+            size = trades // written.shape[0]
+            moves = []
+            for piece in range(written.shape[0]):
+                span = pl.ds(piece * size, size)
+                left, right = piece * size, (piece + 1) * size
+                part = jnp.dot(scaled[left:right], basis, preferred_element_type=jnp.float32)
+                sum_ref[span] = part if total is None else total[left:right] + part
+                moves.append(pltpu.make_async_copy(sum_ref.at[span], out_ref.at[span], written.at[piece]))
+                moves[-1].start()
+            for move in moves:
+                move.wait()
+            return
+        part = jnp.dot(scaled, basis, preferred_element_type=jnp.float32)
         total = part if total is None else total + part
     out_ref[...] = total
 
 
-def add_grad(total, member, gain, basis, adjoints, first, last):
+def add_grad(total, member, gain, basis, adjoints, last):
     carry = int(total is not None)
     trades, own_depth = member.shape[1], basis.shape[1]
     shape = (trades, own_depth)
     count = len(adjoints) * adjoints[0].shape[0]
-    return pl.pallas_call(
-        functools.partial(grad_kernel, first, carry),
+    pieces = math.gcd(trades // 128, PIECES) if trades % 128 == 0 else 1
+    return pl.pallas_call(
+        functools.partial(grad_kernel, carry, last),
         in_specs=[LOCAL] * (3 + carry + len(adjoints)),
-        out_specs=LOCAL,
+        out_specs=pl.BlockSpec(memory_space=pl.ANY) if last else LOCAL,
         out_shape=jax.ShapeDtypeStruct(shape, jnp.float32) if last else pltpu.VMEM(shape, jnp.float32),
+        scratch_shapes=[pltpu.VMEM(shape, jnp.float32), pltpu.SemaphoreType.DMA((pieces,))] if last else [],
         compiler_params=PARAMS,
         cost_estimate=pl.CostEstimate(
             flops=2 * trades * count * (member.shape[0] + own_depth),
@@ -324,19 +343,11 @@
     adjoint = adjoint_of(sums, lags, limits, scale, block_paths)
     adjoints = lax.optimization_barrier([exchanged(adjoint, offsets, peers) for offsets in rounds])
 
+    block = jnp.stack(adjoints)
     total = None
-    firsts = [0, *(len(rounds) * cut // CUTS[-1] for cut in CUTS[:-1])]
-    for first, end in zip(firsts, firsts[1:] + [len(rounds)], strict=True):
-        parts = adjoints[first:end]
-        if total is not None:
-            total, *parts = lax.optimization_barrier((total, *parts))
-        swaps = [jnp.stack(parts) if len(parts) > 1 else parts[0]]
-        swaps = [shifted(swaps[0], "dates", step) for step in range(1, owners)]
-        for step in range(owners):
-            if step:
-                parts = list(swaps[step - 1]) if len(parts) > 1 else [swaps[step - 1]]
-            last = step == owners - 1 and end == len(rounds)
-            total = add_grad(total, member, trade_gain, basis_rows[step], parts, first, last)
+    for step in range(owners):
+        there = list(shifted(block, "dates", step)) if step else adjoints
+        total = add_grad(total, member, trade_gain, basis_rows[step], there, step == owners - 1)
     return total
 
 

time: 29.1 us -> 29.1 us (level)
  no operation moved by 1% of the time
where the time goes in v6:
time: 29.1 us; the launch traced here: 28.9 us
  starting transfers between devices  13.8 us (47%)
  waiting for transfers between devices  9.9 us (34%)
  Pallas kernels  4.86 us (17%)
    ppermute x8, starting transfers between devices, exchanged(): return lax.ppermute(array, ('trades', 'dates'), pairs)  13 us
    ppermute x8, waiting for transfers between devices, exchanged(): return lax.ppermute(array, ('trades', 'dates'), pairs)  8 us
    pallas_call x2, Pallas kernels, add_grad(): pl.pallas_call(functools.partial(grad_kernel, carry, last), in_specs=[LOC...  2.28 us
    ppermute x4, waiting for transfers between devices, shifted(): lax.ppermute(array, axis, [(i, (i + step) % peers) for i in range(peers)])  1.9 us
    pallas_call x1, Pallas kernels, load(): pl.pallas_call(load_kernel, in_specs=[pl.BlockSpec(memory_space=pl.ANY)]...  1.23 us
    pallas_call x1, Pallas kernels, net(): pl.pallas_call(functools.partial(net_kernel, rounds), in_specs=[SCALAR] *...  0.86 us
    ppermute x4, starting transfers between devices, shifted(): lax.ppermute(array, axis, [(i, (i + step) % peers) for i in range(peers)])  0.86 us
  transfers between devices with their start and end apart: 12, of which 7 were waited for; matrix products, arithmetic and copies ran while one was open for 0% of the time, Pallas kernels for 9%

profile of v6, /device:TPU:0, one launch (start us, length us, event | category | flops | bytes accessed | tf_op | source)
XLA Modules:
  0.0 28.9 jit_solution(3279528933698132386)
XLA Ops:
  0.0 0.5 %collective-permute-start = (bf16[4,128,256]{2,1,0:T(8,128)(2,1)}, bf16[4,128,256]{2,1,0:T(8,128)(2,1)S(1)}, u32[]{:S(2)}, u32[]{:S(2)}) collective-permute-start(bf16[4,128,256]{2,1,0:T(8,128)(2,1)} %refs_0_.1), channel_id=1, source_target_pairs={{0,1},{1,0},{2,3},{3,2},{4,5},{5,4},{6,7},{7,6},{8,9},{9,8},{10,11... | collective-permute-start | bytes 786440 | tf_op jit(solution)/shard_map/ppermute | solution.py:65
  0.5 0.1 collective-permute-start.1
  0.5 1.2 %shard_map.73 = (bf16[256,1024]{1,0:T(8,128)(2,1)S(1)}, f32[4,1024]{1,0:T(4,128)S(1)}, bf16[4,128,256]{2,1,0:T(8,128)(2,1)S(1)}, bf16[1024,256]{1,0:T(8,128)(2,1...) custom-call(bf16[4,128,256]{2,1,0:T(8,128)(2,1)} %refs_0_.1, ...), custom_call_target="tpu_custom_call" | custom-call | flops 134217728 | bytes 524288 | tf_op jit(solution)/shard_map/pallas_call | solution.py:100
  1.8 0.1 collective-permute-done.1.refs_2_.refs_1_
  1.8 0.0 collective-permute-done.refs_1_.refs_3_
  1.8 0.9 %shard_map.74 = (f32[128,256]{1,0:T(8,128)S(1)}, f32[128,256]{1,0:T(8,128)S(1)}, f32[128,256]{1,0:T(8,128)S(1)}, f32[128,256]{1,0:T(8,128)S(1)}) custom-call(s32[1]{0:T(128)} %bitcast.4.me_ref, s32[1]{0:T(128)} %bitcast.5.trade_ref, bf16[1024,256]{1,0:T(8,128)(2,1)S(1)} %get-tuple-element.29.coef_ref, s32[1,1024]{1,0:T(1,128)S(1)} %get-tuple-element.30.type_ref, ...), custom_call_target="tpu_custom_call" | custom-call | tf_op jit(solution)/shard_map/pallas_call | solution.py:162
  2.8 4.0 %collective-permute-start.5 = (f16[128,256]{1,0:T(8,128)(2,1)S(1)}, f16[128,256]{1,0:T(8,128)(2,1)S(1)}, u32[]{:S(2)}, u32[]{:S(2)}) collective-permute-start(f16[128,256]{1,0:T(8,128)(2,1)S(1)} %multiply_convert_fusion), channel_id=1, source_target_pairs={{0,8},{1,13},{2,10},{3,15},{4,12},{5,9},{6,14},{7,11},{8,0},{9,5},... | collective-permute-start | bytes 196616 | tf_op jit(solution)/shard_map/ppermute | solution.py:60
  6.8 2.3 %collective-permute-start.4 = (f16[128,256]{1,0:T(8,128)(2,1)S(1)}, f16[128,256]{1,0:T(8,128)(2,1)S(1)}, u32[]{:S(2)}, u32[]{:S(2)}) collective-permute-start(f16[128,256]{1,0:T(8,128)(2,1)S(1)} %multiply_convert_fusion.1), channel_id=1, source_target_pairs={{0,14},{1,11},{2,12},{3,9},{4,10},{5,15},{6,8},{7,13},{8,6},{9,3},... | collective-permute-start | bytes 196616 | tf_op jit(solution)/shard_map/ppermute | solution.py:60
  9.1 0.5 %collective-permute-start.3 = (f16[128,256]{1,0:T(8,128)(2,1)S(1)}, f16[128,256]{1,0:T(8,128)(2,1)S(1)}, u32[]{:S(2)}, u32[]{:S(2)}) collective-permute-start(f16[128,256]{1,0:T(8,128)(2,1)S(1)} %multiply_convert_fusion.2), channel_id=1, source_target_pairs={{0,2},{1,7},{2,0},{3,5},{4,6},{5,3},{6,4},{7,1},{8,10},{9,15},{10,... | collective-permute-start | bytes 196616 | tf_op jit(solution)/shard_map/ppermute | solution.py:60
  9.7 0.7 %collective-permute-start.2 = (f16[128,256]{1,0:T(8,128)(2,1)S(1)}, f16[128,256]{1,0:T(8,128)(2,1)S(1)}, u32[]{:S(2)}, u32[]{:S(2)}) collective-permute-start(f16[128,256]{1,0:T(8,128)(2,1)S(1)} %multiply_convert_fusion.3), channel_id=1, source_target_pairs={{0,0},{1,5},{2,2},{3,7},{4,4},{5,1},{6,6},{7,3},{8,8},{9,13},{10,1... | collective-permute-start | bytes 196616 | tf_op jit(solution)/shard_map/ppermute | solution.py:60
  10.3 0.4 %shard_map.75 = (f32[1024,128]{1,0:T(8,128)S(1)}, bf16[512,128]{1,0:T(8,128)(2,1)S(1)}, bf16[512,128]{1,0:T(8,128)(2,1)S(1)}) custom-call(s32[1]{0:T(128)} %bitcast.4.me_ref, s32[1]{0:T(128)} %bitcast.5.trade_ref, s32[1,1024]{1,0:T(1,128)S(1)} %get-tuple-element.30.type_ref, f32[4,16]{1,0:T(4,128)S(1)} %get-tuple-element.38.refs_0_, ...), custom_call_target="tpu_custom_call" | custom-call | flops 268435456 | tf_op jit(solution)/shard_map/pallas_call | solution.py:240
  10.8 0.0 collective-permute-done.5
  10.8 3.2 %collective-permute-done.4 = f16[128,256]{1,0:T(8,128)(2,1)S(1)} collective-permute-done((f16[128,256]{1,0:T(8,128)(2,1)S(1)}, f16[128,256]{1,0:T(8,128)(2,1)S(1)}, u32[]{:S(2)}, u32[]{:S(2)}) %collective-permute-start.4) | collective-permute-done | bytes 65568 | tf_op jit(solution)/shard_map/ppermute | solution.py:60
  14.0 0.5 %collective-permute-done.3 = f16[128,256]{1,0:T(8,128)(2,1)S(1)} collective-permute-done((f16[128,256]{1,0:T(8,128)(2,1)S(1)}, f16[128,256]{1,0:T(8,128)(2,1)S(1)}, u32[]{:S(2)}, u32[]{:S(2)}) %collective-permute-start.3) | collective-permute-done | bytes 65568 | tf_op jit(solution)/shard_map/ppermute | solution.py:60
  14.5 0.0 collective-permute-done.2
  14.5 0.2 collective-permute-start.6
  14.7 1.2 %collective-permute-done.6.refs_1_ = f32[128,256]{1,0:T(8,128)S(1)} collective-permute-done((f32[128,256]{1,0:T(8,128)S(1)}, f32[128,256]{1,0:T(8,128)S(1)}, u32[]{:S(2)}, u32[]{:S(2)}) %collective-permute-start.6) | collective-permute-done | bytes 131104 | tf_op jit(solution)/shard_map/ppermute | solution.py:65
  16.0 2.5 %collective-permute-start.10 = (bf16[128,256]{1,0:T(8,128)(2,1)S(1)}, bf16[128,256]{1,0:T(8,128)(2,1)S(1)}, u32[]{:S(2)}, u32[]{:S(2)}) collective-permute-start(bf16[128,256]{1,0:T(8,128)(2,1)S(1)} %shard_map.76), channel_id=1, source_target_pairs={{0,8},{1,13},{2,10},{3,15},{4,12},{5,9},{6,14},{7,11},{8,0},{9,5},... | collective-permute-start | bytes 196616 | tf_op jit(solution)/shard_map/ppermute | solution.py:60
  18.5 1.2 %collective-permute-start.9 = (bf16[128,256]{1,0:T(8,128)(2,1)S(1)}, bf16[128,256]{1,0:T(8,128)(2,1)S(1)}, u32[]{:S(2)}, u32[]{:S(2)}) collective-permute-start(bf16[128,256]{1,0:T(8,128)(2,1)S(1)} %shard_map.76), channel_id=1, source_target_pairs={{0,14},{1,11},{2,12},{3,9},{4,10},{5,15},{6,8},{7,13},{8,6},{9,3},... | collective-permute-start | bytes 196616 | tf_op jit(solution)/shard_map/ppermute | solution.py:60
  19.6 1.2 %collective-permute-start.8 = (bf16[128,256]{1,0:T(8,128)(2,1)S(1)}, bf16[128,256]{1,0:T(8,128)(2,1)S(1)}, u32[]{:S(2)}, u32[]{:S(2)}) collective-permute-start(bf16[128,256]{1,0:T(8,128)(2,1)S(1)} %shard_map.76), channel_id=1, source_target_pairs={{0,2},{1,7},{2,0},{3,5},{4,6},{5,3},{6,4},{7,1},{8,10},{9,15},{10,... | collective-permute-start | bytes 196616 | tf_op jit(solution)/shard_map/ppermute | solution.py:60
  20.8 0.7 %collective-permute-start.7 = (bf16[128,256]{1,0:T(8,128)(2,1)S(1)}, bf16[128,256]{1,0:T(8,128)(2,1)S(1)}, u32[]{:S(2)}, u32[]{:S(2)}) collective-permute-start(bf16[128,256]{1,0:T(8,128)(2,1)S(1)} %shard_map.76), channel_id=1, source_target_pairs={{0,0},{1,5},{2,2},{3,7},{4,4},{5,1},{6,6},{7,3},{8,8},{9,13},{10,1... | collective-permute-start | bytes 196616 | tf_op jit(solution)/shard_map/ppermute | solution.py:60
  21.5 2.1 %collective-permute-done.10.refs_3_ = bf16[128,256]{1,0:T(8,128)(2,1)S(1)} collective-permute-done((bf16[128,256]{1,0:T(8,128)(2,1)S(1)}, bf16[128,256]{1,0:T(8,128)(2,1)S(1)}, u32[]{:S(2)}, u32[]{:S(2)}) %collective-permute-start.10) | collective-permute-done | bytes 65568 | tf_op jit(solution)/shard_map/ppermute | solution.py:60
  23.6 2.2 %collective-permute-done.9.refs_2_ = bf16[128,256]{1,0:T(8,128)(2,1)S(1)} collective-permute-done((bf16[128,256]{1,0:T(8,128)(2,1)S(1)}, bf16[128,256]{1,0:T(8,128)(2,1)S(1)}, u32[]{:S(2)}, u32[]{:S(2)}) %collective-permute-start.9) | collective-permute-done | bytes 65568 | tf_op jit(solution)/shard_map/ppermute | solution.py:60
  25.7 0.0 collective-permute-done.8.refs_1_
  25.7 0.0 collective-permute-done.7.refs_0_
  25.8 0.2 collective-permute-start.11
  26.0 0.8 %shard_map.77.refs_0_ = f32[1024,128]{1,0:T(8,128)S(1)} custom-call(bf16[256,1024]{1,0:T(8,128)(2,1)S(1)} %get-tuple-element.28.member_ref, f32[1024,128]{1,0:T(8,128)S(1)} %get-tuple-element.42.gain_ref, bf16[512,128]{1,0:T(8,128)(2,1)S(1)} %get-tuple-element.44.basis_ref, bf16[128,256]{1,0:T(8,128)(2,1)S(1)} %collective-permute-done.7.refs_0_, ...), custom_call_target="tpu_custom_call" | custom-call | flops 402653184 | bytes 524288 | tf_op jit(solution)/shard_map/pallas_call | solution.py:295
  26.8 0.6 %collective-permute-done.11 = bf16[4,128,256]{2,1,0:T(8,128)(2,1)S(1)} collective-permute-done((bf16[4,128,256]{2,1,0:T(8,128)(2,1)S(1)}, bf16[4,128,256]{2,1,0:T(8,128)(2,1)S(1)}, u32[]{:S(2)}, u32[]{:S(2)}) %collective-permute-start.11) | collective-permute-done | bytes 262176 | tf_op jit(solution)/shard_map/ppermute | solution.py:65
  27.4 1.4 %shard_map.78 = f32[1024,128]{1,0:T(8,128)} custom-call(bf16[256,1024]{1,0:T(8,128)(2,1)S(1)} %get-tuple-element.28.member_ref, f32[1024,128]{1,0:T(8,128)S(1)} %get-tuple-element.42.gain_ref, bf16[512,128]{1,0:T(8,128)(2,1)S(1)} %get-tuple-element.43.basis_ref, f32[1024,128]{1,0:T(8,128)S(1)} %shard_map.77.refs_0_, ...), custom_call_target="tpu_custom_call" | custom-call | flops 402653184 | bytes 524288 | tf_op jit(solution)/shard_map/pallas_call | solution.py:295
  (8 shorter events, 0.2 us)
Async XLA Ops:
  0.0 1.8 %collective-permute-start = (bf16[4,128,256]{2,1,0:T(8,128)(2,1)}, bf16[4,128,256]{2,1,0:T(8,128)(2,1)S(1)}, u32[]{:S(2)}, u32[]{:S(2)}) collective-permute-start(bf16[4,128,256]{2,1,0:T(8,128)(2,1)} %refs_0_.1), channel_id=1, source_target_pairs={{0,1},{1,0},{2,3},{3,2},{4,5},{5,4},{6,7},{7,6},{8,9},{9,8},{10,11... | collective-permute-start | bytes 786440 | tf_op jit(solution)/shard_map/ppermute | solution.py:65
  0.5 1.4 %collective-permute-start.1 = (f32[4,16]{1,0:T(4,128)}, f32[4,16]{1,0:T(4,128)S(1)}, u32[]{:S(2)}, u32[]{:S(2)}) collective-permute-start(f32[4,16]{1,0:T(4,128)} %refs_3_.1), channel_id=1, source_target_pairs={{0,1},{1,0},{2,3},{3,2},{4,5},{5,4},{6,7},{7,6},{8,9},{9,8},{10,11... | collective-permute-start | bytes 776 | tf_op jit(solution)/shard_map/ppermute | solution.py:65
  2.8 8.0 %collective-permute-start.5 = (f16[128,256]{1,0:T(8,128)(2,1)S(1)}, f16[128,256]{1,0:T(8,128)(2,1)S(1)}, u32[]{:S(2)}, u32[]{:S(2)}) collective-permute-start(f16[128,256]{1,0:T(8,128)(2,1)S(1)} %multiply_convert_fusion), channel_id=1, source_target_pairs={{0,8},{1,13},{2,10},{3,15},{4,12},{5,9},{6,14},{7,11},{8,0},{9,5},... | collective-permute-start | bytes 196616 | tf_op jit(solution)/shard_map/ppermute | solution.py:60
  6.8 7.1 %collective-permute-start.4 = (f16[128,256]{1,0:T(8,128)(2,1)S(1)}, f16[128,256]{1,0:T(8,128)(2,1)S(1)}, u32[]{:S(2)}, u32[]{:S(2)}) collective-permute-start(f16[128,256]{1,0:T(8,128)(2,1)S(1)} %multiply_convert_fusion.1), channel_id=1, source_target_pairs={{0,14},{1,11},{2,12},{3,9},{4,10},{5,15},{6,8},{7,13},{8,6},{9,3},... | collective-permute-start | bytes 196616 | tf_op jit(solution)/shard_map/ppermute | solution.py:60
  9.1 5.4 %collective-permute-start.3 = (f16[128,256]{1,0:T(8,128)(2,1)S(1)}, f16[128,256]{1,0:T(8,128)(2,1)S(1)}, u32[]{:S(2)}, u32[]{:S(2)}) collective-permute-start(f16[128,256]{1,0:T(8,128)(2,1)S(1)} %multiply_convert_fusion.2), channel_id=1, source_target_pairs={{0,2},{1,7},{2,0},{3,5},{4,6},{5,3},{6,4},{7,1},{8,10},{9,15},{10,... | collective-permute-start | bytes 196616 | tf_op jit(solution)/shard_map/ppermute | solution.py:60
  9.7 4.8 %collective-permute-start.2 = (f16[128,256]{1,0:T(8,128)(2,1)S(1)}, f16[128,256]{1,0:T(8,128)(2,1)S(1)}, u32[]{:S(2)}, u32[]{:S(2)}) collective-permute-start(f16[128,256]{1,0:T(8,128)(2,1)S(1)} %multiply_convert_fusion.3), channel_id=1, source_target_pairs={{0,0},{1,5},{2,2},{3,7},{4,4},{5,1},{6,6},{7,3},{8,8},{9,13},{10,1... | collective-permute-start | bytes 196616 | tf_op jit(solution)/shard_map/ppermute | solution.py:60
  14.5 1.4 %collective-permute-start.6 = (f32[128,256]{1,0:T(8,128)S(1)}, f32[128,256]{1,0:T(8,128)S(1)}, u32[]{:S(2)}, u32[]{:S(2)}) collective-permute-start(f32[128,256]{1,0:T(8,128)S(1)} %convert_add_fusion.refs_0_), channel_id=1, source_target_pairs={{0,1},{1,0},{2,3},{3,2},{4,5},{5,4},{6,7},{7,6},{8,9},{9,8},{10,11... | collective-permute-start | bytes 393224 | tf_op jit(solution)/shard_map/ppermute | solution.py:65
  16.0 7.6 %collective-permute-start.10 = (bf16[128,256]{1,0:T(8,128)(2,1)S(1)}, bf16[128,256]{1,0:T(8,128)(2,1)S(1)}, u32[]{:S(2)}, u32[]{:S(2)}) collective-permute-start(bf16[128,256]{1,0:T(8,128)(2,1)S(1)} %shard_map.76), channel_id=1, source_target_pairs={{0,8},{1,13},{2,10},{3,15},{4,12},{5,9},{6,14},{7,11},{8,0},{9,5},... | collective-permute-start | bytes 196616 | tf_op jit(solution)/shard_map/ppermute | solution.py:60
  18.5 7.3 %collective-permute-start.9 = (bf16[128,256]{1,0:T(8,128)(2,1)S(1)}, bf16[128,256]{1,0:T(8,128)(2,1)S(1)}, u32[]{:S(2)}, u32[]{:S(2)}) collective-permute-start(bf16[128,256]{1,0:T(8,128)(2,1)S(1)} %shard_map.76), channel_id=1, source_target_pairs={{0,14},{1,11},{2,12},{3,9},{4,10},{5,15},{6,8},{7,13},{8,6},{9,3},... | collective-permute-start | bytes 196616 | tf_op jit(solution)/shard_map/ppermute | solution.py:60
  19.6 6.1 %collective-permute-start.8 = (bf16[128,256]{1,0:T(8,128)(2,1)S(1)}, bf16[128,256]{1,0:T(8,128)(2,1)S(1)}, u32[]{:S(2)}, u32[]{:S(2)}) collective-permute-start(bf16[128,256]{1,0:T(8,128)(2,1)S(1)} %shard_map.76), channel_id=1, source_target_pairs={{0,2},{1,7},{2,0},{3,5},{4,6},{5,3},{6,4},{7,1},{8,10},{9,15},{10,... | collective-permute-start | bytes 196616 | tf_op jit(solution)/shard_map/ppermute | solution.py:60
  20.8 4.9 %collective-permute-start.7 = (bf16[128,256]{1,0:T(8,128)(2,1)S(1)}, bf16[128,256]{1,0:T(8,128)(2,1)S(1)}, u32[]{:S(2)}, u32[]{:S(2)}) collective-permute-start(bf16[128,256]{1,0:T(8,128)(2,1)S(1)} %shard_map.76), channel_id=1, source_target_pairs={{0,0},{1,5},{2,2},{3,7},{4,4},{5,1},{6,6},{7,3},{8,8},{9,13},{10,1... | collective-permute-start | bytes 196616 | tf_op jit(solution)/shard_map/ppermute | solution.py:60
  25.8 1.6 %collective-permute-start.11 = (bf16[4,128,256]{2,1,0:T(8,128)(2,1)S(1)}, bf16[4,128,256]{2,1,0:T(8,128)(2,1)S(1)}, u32[]{:S(2)}, u32[]{:S(2)}) collective-permute-start(bf16[4,128,256]{2,1,0:T(8,128)(2,1)S(1)} %pad_maximum_fusion), channel_id=1, source_target_pairs={{0,1},{1,0},{2,3},{3,2},{4,5},{5,4},{6,7},{7,6},{8,9},{9,8},{10,11... | collective-permute-start | bytes 786440 | tf_op jit(solution)/shard_map/ppermute | solution.py:65

commit v7 on v6

--- a/solution.py
+++ b/solution.py
@@ -9,9 +9,10 @@
 from jax.sharding import PartitionSpec as P
 
 LAG_MAX = 2
-ROWS = 512
+ROWS = 1024
 PIECES = 4
-ORDER = (0, 2, 1, 3, 7, 5, 4, 6)
+ORDER_IN = (0, 2, 1, 3, 7, 5, 4, 6)
+ORDER_OUT = (0, 1, 2, 3, 7, 6, 4, 5)
 NT = (((1,), (1,)), ((), ()))
 TN = (((0,), (0,)), ((), ()))
 TT = (((0,), (1,)), ((), ()))
@@ -28,11 +29,18 @@
     return pltpu.VMEM(array.shape, array.dtype)
 
 
-def rounds_of(peers, owners):
-    base = ORDER if peers % len(ORDER) == 0 else range(peers)
-    offsets = [first + offset for first in range(0, peers, len(base)) for offset in base]
-    assert peers % owners == 0
-    return [tuple(offsets[at : at + owners]) for at in range(0, peers, owners)]
+def offsets_of(order, peers):
+    base = order if peers % len(order) == 0 else range(peers)
+    return [first + offset for first in range(0, peers, len(base)) for offset in base]
+
+
+def rounds_of(offsets, owners):
+    assert len(offsets) % owners == 0
+    return [tuple(offsets[at : at + owners]) for at in range(0, len(offsets), owners)]
+
+
+def shared_of(peers, owners):
+    return range(1, 1 + (peers - 1) % owners)
 
 
 def target_of(index, offset, peers):
@@ -58,6 +66,22 @@
         for core in range(owners)
     ]
     return lax.ppermute(array, ("trades", "dates"), pairs)
+
+
+def together_kernel(count, *refs):
+    for at in range(count):
+        refs[-1][at] = refs[at - 1 - count][...]
+
+
+def together_of(arrays, others):
+    shape = (len(arrays),) + arrays[0].shape
+    return pl.pallas_call(
+        functools.partial(together_kernel, len(arrays)),
+        in_specs=[LOCAL] * (len(arrays) + len(others)),
+        out_specs=LOCAL,
+        out_shape=pltpu.VMEM(shape, arrays[0].dtype),
+        compiler_params=PARAMS,
+    )(*others, *arrays)
 
 
 def shifted(array, axis, step):
@@ -112,9 +136,8 @@
     )(*in_hbm(basis, coef, types, gain, lags, limits, sets))
 
 
-def net_kernel(rounds, me_ref, trade_ref, coef_ref, type_ref, member_ref, lags_ref, gain_rows_ref, *refs):
+def net_kernel(rounds, peers, me_ref, trade_ref, coef_ref, type_ref, member_ref, lags_ref, gain_rows_ref, *refs):
     owners = len(rounds[0])
-    peers = owners * len(rounds)
     bases, gains, outs = refs[:owners], refs[owners : 2 * owners - 1], refs[2 * owners - 1 :]
     me, trade = me_ref[0], trade_ref[0]
     coef, member, lags = coef_ref[...], member_ref[...], lags_ref[...]
@@ -155,12 +178,12 @@
                 out_ref[pl.ds(pl.multiple_of(row, block_paths), block_paths)] = value
 
 
-def net(rounds, me, trade, coef, types, member, lags, gain_rows, bases, later_gains):
+def net(rounds, peers, me, trade, coef, types, member, lags, gain_rows, bases, later_gains):
     owners = len(bases)
     local_dates, paths, _ = bases[0].shape
-    rows = local_dates * paths // len(rounds)
-    return pl.pallas_call(
-        functools.partial(net_kernel, rounds),
+    rows = owners * local_dates * paths // peers
+    return pl.pallas_call(
+        functools.partial(net_kernel, rounds, peers),
         in_specs=[SCALAR] * 2 + [LOCAL] * (4 + 2 * owners),
         out_specs=[LOCAL] * len(rounds),
         out_shape=[pltpu.VMEM((rows, member.shape[0]), jnp.float32)] * len(rounds),
@@ -195,9 +218,8 @@
     )(lags, limits, *sums)
 
 
-def ready_kernel(rounds, me_ref, trade_ref, type_ref, *refs):
+def ready_kernel(rounds, near, peers, me_ref, trade_ref, type_ref, *refs):
     owners = len(rounds[0])
-    peers = owners * len(rounds)
     gain_refs, basis_refs = refs[:owners], refs[owners : 2 * owners]
     gain_ref, *out_refs = refs[2 * owners :]
     local_dates, paths, _ = basis_refs[0].shape
@@ -209,7 +231,7 @@
     columns = pl.ds(pl.multiple_of(me * own_depth, own_depth), own_depth)
     for step, out_ref in enumerate(out_refs):
         core = lax.rem(me + (owners - step), owners)
-        for at, offsets in enumerate(rounds):
+        for at, offsets in enumerate(rounds if step else near + rounds):
             source = source_of(trade, offset_at(core, offsets), peers)
             span = pl.ds(pl.multiple_of(source * block_paths, block_paths), block_paths)
             for place, ref in enumerate(basis_refs):
@@ -232,17 +254,17 @@
     gain_ref[...] = lax.dot_general(pieces, expand, TN, preferred_element_type=jnp.float32)
 
 
-def ready(rounds, me, trade, types, gains, bases):
+def ready(rounds, near, peers, me, trade, types, gains, bases):
     owners = len(bases)
     local_dates, paths, depth = bases[0].shape
-    block_rows = owners * local_dates * paths // (owners * len(rounds))
-    rows = block_rows * len(rounds)
-    return pl.pallas_call(
-        functools.partial(ready_kernel, rounds),
+    block_rows = owners * local_dates * paths // peers
+    counts = [len(rounds) + len(near)] + [len(rounds)] * (owners - 1)
+    return pl.pallas_call(
+        functools.partial(ready_kernel, rounds, near, peers),
         in_specs=[SCALAR] * 2 + [LOCAL] * (1 + 2 * owners),
         out_specs=[LOCAL] * (1 + owners),
         out_shape=[pltpu.VMEM((types.shape[1], math.lcm(block_rows, 128)), jnp.float32)]
-        + [pltpu.VMEM((rows, depth // owners), jnp.bfloat16)] * owners,
+        + [pltpu.VMEM((block_rows * count, depth // owners), jnp.bfloat16) for count in counts],
         compiler_params=PARAMS,
         cost_estimate=pl.CostEstimate(flops=types.shape[1] * 256 * 1024, bytes_accessed=0, transcendentals=0),
     )(me, trade, types, *gains, *bases)
@@ -313,7 +335,11 @@
     set_count = thresholds.shape[0]
     peers = lax.axis_size("trades")
     owners = lax.axis_size("dates")
-    rounds = rounds_of(peers, owners)
+    rounds_in = rounds_of(offsets_of(ORDER_IN, peers), owners)
+    shared = shared_of(peers, owners)
+    rounds_out = [offset for offset in offsets_of(ORDER_OUT, peers) if offset > len(shared)]
+    rounds_out = rounds_of(rounds_out, owners)
+    near = [(offset,) * owners for offset in shared]
     block_paths = path_count // peers
     scale = 2.0 / math.sqrt(local_dates * owners * path_count)
     me = lax.axis_index("dates").astype(jnp.int32).reshape(1)
@@ -331,22 +357,22 @@
         thresholds.reshape(1, set_count),
     )
     bases, gains = [basis] + bases, [gain] + gains
-    partials = net(rounds, me, trade, coef, types, member, lags, gain_rows, bases, gains[1:])
+    partials = net(rounds_in, peers, me, trade, coef, types, member, lags, gain_rows, bases, gains[1:])
     arrived = [
         exchanged((partial * 0.5).astype(jnp.float16), offsets, peers)
-        for partial, offsets in zip(partials, rounds, strict=True)
+        for partial, offsets in zip(partials, rounds_in, strict=True)
     ]
-    trade_gain, *basis_rows = ready(rounds, me, trade, types, gains, bases)
+    trade_gain, *basis_rows = ready(rounds_out, near + [(0,) * owners], peers, me, trade, types, gains, bases)
     excess = functools.reduce(jnp.add, [part.astype(jnp.float32) for part in arrived])
     excess, trade_gain, *basis_rows = lax.optimization_barrier((excess, trade_gain, *basis_rows))
     sums = [excess] + [shifted(excess, "dates", step) for step in range(1, owners)]
     adjoint = adjoint_of(sums, lags, limits, scale, block_paths)
-    adjoints = lax.optimization_barrier([exchanged(adjoint, offsets, peers) for offsets in rounds])
-
-    block = jnp.stack(adjoints)
-    total = None
-    for step in range(owners):
-        there = list(shifted(block, "dates", step)) if step else adjoints
+    close = [exchanged(adjoint, offsets, peers) for offsets in near] + [adjoint]
+    apart = [exchanged(adjoint, offsets, peers) for offsets in rounds_out]
+    whole = together_of(apart, close)
+    total = add_grad(None, member, trade_gain, basis_rows[0], close + apart, False)
+    for step in range(1, owners):
+        there = list(shifted(whole, "dates", step))
         total = add_grad(total, member, trade_gain, basis_rows[step], there, step == owners - 1)
     return total
 

time: 29.1 us -> 28.9 us (level)
  starting transfers between devices: 13.8 us -> 13.4 us
    ppermute x8, waiting for transfers between devices: 8 us -> 8.46 us  [exchanged(): return lax.ppermute(array, ('trades', 'dates'), pairs)]
    ppermute x8, starting transfers between devices: 13 us -> 12.5 us  [exchanged(): return lax.ppermute(array, ('trades', 'dates'), pairs)]
    pallas_call x2 -> x3, Pallas kernels: 1.3 us -> 1.3 us  [the longest x1 0.86 us: net(): pl.pallas_call(functools.partial(net_kernel, rounds, peers), in_specs=[SC...]
where the time goes in v7:
time: 28.9 us; the launch traced here: 28.7 us
  starting transfers between devices  13.4 us (46%)
  waiting for transfers between devices  10.1 us (35%)
  Pallas kernels  4.93 us (17%)
    ppermute x8, starting transfers between devices, exchanged(): return lax.ppermute(array, ('trades', 'dates'), pairs)  12.5 us
    ppermute x8, waiting for transfers between devices, exchanged(): return lax.ppermute(array, ('trades', 'dates'), pairs)  8.46 us
    pallas_call x2, Pallas kernels, add_grad(): pl.pallas_call(functools.partial(grad_kernel, carry, last), in_specs=[LOC...  2.35 us
    ppermute x4, waiting for transfers between devices, shifted(): lax.ppermute(array, axis, [(i, (i + step) % peers) for i in range(peers)])  1.68 us
    pallas_call x1, Pallas kernels, load(): pl.pallas_call(load_kernel, in_specs=[pl.BlockSpec(memory_space=pl.ANY)]...  1.23 us
    ppermute x4, starting transfers between devices, shifted(): lax.ppermute(array, axis, [(i, (i + step) % peers) for i in range(peers)])  0.86 us
    pallas_call x1, Pallas kernels, net(): pl.pallas_call(functools.partial(net_kernel, rounds, peers), in_specs=[SC...  0.86 us
  transfers between devices with their start and end apart: 12, of which 7 were waited for; matrix products, arithmetic and copies ran while one was open for 0% of the time, Pallas kernels for 9%

profile of v7, /device:TPU:0, one launch (start us, length us, event | category | flops | bytes accessed | tf_op | source)
XLA Modules:
  0.0 28.7 jit_solution(9980290000583999886)
XLA Ops:
  0.0 0.5 %collective-permute-start = (bf16[4,128,256]{2,1,0:T(8,128)(2,1)}, bf16[4,128,256]{2,1,0:T(8,128)(2,1)S(1)}, u32[]{:S(2)}, u32[]{:S(2)}) collective-permute-start(bf16[4,128,256]{2,1,0:T(8,128)(2,1)} %refs_0_.1), channel_id=1, source_target_pairs={{0,1},{1,0},{2,3},{3,2},{4,5},{5,4},{6,7},{7,6},{8,9},{9,8},{10,11... | collective-permute-start | bytes 786440 | tf_op jit(solution)/shard_map/ppermute | solution.py:89
  0.5 0.1 collective-permute-start.1
  0.5 1.2 %shard_map.73 = (bf16[256,1024]{1,0:T(8,128)(2,1)S(1)}, f32[4,1024]{1,0:T(4,128)S(1)}, bf16[4,128,256]{2,1,0:T(8,128)(2,1)S(1)}, bf16[1024,256]{1,0:T(8,128)(2,1...) custom-call(bf16[4,128,256]{2,1,0:T(8,128)(2,1)} %refs_0_.1, ...), custom_call_target="tpu_custom_call" | custom-call | flops 134217728 | bytes 524288 | tf_op jit(solution)/shard_map/pallas_call | solution.py:124
  1.8 0.1 collective-permute-done.1.refs_2_.refs_1_
  1.8 0.0 collective-permute-done.refs_1_.refs_3_
  1.8 0.9 %shard_map.74 = (f32[128,256]{1,0:T(8,128)S(1)}, f32[128,256]{1,0:T(8,128)S(1)}, f32[128,256]{1,0:T(8,128)S(1)}, f32[128,256]{1,0:T(8,128)S(1)}) custom-call(s32[1]{0:T(128)} %bitcast.4.me_ref, s32[1]{0:T(128)} %bitcast.5.trade_ref, bf16[1024,256]{1,0:T(8,128)(2,1)S(1)} %get-tuple-element.25.coef_ref, s32[1,1024]{1,0:T(1,128)S(1)} %get-tuple-element.26.type_ref, ...), custom_call_target="tpu_custom_call" | custom-call | tf_op jit(solution)/shard_map/pallas_call | solution.py:185
  2.8 4.0 %collective-permute-start.5 = (f16[128,256]{1,0:T(8,128)(2,1)S(1)}, f16[128,256]{1,0:T(8,128)(2,1)S(1)}, u32[]{:S(2)}, u32[]{:S(2)}) collective-permute-start(f16[128,256]{1,0:T(8,128)(2,1)S(1)} %multiply_convert_fusion), channel_id=1, source_target_pairs={{0,8},{1,13},{2,10},{3,15},{4,12},{5,9},{6,14},{7,11},{8,0},{9,5},... | collective-permute-start | bytes 196616 | tf_op jit(solution)/shard_map/ppermute | solution.py:68
  6.8 2.3 %collective-permute-start.4 = (f16[128,256]{1,0:T(8,128)(2,1)S(1)}, f16[128,256]{1,0:T(8,128)(2,1)S(1)}, u32[]{:S(2)}, u32[]{:S(2)}) collective-permute-start(f16[128,256]{1,0:T(8,128)(2,1)S(1)} %multiply_convert_fusion.1), channel_id=1, source_target_pairs={{0,14},{1,11},{2,12},{3,9},{4,10},{5,15},{6,8},{7,13},{8,6},{9,3},... | collective-permute-start | bytes 196616 | tf_op jit(solution)/shard_map/ppermute | solution.py:68
  9.1 0.5 %collective-permute-start.3 = (f16[128,256]{1,0:T(8,128)(2,1)S(1)}, f16[128,256]{1,0:T(8,128)(2,1)S(1)}, u32[]{:S(2)}, u32[]{:S(2)}) collective-permute-start(f16[128,256]{1,0:T(8,128)(2,1)S(1)} %multiply_convert_fusion.2), channel_id=1, source_target_pairs={{0,2},{1,7},{2,0},{3,5},{4,6},{5,3},{6,4},{7,1},{8,10},{9,15},{10,... | collective-permute-start | bytes 196616 | tf_op jit(solution)/shard_map/ppermute | solution.py:68
  9.7 0.7 %collective-permute-start.2 = (f16[128,256]{1,0:T(8,128)(2,1)S(1)}, f16[128,256]{1,0:T(8,128)(2,1)S(1)}, u32[]{:S(2)}, u32[]{:S(2)}) collective-permute-start(f16[128,256]{1,0:T(8,128)(2,1)S(1)} %multiply_convert_fusion.3), channel_id=1, source_target_pairs={{0,0},{1,5},{2,2},{3,7},{4,4},{5,1},{6,6},{7,3},{8,8},{9,13},{10,1... | collective-permute-start | bytes 196616 | tf_op jit(solution)/shard_map/ppermute | solution.py:68
  10.3 0.4 %shard_map.75 = (f32[1024,128]{1,0:T(8,128)S(1)}, bf16[640,128]{1,0:T(8,128)(2,1)S(1)}, bf16[384,128]{1,0:T(8,128)(2,1)S(1)}) custom-call(s32[1]{0:T(128)} %bitcast.4.me_ref, s32[1]{0:T(128)} %bitcast.5.trade_ref, s32[1,1024]{1,0:T(1,128)S(1)} %get-tuple-element.26.type_ref, f32[4,16]{1,0:T(4,128)S(1)} %get-tuple-element.34.refs_0_, ...), custom_call_target="tpu_custom_call" | custom-call | flops 268435456 | tf_op jit(solution)/shard_map/pallas_call | solution.py:262
  10.7 0.0 collective-permute-done.5
  10.8 3.2 %collective-permute-done.4 = f16[128,256]{1,0:T(8,128)(2,1)S(1)} collective-permute-done((f16[128,256]{1,0:T(8,128)(2,1)S(1)}, f16[128,256]{1,0:T(8,128)(2,1)S(1)}, u32[]{:S(2)}, u32[]{:S(2)}) %collective-permute-start.4) | collective-permute-done | bytes 65568 | tf_op jit(solution)/shard_map/ppermute | solution.py:68
  14.0 0.5 %collective-permute-done.3 = f16[128,256]{1,0:T(8,128)(2,1)S(1)} collective-permute-done((f16[128,256]{1,0:T(8,128)(2,1)S(1)}, f16[128,256]{1,0:T(8,128)(2,1)S(1)}, u32[]{:S(2)}, u32[]{:S(2)}) %collective-permute-start.3) | collective-permute-done | bytes 65568 | tf_op jit(solution)/shard_map/ppermute | solution.py:68
  14.5 0.0 collective-permute-done.2
  14.5 0.2 collective-permute-start.6
  14.7 1.2 %collective-permute-done.6.refs_1_ = f32[128,256]{1,0:T(8,128)S(1)} collective-permute-done((f32[128,256]{1,0:T(8,128)S(1)}, f32[128,256]{1,0:T(8,128)S(1)}, u32[]{:S(2)}, u32[]{:S(2)}) %collective-permute-start.6) | collective-permute-done | bytes 131104 | tf_op jit(solution)/shard_map/ppermute | solution.py:89
  16.0 2.5 %collective-permute-start.10 = (bf16[128,256]{1,0:T(8,128)(2,1)S(1)}, bf16[128,256]{1,0:T(8,128)(2,1)S(1)}, u32[]{:S(2)}, u32[]{:S(2)}) collective-permute-start(bf16[128,256]{1,0:T(8,128)(2,1)S(1)} %shard_map.76.refs_1_), channel_id=1, source_target_pairs={{0,8},{1,11},{2,10},{3,9},{4,12},{5,15},{6,14},{7,13},{8,0},{9,3},... | collective-permute-start | bytes 196616 | tf_op jit(solution)/shard_map/ppermute | solution.py:68
  18.5 1.2 %collective-permute-start.9 = (bf16[128,256]{1,0:T(8,128)(2,1)S(1)}, bf16[128,256]{1,0:T(8,128)(2,1)S(1)}, u32[]{:S(2)}, u32[]{:S(2)}) collective-permute-start(bf16[128,256]{1,0:T(8,128)(2,1)S(1)} %shard_map.76.refs_1_), channel_id=1, source_target_pairs={{0,14},{1,13},{2,12},{3,15},{4,10},{5,9},{6,8},{7,11},{8,6},{9,5},... | collective-permute-start | bytes 196616 | tf_op jit(solution)/shard_map/ppermute | solution.py:68
  19.6 0.8 %collective-permute-start.8 = (bf16[128,256]{1,0:T(8,128)(2,1)S(1)}, bf16[128,256]{1,0:T(8,128)(2,1)S(1)}, u32[]{:S(2)}, u32[]{:S(2)}) collective-permute-start(bf16[128,256]{1,0:T(8,128)(2,1)S(1)} %shard_map.76.refs_1_), channel_id=1, source_target_pairs={{0,4},{1,7},{2,6},{3,5},{4,0},{5,3},{6,2},{7,1},{8,12},{9,15},{10,... | collective-permute-start | bytes 196616 | tf_op jit(solution)/shard_map/ppermute | solution.py:68
  20.4 0.6 %collective-permute-start.7 = (bf16[128,256]{1,0:T(8,128)(2,1)S(1)}, bf16[128,256]{1,0:T(8,128)(2,1)S(1)}, u32[]{:S(2)}, u32[]{:S(2)}) collective-permute-start(bf16[128,256]{1,0:T(8,128)(2,1)S(1)} %shard_map.76.refs_1_), channel_id=1, source_target_pairs={{0,2},{1,3},{2,0},{3,1},{4,6},{5,7},{6,4},{7,5},{8,10},{9,11},{10,... | collective-permute-start | bytes 196616 | tf_op jit(solution)/shard_map/ppermute | solution.py:68
  21.0 2.0 %collective-permute-done.10.refs_4_ = bf16[128,256]{1,0:T(8,128)(2,1)S(1)} collective-permute-done((bf16[128,256]{1,0:T(8,128)(2,1)S(1)}, bf16[128,256]{1,0:T(8,128)(2,1)S(1)}, u32[]{:S(2)}, u32[]{:S(2)}) %collective-permute-start.10) | collective-permute-done | bytes 65568 | tf_op jit(solution)/shard_map/ppermute | solution.py:68
  23.0 2.8 %collective-permute-done.9.refs_3_ = bf16[128,256]{1,0:T(8,128)(2,1)S(1)} collective-permute-done((bf16[128,256]{1,0:T(8,128)(2,1)S(1)}, bf16[128,256]{1,0:T(8,128)(2,1)S(1)}, u32[]{:S(2)}, u32[]{:S(2)}) %collective-permute-start.9) | collective-permute-done | bytes 65568 | tf_op jit(solution)/shard_map/ppermute | solution.py:68
  25.7 0.0 collective-permute-done.8.refs_2_
  25.7 0.0 collective-permute-done.7.refs_0_
  25.8 0.2 collective-permute-start.11
  25.9 1.0 %shard_map.77.refs_0_ = f32[1024,128]{1,0:T(8,128)S(1)} custom-call(bf16[256,1024]{1,0:T(8,128)(2,1)S(1)} %get-tuple-element.24.member_ref, f32[1024,128]{1,0:T(8,128)S(1)} %get-tuple-element.38.gain_ref, bf16[640,128]{1,0:T(8,128)(2,1)S(1)} %get-tuple-element.40.basis_ref, bf16[128,256]{1,0:T(8,128)(2,1)S(1)} %collective-permute-done.7.refs_0_, ...), custom_call_target="tpu_custom_call" | custom-call | flops 503316480 | bytes 524288 | tf_op jit(solution)/shard_map/pallas_call | solution.py:317
  26.9 0.4 %collective-permute-done.11 = bf16[3,128,256]{2,1,0:T(8,128)(2,1)S(1)} collective-permute-done((bf16[3,128,256]{2,1,0:T(8,128)(2,1)S(1)}, bf16[3,128,256]{2,1,0:T(8,128)(2,1)S(1)}, u32[]{:S(2)}, u32[]{:S(2)}) %collective-permute-start.11) | collective-permute-done | bytes 196640 | tf_op jit(solution)/shard_map/ppermute | solution.py:89
  27.3 1.4 %shard_map.79 = f32[1024,128]{1,0:T(8,128)} custom-call(bf16[256,1024]{1,0:T(8,128)(2,1)S(1)} %get-tuple-element.24.member_ref, f32[1024,128]{1,0:T(8,128)S(1)} %get-tuple-element.38.gain_ref, bf16[384,128]{1,0:T(8,128)(2,1)S(1)} %get-tuple-element.39.basis_ref, f32[1024,128]{1,0:T(8,128)S(1)} %shard_map.77.refs_0_, ...), custom_call_target="tpu_custom_call" | custom-call | flops 301989888 | bytes 524288 | tf_op jit(solution)/shard_map/pallas_call | solution.py:317
  (8 shorter events, 0.2 us)
Async XLA Ops:
  0.0 1.8 %collective-permute-start = (bf16[4,128,256]{2,1,0:T(8,128)(2,1)}, bf16[4,128,256]{2,1,0:T(8,128)(2,1)S(1)}, u32[]{:S(2)}, u32[]{:S(2)}) collective-permute-start(bf16[4,128,256]{2,1,0:T(8,128)(2,1)} %refs_0_.1), channel_id=1, source_target_pairs={{0,1},{1,0},{2,3},{3,2},{4,5},{5,4},{6,7},{7,6},{8,9},{9,8},{10,11... | collective-permute-start | bytes 786440 | tf_op jit(solution)/shard_map/ppermute | solution.py:89
  0.5 1.4 %collective-permute-start.1 = (f32[4,16]{1,0:T(4,128)}, f32[4,16]{1,0:T(4,128)S(1)}, u32[]{:S(2)}, u32[]{:S(2)}) collective-permute-start(f32[4,16]{1,0:T(4,128)} %refs_3_.1), channel_id=1, source_target_pairs={{0,1},{1,0},{2,3},{3,2},{4,5},{5,4},{6,7},{7,6},{8,9},{9,8},{10,11... | collective-permute-start | bytes 776 | tf_op jit(solution)/shard_map/ppermute | solution.py:89
  2.8 8.0 %collective-permute-start.5 = (f16[128,256]{1,0:T(8,128)(2,1)S(1)}, f16[128,256]{1,0:T(8,128)(2,1)S(1)}, u32[]{:S(2)}, u32[]{:S(2)}) collective-permute-start(f16[128,256]{1,0:T(8,128)(2,1)S(1)} %multiply_convert_fusion), channel_id=1, source_target_pairs={{0,8},{1,13},{2,10},{3,15},{4,12},{5,9},{6,14},{7,11},{8,0},{9,5},... | collective-permute-start | bytes 196616 | tf_op jit(solution)/shard_map/ppermute | solution.py:68
  6.8 7.1 %collective-permute-start.4 = (f16[128,256]{1,0:T(8,128)(2,1)S(1)}, f16[128,256]{1,0:T(8,128)(2,1)S(1)}, u32[]{:S(2)}, u32[]{:S(2)}) collective-permute-start(f16[128,256]{1,0:T(8,128)(2,1)S(1)} %multiply_convert_fusion.1), channel_id=1, source_target_pairs={{0,14},{1,11},{2,12},{3,9},{4,10},{5,15},{6,8},{7,13},{8,6},{9,3},... | collective-permute-start | bytes 196616 | tf_op jit(solution)/shard_map/ppermute | solution.py:68
  9.1 5.4 %collective-permute-start.3 = (f16[128,256]{1,0:T(8,128)(2,1)S(1)}, f16[128,256]{1,0:T(8,128)(2,1)S(1)}, u32[]{:S(2)}, u32[]{:S(2)}) collective-permute-start(f16[128,256]{1,0:T(8,128)(2,1)S(1)} %multiply_convert_fusion.2), channel_id=1, source_target_pairs={{0,2},{1,7},{2,0},{3,5},{4,6},{5,3},{6,4},{7,1},{8,10},{9,15},{10,... | collective-permute-start | bytes 196616 | tf_op jit(solution)/shard_map/ppermute | solution.py:68
  9.7 4.8 %collective-permute-start.2 = (f16[128,256]{1,0:T(8,128)(2,1)S(1)}, f16[128,256]{1,0:T(8,128)(2,1)S(1)}, u32[]{:S(2)}, u32[]{:S(2)}) collective-permute-start(f16[128,256]{1,0:T(8,128)(2,1)S(1)} %multiply_convert_fusion.3), channel_id=1, source_target_pairs={{0,0},{1,5},{2,2},{3,7},{4,4},{5,1},{6,6},{7,3},{8,8},{9,13},{10,1... | collective-permute-start | bytes 196616 | tf_op jit(solution)/shard_map/ppermute | solution.py:68
  14.5 1.4 %collective-permute-start.6 = (f32[128,256]{1,0:T(8,128)S(1)}, f32[128,256]{1,0:T(8,128)S(1)}, u32[]{:S(2)}, u32[]{:S(2)}) collective-permute-start(f32[128,256]{1,0:T(8,128)S(1)} %convert_add_fusion.refs_0_), channel_id=1, source_target_pairs={{0,1},{1,0},{2,3},{3,2},{4,5},{5,4},{6,7},{7,6},{8,9},{9,8},{10,11... | collective-permute-start | bytes 393224 | tf_op jit(solution)/shard_map/ppermute | solution.py:89
  16.0 7.0 %collective-permute-start.10 = (bf16[128,256]{1,0:T(8,128)(2,1)S(1)}, bf16[128,256]{1,0:T(8,128)(2,1)S(1)}, u32[]{:S(2)}, u32[]{:S(2)}) collective-permute-start(bf16[128,256]{1,0:T(8,128)(2,1)S(1)} %shard_map.76.refs_1_), channel_id=1, source_target_pairs={{0,8},{1,11},{2,10},{3,9},{4,12},{5,15},{6,14},{7,13},{8,0},{9,3},... | collective-permute-start | bytes 196616 | tf_op jit(solution)/shard_map/ppermute | solution.py:68
  18.5 7.3 %collective-permute-start.9 = (bf16[128,256]{1,0:T(8,128)(2,1)S(1)}, bf16[128,256]{1,0:T(8,128)(2,1)S(1)}, u32[]{:S(2)}, u32[]{:S(2)}) collective-permute-start(bf16[128,256]{1,0:T(8,128)(2,1)S(1)} %shard_map.76.refs_1_), channel_id=1, source_target_pairs={{0,14},{1,13},{2,12},{3,15},{4,10},{5,9},{6,8},{7,11},{8,6},{9,5},... | collective-permute-start | bytes 196616 | tf_op jit(solution)/shard_map/ppermute | solution.py:68
  19.6 6.1 %collective-permute-start.8 = (bf16[128,256]{1,0:T(8,128)(2,1)S(1)}, bf16[128,256]{1,0:T(8,128)(2,1)S(1)}, u32[]{:S(2)}, u32[]{:S(2)}) collective-permute-start(bf16[128,256]{1,0:T(8,128)(2,1)S(1)} %shard_map.76.refs_1_), channel_id=1, source_target_pairs={{0,4},{1,7},{2,6},{3,5},{4,0},{5,3},{6,2},{7,1},{8,12},{9,15},{10,... | collective-permute-start | bytes 196616 | tf_op jit(solution)/shard_map/ppermute | solution.py:68
  20.4 5.4 %collective-permute-start.7 = (bf16[128,256]{1,0:T(8,128)(2,1)S(1)}, bf16[128,256]{1,0:T(8,128)(2,1)S(1)}, u32[]{:S(2)}, u32[]{:S(2)}) collective-permute-start(bf16[128,256]{1,0:T(8,128)(2,1)S(1)} %shard_map.76.refs_1_), channel_id=1, source_target_pairs={{0,2},{1,3},{2,0},{3,1},{4,6},{5,7},{6,4},{7,5},{8,10},{9,11},{10,... | collective-permute-start | bytes 196616 | tf_op jit(solution)/shard_map/ppermute | solution.py:68
  25.8 1.5 %collective-permute-start.11 = (bf16[3,128,256]{2,1,0:T(8,128)(2,1)S(1)}, bf16[3,128,256]{2,1,0:T(8,128)(2,1)S(1)}, u32[]{:S(2)}, u32[]{:S(2)}) collective-permute-start(bf16[3,128,256]{2,1,0:T(8,128)(2,1)S(1)} %shard_map.78), channel_id=1, source_target_pairs={{0,1},{1,0},{2,3},{3,2},{4,5},{5,4},{6,7},{7,6},{8,9},{9,8},{10,11... | collective-permute-start | bytes 589832 | tf_op jit(solution)/shard_map/ppermute | solution.py:89

commit v8 on v7

--- a/solution.py
+++ b/solution.py
@@ -11,7 +11,7 @@
 LAG_MAX = 2
 ROWS = 1024
 PIECES = 4
-ORDER_IN = (0, 2, 1, 3, 7, 5, 4, 6)
+ORDER_IN = (0, 2, 1, 3, 6, 7, 5, 4)
 ORDER_OUT = (0, 1, 2, 3, 7, 6, 4, 5)
 NT = (((1,), (1,)), ((), ()))
 TN = (((0,), (0,)), ((), ()))

time: 28.9 us -> 28.6 us (0.990)
  waiting for transfers between devices: 10.1 us -> 9.54 us
  starting transfers between devices: 13.4 us -> 13.7 us
    ppermute x4, starting transfers between devices: 0.86 us -> 1.17 us  [shifted(): lax.ppermute(array, axis, [(i, (i + step) % peers) for i in range(peers)])]
    ppermute x4, waiting for transfers between devices: 1.68 us -> 1.37 us  [shifted(): lax.ppermute(array, axis, [(i, (i + step) % peers) for i in range(peers)])]
    ppermute x8, waiting for transfers between devices: 8.46 us -> 8.17 us  [exchanged(): return lax.ppermute(array, ('trades', 'dates'), pairs)]
where the time goes in v8:
time: 28.6 us; the launch traced here: 28.4 us
  starting transfers between devices  13.7 us (48%)
  waiting for transfers between devices  9.54 us (33%)
  Pallas kernels  4.92 us (17%)
    ppermute x8, starting transfers between devices, exchanged(): return lax.ppermute(array, ('trades', 'dates'), pairs)  12.5 us
    ppermute x8, waiting for transfers between devices, exchanged(): return lax.ppermute(array, ('trades', 'dates'), pairs)  8.17 us
    pallas_call x2, Pallas kernels, add_grad(): pl.pallas_call(functools.partial(grad_kernel, carry, last), in_specs=[LOC...  2.35 us
    ppermute x4, waiting for transfers between devices, shifted(): lax.ppermute(array, axis, [(i, (i + step) % peers) for i in range(peers)])  1.37 us
    pallas_call x1, Pallas kernels, load(): pl.pallas_call(load_kernel, in_specs=[pl.BlockSpec(memory_space=pl.ANY)]...  1.23 us
    ppermute x4, starting transfers between devices, shifted(): lax.ppermute(array, axis, [(i, (i + step) % peers) for i in range(peers)])  1.17 us
    pallas_call x1, Pallas kernels, net(): pl.pallas_call(functools.partial(net_kernel, rounds, peers), in_specs=[SC...  0.86 us
  transfers between devices with their start and end apart: 12, of which 7 were waited for; matrix products, arithmetic and copies ran while one was open for 0% of the time, Pallas kernels for 9%

profile of v8, /device:TPU:0, one launch (start us, length us, event | category | flops | bytes accessed | tf_op | source)
XLA Modules:
  0.0 28.4 jit_solution(1628409473250280654)
XLA Ops:
  0.0 0.5 %collective-permute-start = (bf16[4,128,256]{2,1,0:T(8,128)(2,1)}, bf16[4,128,256]{2,1,0:T(8,128)(2,1)S(1)}, u32[]{:S(2)}, u32[]{:S(2)}) collective-permute-start(bf16[4,128,256]{2,1,0:T(8,128)(2,1)} %refs_0_.1), channel_id=1, source_target_pairs={{0,1},{1,0},{2,3},{3,2},{4,5},{5,4},{6,7},{7,6},{8,9},{9,8},{10,11... | collective-permute-start | bytes 786440 | tf_op jit(solution)/shard_map/ppermute | solution.py:89
  0.5 0.1 collective-permute-start.1
  0.5 1.2 %shard_map.73 = (bf16[256,1024]{1,0:T(8,128)(2,1)S(1)}, f32[4,1024]{1,0:T(4,128)S(1)}, bf16[4,128,256]{2,1,0:T(8,128)(2,1)S(1)}, bf16[1024,256]{1,0:T(8,128)(2,1...) custom-call(bf16[4,128,256]{2,1,0:T(8,128)(2,1)} %refs_0_.1, ...), custom_call_target="tpu_custom_call" | custom-call | flops 134217728 | bytes 524288 | tf_op jit(solution)/shard_map/pallas_call | solution.py:124
  1.8 0.1 collective-permute-done.1.refs_2_.refs_1_
  1.8 0.0 collective-permute-done.refs_1_.refs_3_
  1.8 0.9 %shard_map.74 = (f32[128,256]{1,0:T(8,128)S(1)}, f32[128,256]{1,0:T(8,128)S(1)}, f32[128,256]{1,0:T(8,128)S(1)}, f32[128,256]{1,0:T(8,128)S(1)}) custom-call(s32[1]{0:T(128)} %bitcast.4.me_ref, s32[1]{0:T(128)} %bitcast.5.trade_ref, bf16[1024,256]{1,0:T(8,128)(2,1)S(1)} %get-tuple-element.25.coef_ref, s32[1,1024]{1,0:T(1,128)S(1)} %get-tuple-element.26.type_ref, ...), custom_call_target="tpu_custom_call" | custom-call | tf_op jit(solution)/shard_map/pallas_call | solution.py:185
  2.8 5.0 %collective-permute-start.5 = (f16[128,256]{1,0:T(8,128)(2,1)S(1)}, f16[128,256]{1,0:T(8,128)(2,1)S(1)}, u32[]{:S(2)}, u32[]{:S(2)}) collective-permute-start(f16[128,256]{1,0:T(8,128)(2,1)S(1)} %multiply_convert_fusion), channel_id=1, source_target_pairs={{0,10},{1,9},{2,8},{3,11},{4,14},{5,13},{6,12},{7,15},{8,2},{9,1},... | collective-permute-start | bytes 196616 | tf_op jit(solution)/shard_map/ppermute | solution.py:68
  7.8 1.3 %collective-permute-start.4 = (f16[128,256]{1,0:T(8,128)(2,1)S(1)}, f16[128,256]{1,0:T(8,128)(2,1)S(1)}, u32[]{:S(2)}, u32[]{:S(2)}) collective-permute-start(f16[128,256]{1,0:T(8,128)(2,1)S(1)} %multiply_convert_fusion.1), channel_id=1, source_target_pairs={{0,12},{1,15},{2,14},{3,13},{4,8},{5,11},{6,10},{7,9},{8,4},{9,7},... | collective-permute-start | bytes 196616 | tf_op jit(solution)/shard_map/ppermute | solution.py:68
  9.1 0.5 %collective-permute-start.3 = (f16[128,256]{1,0:T(8,128)(2,1)S(1)}, f16[128,256]{1,0:T(8,128)(2,1)S(1)}, u32[]{:S(2)}, u32[]{:S(2)}) collective-permute-start(f16[128,256]{1,0:T(8,128)(2,1)S(1)} %multiply_convert_fusion.2), channel_id=1, source_target_pairs={{0,2},{1,7},{2,0},{3,5},{4,6},{5,3},{6,4},{7,1},{8,10},{9,15},{10,... | collective-permute-start | bytes 196616 | tf_op jit(solution)/shard_map/ppermute | solution.py:68
  9.7 0.7 %collective-permute-start.2 = (f16[128,256]{1,0:T(8,128)(2,1)S(1)}, f16[128,256]{1,0:T(8,128)(2,1)S(1)}, u32[]{:S(2)}, u32[]{:S(2)}) collective-permute-start(f16[128,256]{1,0:T(8,128)(2,1)S(1)} %multiply_convert_fusion.3), channel_id=1, source_target_pairs={{0,0},{1,5},{2,2},{3,7},{4,4},{5,1},{6,6},{7,3},{8,8},{9,13},{10,1... | collective-permute-start | bytes 196616 | tf_op jit(solution)/shard_map/ppermute | solution.py:68
  10.3 0.4 %shard_map.75 = (f32[1024,128]{1,0:T(8,128)S(1)}, bf16[640,128]{1,0:T(8,128)(2,1)S(1)}, bf16[384,128]{1,0:T(8,128)(2,1)S(1)}) custom-call(s32[1]{0:T(128)} %bitcast.4.me_ref, s32[1]{0:T(128)} %bitcast.5.trade_ref, s32[1,1024]{1,0:T(1,128)S(1)} %get-tuple-element.26.type_ref, f32[4,16]{1,0:T(4,128)S(1)} %get-tuple-element.34.refs_0_, ...), custom_call_target="tpu_custom_call" | custom-call | flops 268435456 | tf_op jit(solution)/shard_map/pallas_call | solution.py:262
  10.7 1.0 %collective-permute-done.5 = f16[128,256]{1,0:T(8,128)(2,1)S(1)} collective-permute-done((f16[128,256]{1,0:T(8,128)(2,1)S(1)}, f16[128,256]{1,0:T(8,128)(2,1)S(1)}, u32[]{:S(2)}, u32[]{:S(2)}) %collective-permute-start.5) | collective-permute-done | bytes 65568 | tf_op jit(solution)/shard_map/ppermute | solution.py:68
  11.8 2.4 %collective-permute-done.4 = f16[128,256]{1,0:T(8,128)(2,1)S(1)} collective-permute-done((f16[128,256]{1,0:T(8,128)(2,1)S(1)}, f16[128,256]{1,0:T(8,128)(2,1)S(1)}, u32[]{:S(2)}, u32[]{:S(2)}) %collective-permute-start.4) | collective-permute-done | bytes 65568 | tf_op jit(solution)/shard_map/ppermute | solution.py:68
  14.2 0.0 collective-permute-done.3
  14.2 0.0 collective-permute-done.2
  14.2 0.3 %collective-permute-start.6 = (f32[128,256]{1,0:T(8,128)S(1)}, f32[128,256]{1,0:T(8,128)S(1)}, u32[]{:S(2)}, u32[]{:S(2)}) collective-permute-start(f32[128,256]{1,0:T(8,128)S(1)} %convert_add_fusion.refs_0_), channel_id=1, source_target_pairs={{0,1},{1,0},{2,3},{3,2},{4,5},{5,4},{6,7},{7,6},{8,9},{9,8},{10,11... | collective-permute-start | bytes 393224 | tf_op jit(solution)/shard_map/ppermute | solution.py:89
  14.6 1.1 %collective-permute-done.6.refs_1_ = f32[128,256]{1,0:T(8,128)S(1)} collective-permute-done((f32[128,256]{1,0:T(8,128)S(1)}, f32[128,256]{1,0:T(8,128)S(1)}, u32[]{:S(2)}, u32[]{:S(2)}) %collective-permute-start.6) | collective-permute-done | bytes 131104 | tf_op jit(solution)/shard_map/ppermute | solution.py:89
  15.7 2.2 %collective-permute-start.10 = (bf16[128,256]{1,0:T(8,128)(2,1)S(1)}, bf16[128,256]{1,0:T(8,128)(2,1)S(1)}, u32[]{:S(2)}, u32[]{:S(2)}) collective-permute-start(bf16[128,256]{1,0:T(8,128)(2,1)S(1)} %shard_map.76.refs_1_), channel_id=1, source_target_pairs={{0,8},{1,11},{2,10},{3,9},{4,12},{5,15},{6,14},{7,13},{8,0},{9,3},... | collective-permute-start | bytes 196616 | tf_op jit(solution)/shard_map/ppermute | solution.py:68
  17.9 2.0 %collective-permute-start.9 = (bf16[128,256]{1,0:T(8,128)(2,1)S(1)}, bf16[128,256]{1,0:T(8,128)(2,1)S(1)}, u32[]{:S(2)}, u32[]{:S(2)}) collective-permute-start(bf16[128,256]{1,0:T(8,128)(2,1)S(1)} %shard_map.76.refs_1_), channel_id=1, source_target_pairs={{0,14},{1,13},{2,12},{3,15},{4,10},{5,9},{6,8},{7,11},{8,6},{9,5},... | collective-permute-start | bytes 196616 | tf_op jit(solution)/shard_map/ppermute | solution.py:68
  19.9 0.0 collective-permute-start.8
  19.9 0.8 %collective-permute-start.7 = (bf16[128,256]{1,0:T(8,128)(2,1)S(1)}, bf16[128,256]{1,0:T(8,128)(2,1)S(1)}, u32[]{:S(2)}, u32[]{:S(2)}) collective-permute-start(bf16[128,256]{1,0:T(8,128)(2,1)S(1)} %shard_map.76.refs_1_), channel_id=1, source_target_pairs={{0,2},{1,3},{2,0},{3,1},{4,6},{5,7},{6,4},{7,5},{8,10},{9,11},{10,... | collective-permute-start | bytes 196616 | tf_op jit(solution)/shard_map/ppermute | solution.py:68
  20.7 2.2 %collective-permute-done.10.refs_4_ = bf16[128,256]{1,0:T(8,128)(2,1)S(1)} collective-permute-done((bf16[128,256]{1,0:T(8,128)(2,1)S(1)}, bf16[128,256]{1,0:T(8,128)(2,1)S(1)}, u32[]{:S(2)}, u32[]{:S(2)}) %collective-permute-start.10) | collective-permute-done | bytes 65568 | tf_op jit(solution)/shard_map/ppermute | solution.py:68
  23.0 2.4 %collective-permute-done.9.refs_3_ = bf16[128,256]{1,0:T(8,128)(2,1)S(1)} collective-permute-done((bf16[128,256]{1,0:T(8,128)(2,1)S(1)}, bf16[128,256]{1,0:T(8,128)(2,1)S(1)}, u32[]{:S(2)}, u32[]{:S(2)}) %collective-permute-start.9) | collective-permute-done | bytes 65568 | tf_op jit(solution)/shard_map/ppermute | solution.py:68
  25.4 0.0 collective-permute-done.8.refs_2_
  25.4 0.0 collective-permute-done.7.refs_0_
  25.4 0.3 %collective-permute-start.11 = (bf16[3,128,256]{2,1,0:T(8,128)(2,1)S(1)}, bf16[3,128,256]{2,1,0:T(8,128)(2,1)S(1)}, u32[]{:S(2)}, u32[]{:S(2)}) collective-permute-start(bf16[3,128,256]{2,1,0:T(8,128)(2,1)S(1)} %shard_map.78), channel_id=1, source_target_pairs={{0,1},{1,0},{2,3},{3,2},{4,5},{5,4},{6,7},{7,6},{8,9},{9,8},{10,11... | collective-permute-start | bytes 589832 | tf_op jit(solution)/shard_map/ppermute | solution.py:89
  25.8 1.0 %shard_map.77.refs_0_ = f32[1024,128]{1,0:T(8,128)S(1)} custom-call(bf16[256,1024]{1,0:T(8,128)(2,1)S(1)} %get-tuple-element.24.member_ref, f32[1024,128]{1,0:T(8,128)S(1)} %get-tuple-element.38.gain_ref, bf16[640,128]{1,0:T(8,128)(2,1)S(1)} %get-tuple-element.40.basis_ref, bf16[128,256]{1,0:T(8,128)(2,1)S(1)} %collective-permute-done.7.refs_0_, ...), custom_call_target="tpu_custom_call" | custom-call | flops 503316480 | bytes 524288 | tf_op jit(solution)/shard_map/pallas_call | solution.py:317
  26.7 0.2 collective-permute-done.11
  27.0 1.4 %shard_map.79 = f32[1024,128]{1,0:T(8,128)} custom-call(bf16[256,1024]{1,0:T(8,128)(2,1)S(1)} %get-tuple-element.24.member_ref, f32[1024,128]{1,0:T(8,128)S(1)} %get-tuple-element.38.gain_ref, bf16[384,128]{1,0:T(8,128)(2,1)S(1)} %get-tuple-element.39.basis_ref, f32[1024,128]{1,0:T(8,128)S(1)} %shard_map.77.refs_0_, ...), custom_call_target="tpu_custom_call" | custom-call | flops 301989888 | bytes 524288 | tf_op jit(solution)/shard_map/pallas_call | solution.py:317
  (8 shorter events, 0.2 us)
Async XLA Ops:
  0.0 1.8 %collective-permute-start = (bf16[4,128,256]{2,1,0:T(8,128)(2,1)}, bf16[4,128,256]{2,1,0:T(8,128)(2,1)S(1)}, u32[]{:S(2)}, u32[]{:S(2)}) collective-permute-start(bf16[4,128,256]{2,1,0:T(8,128)(2,1)} %refs_0_.1), channel_id=1, source_target_pairs={{0,1},{1,0},{2,3},{3,2},{4,5},{5,4},{6,7},{7,6},{8,9},{9,8},{10,11... | collective-permute-start | bytes 786440 | tf_op jit(solution)/shard_map/ppermute | solution.py:89
  0.5 1.4 %collective-permute-start.1 = (f32[4,16]{1,0:T(4,128)}, f32[4,16]{1,0:T(4,128)S(1)}, u32[]{:S(2)}, u32[]{:S(2)}) collective-permute-start(f32[4,16]{1,0:T(4,128)} %refs_3_.1), channel_id=1, source_target_pairs={{0,1},{1,0},{2,3},{3,2},{4,5},{5,4},{6,7},{7,6},{8,9},{9,8},{10,11... | collective-permute-start | bytes 776 | tf_op jit(solution)/shard_map/ppermute | solution.py:89
  2.8 9.0 %collective-permute-start.5 = (f16[128,256]{1,0:T(8,128)(2,1)S(1)}, f16[128,256]{1,0:T(8,128)(2,1)S(1)}, u32[]{:S(2)}, u32[]{:S(2)}) collective-permute-start(f16[128,256]{1,0:T(8,128)(2,1)S(1)} %multiply_convert_fusion), channel_id=1, source_target_pairs={{0,10},{1,9},{2,8},{3,11},{4,14},{5,13},{6,12},{7,15},{8,2},{9,1},... | collective-permute-start | bytes 196616 | tf_op jit(solution)/shard_map/ppermute | solution.py:68
  7.8 6.4 %collective-permute-start.4 = (f16[128,256]{1,0:T(8,128)(2,1)S(1)}, f16[128,256]{1,0:T(8,128)(2,1)S(1)}, u32[]{:S(2)}, u32[]{:S(2)}) collective-permute-start(f16[128,256]{1,0:T(8,128)(2,1)S(1)} %multiply_convert_fusion.1), channel_id=1, source_target_pairs={{0,12},{1,15},{2,14},{3,13},{4,8},{5,11},{6,10},{7,9},{8,4},{9,7},... | collective-permute-start | bytes 196616 | tf_op jit(solution)/shard_map/ppermute | solution.py:68
  9.1 5.1 %collective-permute-start.3 = (f16[128,256]{1,0:T(8,128)(2,1)S(1)}, f16[128,256]{1,0:T(8,128)(2,1)S(1)}, u32[]{:S(2)}, u32[]{:S(2)}) collective-permute-start(f16[128,256]{1,0:T(8,128)(2,1)S(1)} %multiply_convert_fusion.2), channel_id=1, source_target_pairs={{0,2},{1,7},{2,0},{3,5},{4,6},{5,3},{6,4},{7,1},{8,10},{9,15},{10,... | collective-permute-start | bytes 196616 | tf_op jit(solution)/shard_map/ppermute | solution.py:68
  9.7 4.6 %collective-permute-start.2 = (f16[128,256]{1,0:T(8,128)(2,1)S(1)}, f16[128,256]{1,0:T(8,128)(2,1)S(1)}, u32[]{:S(2)}, u32[]{:S(2)}) collective-permute-start(f16[128,256]{1,0:T(8,128)(2,1)S(1)} %multiply_convert_fusion.3), channel_id=1, source_target_pairs={{0,0},{1,5},{2,2},{3,7},{4,4},{5,1},{6,6},{7,3},{8,8},{9,13},{10,1... | collective-permute-start | bytes 196616 | tf_op jit(solution)/shard_map/ppermute | solution.py:68
  14.2 1.4 %collective-permute-start.6 = (f32[128,256]{1,0:T(8,128)S(1)}, f32[128,256]{1,0:T(8,128)S(1)}, u32[]{:S(2)}, u32[]{:S(2)}) collective-permute-start(f32[128,256]{1,0:T(8,128)S(1)} %convert_add_fusion.refs_0_), channel_id=1, source_target_pairs={{0,1},{1,0},{2,3},{3,2},{4,5},{5,4},{6,7},{7,6},{8,9},{9,8},{10,11... | collective-permute-start | bytes 393224 | tf_op jit(solution)/shard_map/ppermute | solution.py:89
  15.7 7.3 %collective-permute-start.10 = (bf16[128,256]{1,0:T(8,128)(2,1)S(1)}, bf16[128,256]{1,0:T(8,128)(2,1)S(1)}, u32[]{:S(2)}, u32[]{:S(2)}) collective-permute-start(bf16[128,256]{1,0:T(8,128)(2,1)S(1)} %shard_map.76.refs_1_), channel_id=1, source_target_pairs={{0,8},{1,11},{2,10},{3,9},{4,12},{5,15},{6,14},{7,13},{8,0},{9,3},... | collective-permute-start | bytes 196616 | tf_op jit(solution)/shard_map/ppermute | solution.py:68
  17.9 7.5 %collective-permute-start.9 = (bf16[128,256]{1,0:T(8,128)(2,1)S(1)}, bf16[128,256]{1,0:T(8,128)(2,1)S(1)}, u32[]{:S(2)}, u32[]{:S(2)}) collective-permute-start(bf16[128,256]{1,0:T(8,128)(2,1)S(1)} %shard_map.76.refs_1_), channel_id=1, source_target_pairs={{0,14},{1,13},{2,12},{3,15},{4,10},{5,9},{6,8},{7,11},{8,6},{9,5},... | collective-permute-start | bytes 196616 | tf_op jit(solution)/shard_map/ppermute | solution.py:68
  19.9 5.5 %collective-permute-start.8 = (bf16[128,256]{1,0:T(8,128)(2,1)S(1)}, bf16[128,256]{1,0:T(8,128)(2,1)S(1)}, u32[]{:S(2)}, u32[]{:S(2)}) collective-permute-start(bf16[128,256]{1,0:T(8,128)(2,1)S(1)} %shard_map.76.refs_1_), channel_id=1, source_target_pairs={{0,4},{1,7},{2,6},{3,5},{4,0},{5,3},{6,2},{7,1},{8,12},{9,15},{10,... | collective-permute-start | bytes 196616 | tf_op jit(solution)/shard_map/ppermute | solution.py:68
  19.9 5.5 %collective-permute-start.7 = (bf16[128,256]{1,0:T(8,128)(2,1)S(1)}, bf16[128,256]{1,0:T(8,128)(2,1)S(1)}, u32[]{:S(2)}, u32[]{:S(2)}) collective-permute-start(bf16[128,256]{1,0:T(8,128)(2,1)S(1)} %shard_map.76.refs_1_), channel_id=1, source_target_pairs={{0,2},{1,3},{2,0},{3,1},{4,6},{5,7},{6,4},{7,5},{8,10},{9,11},{10,... | collective-permute-start | bytes 196616 | tf_op jit(solution)/shard_map/ppermute | solution.py:68
  25.4 1.5 %collective-permute-start.11 = (bf16[3,128,256]{2,1,0:T(8,128)(2,1)S(1)}, bf16[3,128,256]{2,1,0:T(8,128)(2,1)S(1)}, u32[]{:S(2)}, u32[]{:S(2)}) collective-permute-start(bf16[3,128,256]{2,1,0:T(8,128)(2,1)S(1)} %shard_map.78), channel_id=1, source_target_pairs={{0,1},{1,0},{2,3},{3,2},{4,5},{5,4},{6,7},{7,6},{8,9},{9,8},{10,11... | collective-permute-start | bytes 589832 | tf_op jit(solution)/shard_map/ppermute | solution.py:89
